TPU v7x, 128 devices: a whole 4x4x4 slice. The times are simulated.
128 devices in a mesh: fsdp: 32 (over z, y, core), sp: 4 (over x).
Axes of the slice: x: 4, y: 4, z: 4, core: 2. Of those that a mesh axis runs over, the one named last changes fastest.
Arguments:
- hidden_in: bfloat16 [32, 1024, 768], P('fsdp', 'sp'), may hold values from -6 to 6
- lengths: int32 [32], P('fsdp'), may hold values from 128 to 1024, as said below
- qkv_weight: bfloat16 [768, 2304], P('fsdp'), may hold values from -0.21875 to 0.21875
- query_bias: bfloat16 [768], P('fsdp'), may hold values from -3 to 3
- value_bias: bfloat16 [768], P('fsdp'), may hold values from -3 to 3
- context_weight: bfloat16 [768, 768], P('fsdp'), may hold values from -6 to 6
- context_bias: bfloat16 [768], P('fsdp'), may hold values from -3 to 3
- first_gain: bfloat16 [768], P('fsdp'), may hold values from 0.25 to 1.75
- first_shift: bfloat16 [768], P('fsdp'), may hold values from -3 to 3
- expand_weight: bfloat16 [768, 3072], P('fsdp'), may hold values from -0.21875 to 0.21875
- expand_bias: bfloat16 [3072], P('fsdp'), may hold values from -3 to 3
- reduce_weight: bfloat16 [3072, 768], P('fsdp'), may hold values from -0.109375 to 0.109375
- reduce_bias: bfloat16 [768], P('fsdp'), may hold values from -3 to 3
- second_gain: bfloat16 [768], P('fsdp'), may hold values from 0.25 to 1.75
- second_shift: bfloat16 [768], P('fsdp'), may hold values from -3 to 3
- out_grad: bfloat16 [32, 1024, 768], P('fsdp', 'sp'), may hold values from -6 to 6
Outputs:
- hidden_out: bfloat16 [32, 1024, 768], P('fsdp', 'sp')
- input_grad: bfloat16 [32, 1024, 768], P('fsdp', 'sp')
- qkv_weight_grad: float32 [768, 2304], P('fsdp')
- query_bias_grad: float32 [768], P('fsdp')
- value_bias_grad: float32 [768], P('fsdp')
- context_weight_grad: float32 [768, 768], P('fsdp')
- context_bias_grad: float32 [768], P('fsdp')
- first_gain_grad: float32 [768], P('fsdp')
- first_shift_grad: float32 [768], P('fsdp')
- expand_weight_grad: float32 [768, 3072], P('fsdp')
- expand_bias_grad: float32 [3072], P('fsdp')
- reduce_weight_grad: float32 [3072, 768], P('fsdp')
- reduce_bias_grad: float32 [768], P('fsdp')
- second_gain_grad: float32 [768], P('fsdp')
- second_shift_grad: float32 [768], P('fsdp')
Inputs may be any that keep to these rules, and one draw needn't show every extreme that they name: lengths of a sequence counts its valid positions from its start; later positions are padding. In every group of 1 sequence one has more than 768, and some sequence has exactly 1024.
All inputs are finite; a program needn't handle non-finite values.
Results may differ from a plain program's by a relative error of at most 0.025.
Values may be sent and summed in bfloat16 or wider, within the bound.
No kernel may reach another device: no remote copies, remote signals or barrier semaphores. Data moves between devices by JAX's collectives and lax.ppermute only.
A program may use at most 128 MiB of HBM per device.

v0:
```python
import functools

import jax
import jax.numpy as jnp
from jax import lax
from jax.experimental import pallas as pl
from jax.experimental.pallas import tpu as pltpu
from jax.sharding import PartitionSpec as P

D = 768
H = 12
DH = 64
FF = 3072
SP = 4
LOCAL = 256
LEN = 1024
HEADS = H // SP
HW = HEADS * DH
BLOCK = 256

EPSILON = 1e-06
SCALING = 0.125
MASKED = -1000000000.0
F32 = jnp.float32
BF16 = jnp.bfloat16


def normalize(values, gain_row, shift_row):
    average = jnp.mean(values, axis=-1, keepdims=True)
    centred = values - average
    inv_std = lax.rsqrt(jnp.mean(centred * centred, axis=-1, keepdims=True) + EPSILON)
    normed = centred * inv_std
    return (normed * gain_row + shift_row, normed, inv_std)


def normalize_back(upstream, normed, inv_std, gain_row):
    weighted = upstream * gain_row
    return inv_std * (
        weighted
        - jnp.mean(weighted, axis=-1, keepdims=True)
        - normed * jnp.mean(weighted * normed, axis=-1, keepdims=True)
    )


def dot(left_side, right_side):
    return jnp.dot(left_side, right_side, preferred_element_type=F32)


def rows_first(left_side, right_side):
    return lax.dot_general(
        left_side, right_side, (((0,), (0,)), ((), ())), preferred_element_type=F32
    )


def by_transpose(left_side, right_side):
    return lax.dot_general(
        left_side, right_side, (((1,), (1,)), ((), ())), preferred_element_type=F32
    )


def smooth_gate(values):
    return jax.nn.gelu(values, approximate=True)


def column_sum(values):
    return jnp.sum(values.astype(F32), axis=0)


def to_x(values, step):
    return lax.ppermute(values, "sp", [(i, (i + step) % SP) for i in range(SP)])


ORDER = (1, 3, 2)


def rolled(values, start):
    count = values.shape[0]
    return lax.dynamic_slice_in_dim(
        jnp.concatenate([values, values], axis=0), start % count, count, axis=0
    )


def masked_keys(info_ref, shape, dim):
    at = lax.broadcasted_iota(jnp.int32, shape, dim)
    block = (info_ref[0] + lax.shift_right_logical(at, 8)) & 3
    return (block * LOCAL + (at & (LOCAL - 1))) < info_ref[1]


def attend_kernel(info_ref, qkv_ref, context_ref):
    valid = masked_keys(info_ref, (1, LEN), 1)

    @pl.loop(0, LEN // BLOCK)
    def _(step):
        rows = pl.ds(pl.multiple_of(step * BLOCK, BLOCK), BLOCK)
        outs = []
        for head in range(HEADS):
            cols = head * DH
            keys = qkv_ref[:, HW + cols : HW + cols + DH]
            vals = qkv_ref[:, 2 * HW + cols : 2 * HW + cols + DH]
            queries = qkv_ref[rows, cols : cols + DH] * jnp.asarray(SCALING, BF16)
            scores = jnp.where(valid, by_transpose(queries, keys), MASKED)
            weights = jnp.exp(scores - jnp.max(scores, axis=-1, keepdims=True))
            totals = jnp.sum(weights, axis=-1, keepdims=True)
            outs.append(dot(weights.astype(BF16), vals) * (1.0 / totals))
        context_ref[rows, :] = jnp.concatenate(outs, axis=1).astype(BF16)


def attend_back_kernel(info_ref, qkv_ref, grad_ref, out_ref, key_sum, value_sum):
    valid = masked_keys(info_ref, (LEN, 1), 0)
    key_sum[...] = jnp.zeros_like(key_sum)
    value_sum[...] = jnp.zeros_like(value_sum)

    @pl.loop(0, LEN // BLOCK)
    def _(step):
        rows = pl.ds(pl.multiple_of(step * BLOCK, BLOCK), BLOCK)
        outs = []
        for head in range(HEADS):
            cols = head * DH
            keys = qkv_ref[:, HW + cols : HW + cols + DH]
            vals = qkv_ref[:, 2 * HW + cols : 2 * HW + cols + DH]
            queries = qkv_ref[rows, cols : cols + DH] * jnp.asarray(SCALING, BF16)
            grads = grad_ref[rows, cols : cols + DH]
            scores = jnp.where(valid, by_transpose(keys, queries), MASKED)
            weights = jnp.exp(scores - jnp.max(scores, axis=0, keepdims=True))
            probs = weights * (1.0 / jnp.sum(weights, axis=0, keepdims=True))
            value_sum[head] += dot(probs.astype(BF16), grads)
            prob_grad = by_transpose(vals, grads)
            centre = jnp.sum(probs * prob_grad, axis=0, keepdims=True)
            score_grad = (probs * (prob_grad - centre)).astype(BF16)
            key_sum[head] += dot(score_grad, queries)
            outs.append(rows_first(score_grad, keys) * SCALING)
        out_ref[rows, :HW] = jnp.concatenate(outs, axis=1).astype(BF16)

    for part, total in ((1, key_sum), (2, value_sum)):
        out_ref[:, part * HW : (part + 1) * HW] = jnp.concatenate(
            [total[head] for head in range(HEADS)], axis=1
        ).astype(BF16)


def reduce_grad_kernel(active_ref, grad_ref, out_ref):
    full = rows_first(active_ref[...], grad_ref[...]).reshape(8, 4, 24, D)
    for part in range(4):
        out_ref[:, part * D : (part + 1) * D] = full[:, part].reshape(192, D).astype(BF16)


def other_grad_kernel(info_ref, first_ref, expand_ref, context_ref, branch_ref, held_ref, out_ref):
    step = pl.program_id(0)

    @pl.when(step < 4)
    def _():
        out_ref[...] = rows_first(first_ref[...], expand_ref[...]).astype(BF16)

    @pl.when(step == 4)
    def _():
        for block in range(SP):
            rows = pl.multiple_of(((info_ref[0] + block) & 3) * HW, HW)
            out_ref[pl.ds(rows, HW), :] = rows_first(
                context_ref[:, block * HW : (block + 1) * HW], branch_ref[...]
            ).astype(BF16)


SMEM = pl.BlockSpec(memory_space=pltpu.SMEM)
VMEM = pl.BlockSpec(memory_space=pltpu.VMEM)
PARAMS = pltpu.CompilerParams(vmem_limit_bytes=40 * 1024 * 1024)


def attend(info, qkv):
    return pl.pallas_call(
        attend_kernel,
        out_shape=jax.ShapeDtypeStruct((LEN, HW), BF16),
        in_specs=[SMEM, VMEM],
        out_specs=VMEM,
        compiler_params=PARAMS,
        cost_estimate=pl.CostEstimate(
            flops=4 * HEADS * LEN * LEN * 256, bytes_accessed=LEN * HW * 8, transcendentals=0
        ),
        name="attend",
    )(info, qkv)


def attend_back(info, qkv, grads):
    return pl.pallas_call(
        attend_back_kernel,
        out_shape=jax.ShapeDtypeStruct((LEN, 3 * HW), BF16),
        in_specs=[SMEM, VMEM, VMEM],
        out_specs=VMEM,
        scratch_shapes=[pltpu.VMEM((HEADS, LEN, DH), F32), pltpu.VMEM((HEADS, LEN, DH), F32)],
        compiler_params=PARAMS,
        cost_estimate=pl.CostEstimate(
            flops=10 * HEADS * LEN * LEN * 256, bytes_accessed=LEN * HW * 14, transcendentals=0
        ),
        name="attend_back",
    )(info, qkv, grads)


PACKED = 2 * FF + D


def reduce_grad(active, reduced_grad):
    return pl.pallas_call(
        reduce_grad_kernel,
        out_shape=jax.ShapeDtypeStruct((D, PACKED), BF16),
        grid=(4,),
        in_specs=[
            pl.BlockSpec((LOCAL, D), lambda i: (0, i)),
            pl.BlockSpec((LOCAL, D), lambda i: (0, 0)),
        ],
        out_specs=pl.BlockSpec((192, FF), lambda i: (i, 0)),
        compiler_params=PARAMS,
        cost_estimate=pl.CostEstimate(
            flops=2 * LOCAL * D * FF, bytes_accessed=8 * 1024 * 1024, transcendentals=0
        ),
        name="reduce_grad",
    )(active, reduced_grad)


def other_grads(info, first_low, expand_grad, context_tok, branch_grad, held):
    whole = pl.BlockSpec((LOCAL, D), lambda i: (0, 0))
    return pl.pallas_call(
        other_grad_kernel,
        out_shape=jax.ShapeDtypeStruct((D, PACKED), BF16),
        grid=(5,),
        in_specs=[
            SMEM,
            whole,
            pl.BlockSpec((LOCAL, D), lambda i: (0, jnp.minimum(i, 3))),
            whole,
            whole,
            pl.BlockSpec(memory_space=pl.ANY),
        ],
        out_specs=pl.BlockSpec((D, D), lambda i: (0, 4 + i)),
        input_output_aliases={5: 0},
        compiler_params=PARAMS,
        cost_estimate=pl.CostEstimate(
            flops=2 * LOCAL * D * (FF + D), bytes_accessed=8 * 1024 * 1024, transcendentals=0
        ),
        name="other_grads",
    )(info, first_low, expand_grad, context_tok, branch_grad, held)


def from_x(values, x_at):
    pieces = [values] + [to_x(values, -step) for step in (1, 2, 3)]
    return rolled(jnp.stack(pieces), SP - x_at)


def per_device(
    hidden_in,
    lengths,
    qkv_weight,
    query_bias,
    value_bias,
    context_weight,
    context_bias,
    first_gain,
    first_shift,
    expand_weight,
    expand_bias,
    reduce_weight,
    reduce_bias,
    second_gain,
    second_shift,
    out_grad,
):
    x_at = lax.axis_index("sp")
    own = hidden_in[0]
    tokens = [own] + [None] * 3
    for step in ORDER:
        tokens[step] = to_x(own, -step)

    row_at = lax.broadcasted_iota(jnp.int32, (8, D), 0)
    vectors = jnp.pad(expand_bias, (0, D - 96))[None]
    for row, part in enumerate(
        (context_bias, first_gain, first_shift, reduce_bias, second_gain, second_shift)
    ):
        vectors = jnp.where(row_at == row, jnp.pad(part, (0, D - 24))[None], vectors)
    packed = jnp.concatenate(
        [context_weight, reduce_weight]
        + [expand_weight[:, D * block : D * (block + 1)] for block in range(4)]
        + [vectors],
        axis=0,
    )
    packed = lax.all_gather(packed, "fsdp", axis=0, tiled=False)

    early = jnp.concatenate(
        [lax.dynamic_slice(qkv_weight, (0, part * D + x_at * HW), (24, HW)) for part in range(3)],
        axis=1,
    )
    row_at = lax.broadcasted_iota(jnp.int32, (26, 3 * HW), 0)
    early = jnp.where(
        row_at < 24,
        jnp.pad(early, ((0, 2), (0, 0))),
        jnp.where(
            row_at == 24,
            jnp.pad(query_bias, (0, 3 * HW - 24))[None],
            jnp.pad(value_bias, (0, 3 * HW - 24))[None],
        ),
    )
    early = lax.all_to_all(
        jnp.broadcast_to(early[None], (32, 26, 3 * HW)),
        "fsdp",
        split_axis=0,
        concat_axis=0,
        tiled=True,
    )
    qkv_full = early[:, :24].reshape(D, 3 * HW)
    query_full = early[:, 24, :24].reshape(D).astype(F32)
    value_full = early[:, 25, :24].reshape(D).astype(F32)

    everyone = jnp.concatenate(tokens, axis=0)
    offsets = jnp.concatenate(
        [
            lax.dynamic_slice_in_dim(query_full, x_at * HW, HW),
            jnp.zeros((HW,), F32),
            lax.dynamic_slice_in_dim(value_full, x_at * HW, HW),
        ]
    )
    qkv = (dot(everyone, qkv_full) + offsets).astype(BF16)
    info = jnp.stack([x_at.astype(jnp.int32), lengths[0]])
    context = attend(info, qkv)

    groups = [context[:LOCAL]] + [None] * 3
    for step in ORDER:
        groups[SP - step] = to_x(context[step * LOCAL : (step + 1) * LOCAL], step)
    context_tok = jnp.concatenate(groups, axis=1)

    context_full = rolled(packed[:, :24].reshape(SP, HW, D), x_at).reshape(D, D)
    reduce_full = packed[:, 24:120].reshape(FF, D)
    context_add, gain_one, shift_one, reduce_add, gain_two, shift_two = (
        packed[:, 216 + row, :24].reshape(D).astype(F32) for row in range(6)
    )
    expand_add = packed[:, 222, :96].reshape(FF).astype(F32)
    expand_full = jnp.concatenate(
        [packed[:, 120 + 24 * block : 144 + 24 * block].reshape(D, D) for block in range(4)], axis=1
    )

    branch = dot(context_tok, context_full) + context_add
    first_out, normed_one, inv_one = normalize(own.astype(F32) + branch, gain_one, shift_one)
    first_low = first_out.astype(BF16)
    expand = dot(first_low, expand_full) + expand_add
    active = smooth_gate(expand).astype(BF16)
    reduced = dot(active, reduce_full) + reduce_add
    second_out, normed_two, inv_two = normalize(first_out + reduced, gain_two, shift_two)
    hidden_out = second_out.astype(BF16)[None]

    out_rows = out_grad[0].astype(F32)
    second_gain_grad = jnp.sum(out_rows * normed_two, axis=0)
    second_shift_grad = jnp.sum(out_rows, axis=0)
    grad_two = normalize_back(out_rows, normed_two, inv_two, gain_two)
    reduced_grad = grad_two.astype(BF16)
    reduce_bias_grad = column_sum(reduced_grad)

    held = reduce_grad(active, reduced_grad)

    active_grad = by_transpose(reduced_grad, reduce_full).astype(BF16)
    gate_value, gate_pullback = jax.vjp(smooth_gate, expand)
    expand_grad = gate_pullback(active_grad.astype(F32))[0].astype(BF16)
    expand_bias_grad = column_sum(expand_grad)
    first_grad = by_transpose(expand_grad, expand_full) + grad_two
    first_gain_grad = jnp.sum(first_grad * normed_one, axis=0)
    first_shift_grad = jnp.sum(first_grad, axis=0)
    grad_one = normalize_back(first_grad, normed_one, inv_one, gain_one)
    branch_grad = grad_one.astype(BF16)
    context_bias_grad = column_sum(branch_grad)
    packed_grads = other_grads(info, first_low, expand_grad, context_tok, branch_grad, held)
    packed_grads = lax.psum_scatter(packed_grads, "fsdp", scatter_dimension=0, tiled=True)
    context_grad = by_transpose(branch_grad, context_full).astype(BF16)
    blocks = [context_grad[:, :HW]] + [None] * 3
    for step in ORDER:
        blocks[SP - step] = to_x(context_grad[:, step * HW : (step + 1) * HW], step)
    grad_heads = jnp.concatenate(blocks, axis=0)

    qkv_grad = attend_back(info, qkv, grad_heads)

    partial = by_transpose(qkv_grad, qkv_full).astype(BF16)
    input_sum = grad_one + partial[:LOCAL].astype(F32)
    for step in ORDER:
        input_sum = input_sum + to_x(partial[step * LOCAL : (step + 1) * LOCAL], step).astype(F32)
    input_grad = input_sum.astype(BF16)[None]

    qkv_weight_grad = rows_first(everyone, qkv_grad)
    sums = column_sum(qkv_grad)
    two = jnp.zeros((2, D), F32)
    two = lax.dynamic_update_slice(two, jnp.stack([sums[:HW], sums[2 * HW :]]), (0, x_at * HW))
    late = jnp.stack(
        [context_bias_grad, first_gain_grad, first_shift_grad, reduce_bias_grad, second_gain_grad, second_shift_grad],
        axis=0,
    )
    late = jnp.concatenate([two, late], axis=0).T
    second_round = jnp.concatenate([qkv_weight_grad, late, expand_bias_grad.reshape(D, 4)], axis=1)
    second_round = lax.all_to_all(
        second_round.astype(BF16).reshape(32, 24, 3 * HW + 12),
        "fsdp",
        split_axis=0,
        concat_axis=0,
        tiled=True,
    )
    second_round = jnp.sum(second_round.astype(F32), axis=0).astype(BF16)
    second_round = from_x(second_round, x_at).astype(F32)
    qkv_out = jnp.transpose(second_round[:, :, : 3 * HW].reshape(SP, 24, 3, HW), (1, 2, 0, 3))
    qkv_out = qkv_out.reshape(24, 3 * D)
    vector_out = jnp.sum(second_round[:, :, 3 * HW :], axis=0)
    eight = vector_out[:, :8].T
    expand_bias_out = vector_out[:, 8:].reshape(96)

    total = packed_grads.astype(F32)
    for step in ORDER:
        total = total + to_x(packed_grads, step).astype(F32)
    reduce_out = jnp.swapaxes(total[:, :FF].reshape(24, 4, D), 0, 1).reshape(96, D)
    expand_out = total[:, FF : 2 * FF]
    context_out = total[:, 2 * FF :]

    return (
        hidden_out,
        input_grad,
        qkv_out,
        eight[0],
        eight[1],
        context_out,
        eight[2],
        eight[3],
        eight[4],
        expand_out,
        expand_bias_out,
        reduce_out,
        eight[5],
        eight[6],
        eight[7],
    )


def solution(mesh):
    sequences = P("fsdp", "sp", None)
    matrix = P("fsdp", None)
    vector = P("fsdp")
    return jax.shard_map(
        per_device,
        mesh=mesh,
        in_specs=(
            sequences, vector, matrix, vector, vector, matrix, vector, vector, vector,
            matrix, vector, matrix, vector, vector, vector, sequences,
        ),
        out_specs=(
            sequences, sequences, matrix, vector, vector, matrix, vector, vector, vector,
            matrix, vector, matrix, vector, vector, vector,
        ),
        check_vma=False,
    )
```

profile of v0, /device:TPU:6, one launch (start us, length us, event | category | flops | bytes accessed | tf_op | source)
XLA Modules:
  0.0 255.8 jit_solution(5890084581774584590)
XLA Ops:
  11.9 0.8 constant_dynamic-update-slice_fusion.2
  12.7 0.9 constant_dynamic-update-slice_fusion.1
  13.6 0.8 slice_dynamic-update-slice_fusion.3
  14.4 0.8 slice_dynamic-update-slice_fusion.2
  15.2 0.8 slice_dynamic-update-slice_fusion.1
  15.9 0.8 slice_dynamic-update-slice_fusion
  16.8 0.7 copy-done.14
  18.9 0.8 constant_dynamic-slice_fusion.2
  19.8 1.2 broadcast_in_dim.107
  21.0 8.3 %all-to-all-start = ((bf16[32,26,576]{2,1,0:T(8,128)(2,1)}), bf16[32,26,576]{2,1,0:T(8,128)(2,1)S(1)}, u32[]{:S(2)}, u32[]{:S(2)}) async-start(bf16[32,26,576]{2,1,0:T(8,128)(2,1)} %broadcast_in_dim.107), calls=%async_computation | async-start | bytes 2621440 | tf_op jit(solution)/shard_map/all_to_all | solution.py:298
  29.9 2.4 collective-permute-start.1
  33.1 22.0 %all-to-all-done = bf16[32,26,576]{2,1,0:T(8,128)(2,1)S(1)} async-done(((bf16[32,26,576]{2,1,0:T(8,128)(2,1)}), bf16[32,26,576]{2,1,0:T(8,128)(2,1)S(1)}, u32[]{:S(2)}, u32[]{:S(2)}) %all-to-all-start) | async-done | bytes 958496 | tf_op jit(solution)/shard_map/all_to_all | solution.py:298
  55.7 0.9 copy-done.12
  56.6 1.4 add_convert_fusion.qkv_ref
  58.0 7.5 %attend.1 = bf16[1024,192]{1,0:T(8,128)(2,1)S(1)} custom-call(s32[2]{0:T(128)S(1)} %pad_add_fusion.info_ref, bf16[1024,576]{1,0:T(8,128)(2,1)S(1)} %add_convert_fusion.qkv_ref), custom_call_target="tpu_custom_call" | custom-call | flops 3221225472 | bytes 1572864 | tf_op jit(solution)/shard_map/attend/pallas_call | solution.py:168
  66.1 2.4 collective-permute-start.4
  68.6 3.5 %collective-permute-done.5 = bf16[256,192]{1,0:T(8,128)(2,1)S(1)} collective-permute-done((bf16[256,192]{1,0:T(8,128)(2,1)S(1)}, bf16[256,192]{1,0:T(8,128)(2,1)S(1)}, u32[]{:S(2)}, u32[]{:S(2)}) %collective-permute-start.5) | collective-permute-done | bytes 98336 | tf_op jit(solution)/shard_map/ppermute | solution.py:70
  72.0 1.8 collective-permute-done.4
  73.8 1.8 collective-permute-done.3
  75.8 12.7 %all-gather.3.cloned.1.call-done = bf16[7168,768]{1,0:T(8,128)(2,1)} async-done(((bf16[224,768]{1,0:T(8,128)(2,1)}), bf16[7168,768]{1,0:T(8,128)(2,1)}) %all-gather.3.cloned.1.call-update) | async-done | bytes 11010064 | tf_op jit(solution)/shard_map/all_gather | solution.py:282
  88.5 0.9 fusion.29
  89.4 1.4 fusion.40
  90.8 4.9 %slice.212 = bf16[32,96,768]{2,1,0:T(8,128)(2,1)} slice(bf16[32,224,768]{2,1,0:T(8,128)(2,1)} %bitcast.80), slice={[0:32], [24:120], [0:768]} | slice | bytes 9437184 | tf_op jit(solution)/shard_map/slice | solution.py:327
  95.6 5.2 %fusion.41 = (bf16[32,24,768]{2,1,0:T(8,128)(2,1)}, bf16[32,24,768]{2,1,0:T(8,128)(2,1)}, bf16[32,24,768]{2,1,0:T(8,128)(2,1)}, bf16[32,24,768]{2,1,0:T(8,128)(2,1)}, bf16[32,24,768]{2,1,0:T(8,128)(2,1)}) fusion(bf16[32,224,768]{2,1,0:T(8,128)(2,1)} %bitcast.81), kind=kLoop, calls=%fused_computation.134 | loop fusion | bytes 11796480 | tf_op jit(solution)/shard_map/slice | solution.py:333
  101.6 1.8 fusion.12
  104.5 5.8 %multiply_convert_fusion = (bf16[256,3072]{1,0:T(8,128)(2,1)S(1)}, f32[256,3072]{1,0:T(8,128)}) fusion(f32[3072]{0:T(1024)S(1)} %reshape.201, bf16[256,768]{1,0:T(8,128)(2,1)S(1)} %fusion.20.first_ref, bf16[768,768]{1,0:T(8,128)(2,1)S(1)} %bitcast.92, bf16[768,768]{1,0:T(8,128)(2,1)S(1)} %bitcast.94, bf16[768,768]{1,0:T(8,128)(2,1)S(1)} %bitcast.96, ...), kind=kOutput, calls=%fused_computation.17 | convolution fusion | flops 1234698240 | bytes 9842688 | tf_op jit(solution)/shard_map/dot_general | solution.py:46
  110.3 1.5 fusion.48
  112.0 1.1 fusion.19
  113.5 2.5 reduce_grad.1.held_ref
  116.0 4.6 %fusion.49 = (bf16[3072]{0:T(1024)(128)(2,1)S(1)}, bf16[256,3072]{1,0:T(8,128)(2,1)S(1)}) fusion(f32[256,3072]{1,0:T(8,128)} %get-tuple-element.70, bf16[256,768]{1,0:T(8,128)(2,1)S(1)} %get-tuple-element.33.grad_ref, bf16[3072,768]{1,0:T(8,128)(2,1)S(1)} %bitcast.86), kind=kOutput, calls=%fused_computation.142 | convolution fusion | flops 1226044416 | bytes 9836544 | tf_op jit(solution)/shard_map/dot_general | solution.py:56
  120.6 1.8 multiply_reduce_fusion
  122.4 1.2 fusion.39
  123.6 3.8 %other_grads.1 = bf16[768,6912]{1,0:T(8,128)(2,1)S(1)} custom-call(s32[2]{0:T(128)S(1)} %pad_add_fusion.info_ref, bf16[256,768]{1,0:T(8,128)(2,1)S(1)} %fusion.20.first_ref, bf16[256,3072]{1,0:T(8,128)(2,1)S(1)} %get-tuple-element.75.expand_ref, bf16[256,768]{1,0:T(8,128)(2,1)S(1)} %pad_maximum_fusion.6.context_ref, ...), custom_call_target="tpu_custom_call", output_to_operand_aliasing={{}: (5, {})} | custom-call | flops 1509949440 | bytes 8388608 | tf_op jit(solution)/shard_map/other_grads/pallas_call | solution.py:219
  127.5 4.0 %copy-done = bf16[768,6912]{1,0:T(8,128)(2,1)} copy-done((bf16[768,6912]{1,0:T(8,128)(2,1)}, bf16[768,6912]{1,0:T(8,128)(2,1)S(1)}, u32[]{:S(2)}) %copy-start) | copy-done | bytes 10616856
  132.8 2.3 collective-permute-start.7
  135.3 1.1 concatenate.54
  136.4 2.1 collective-permute-done.8
  138.5 2.1 collective-permute-done.7
  140.7 1.8 collective-permute-done.6
  142.6 16.9 %attend_back.1 = bf16[1024,576]{1,0:T(8,128)(2,1)S(1)} custom-call(s32[2]{0:T(128)S(1)} %pad_add_fusion.info_ref, bf16[1024,576]{1,0:T(8,128)(2,1)S(1)} %add_convert_fusion.qkv_ref, bf16[1024,192]{1,0:T(8,128)(2,1)S(1)} %pad_maximum_fusion.5.grad_ref), custom_call_target="tpu_custom_call" | custom-call | flops 8053063680 | bytes 2752512 | tf_op jit(solution)/shard_map/attend_back/pallas_call | solution.py:182
  159.6 1.2 convolution_convert_fusion.2
  162.2 1.2 pad_maximum_fusion.2
  163.4 5.5 %all-to-all-start.1 = ((bf16[32,24,588]{2,1,0:T(8,128)(2,1)}), bf16[32,24,588]{2,1,0:T(8,128)(2,1)S(1)}, u32[]{:S(2)}, u32[]{:S(2)}) async-start(bf16[32,24,588]{2,1,0:T(8,128)(2,1)} %pad_maximum_fusion.2), calls=%async_computation.1 | async-start | bytes 1966080 | tf_op jit(solution)/shard_map/all_to_all | solution.py:390
  168.9 2.7 %convolution_convert_fusion.1 = bf16[1024,768]{1,0:T(8,128)(2,1)S(1)} fusion(bf16[1024,576]{1,0:T(8,128)(2,1)S(1)} %attend_back.1, bf16[768,576]{1,0:T(8,128)(2,1)} %bitcast.100), kind=kOutput, calls=%fused_computation.22 | convolution fusion | flops 906756096 | bytes 3637248 | tf_op jit(solution)/shard_map/dot_general | solution.py:56
  171.6 1.1 copy-done.4
  172.8 0.9 collective-permute-start.9
  173.7 2.1 collective-permute-start.11
  176.1 8.7 %collective-permute-done.9 = bf16[256,768]{1,0:T(8,128)(2,1)S(1)} collective-permute-done((bf16[256,768]{1,0:T(8,128)(2,1)S(1)}, bf16[256,768]{1,0:T(8,128)(2,1)S(1)}, u32[]{:S(2)}, u32[]{:S(2)}) %collective-permute-start.9) | collective-permute-done | bytes 393248 | tf_op jit(solution)/shard_map/ppermute | solution.py:70
  184.8 2.5 collective-permute-done.11
  187.3 7.4 %collective-permute-done.10 = bf16[256,768]{1,0:T(8,128)(2,1)} collective-permute-done((bf16[256,768]{1,0:T(8,128)(2,1)S(1)}, bf16[256,768]{1,0:T(8,128)(2,1)}, u32[]{:S(2)}, u32[]{:S(2)}) %collective-permute-start.10) | collective-permute-done | bytes 393248 | tf_op jit(solution)/shard_map/ppermute | solution.py:70
  194.7 2.2 fusion.22
  197.1 0.8 collective-permute-start.14
  197.9 2.0 collective-permute-start.13
  200.4 4.6 %collective-permute-done.12 = bf16[24,588]{1,0:T(8,128)(2,1)S(1)} collective-permute-done((bf16[24,588]{1,0:T(8,128)(2,1)S(1)}, bf16[24,588]{1,0:T(8,128)(2,1)S(1)}, u32[]{:S(2)}, u32[]{:S(2)}) %collective-permute-start.12) | collective-permute-done | bytes 28256 | tf_op jit(solution)/shard_map/ppermute | solution.py:70
  206.3 0.9 reshape.192
  207.1 21.5 %reduce-scatter.2.cloned.1.call-done = bf16[24,6912]{1,0:T(8,128)(2,1)} async-done(((bf16[768,6912]{1,0:T(8,128)(2,1)}), bf16[24,6912]{1,0:T(8,128)(2,1)}) %reduce-scatter.2.cloned.1.call-update) | async-done | bytes 331792 | tf_op jit(solution)/shard_map/reduce_scatter | solution.py:365
  228.7 1.4 collective-permute-start.17
  230.1 3.2 %collective-permute-start.15 = (bf16[24,6912]{1,0:T(8,128)(2,1)}, bf16[24,6912]{1,0:T(8,128)(2,1)S(1)}, u32[]{:S(2)}, u32[]{:S(2)}) collective-permute-start(bf16[24,6912]{1,0:T(8,128)(2,1)} %reduce-scatter.2.cloned.1.call-done), channel_id=1, source_target_pairs={{0,1},{1,2},{2,3},{3,0},{4,5},{5,6},{6,7},{7,4},{8,9},{9,10},{10,1... | collective-permute-start | bytes 995336 | tf_op jit(solution)/shard_map/ppermute | solution.py:70
  233.3 0.8 slice_reduce_fusion.1
  234.2 7.0 %collective-permute-done.17 = bf16[24,6912]{1,0:T(8,128)(2,1)S(1)} collective-permute-done((bf16[24,6912]{1,0:T(8,128)(2,1)}, bf16[24,6912]{1,0:T(8,128)(2,1)S(1)}, u32[]{:S(2)}, u32[]{:S(2)}) %collective-permute-start.17) | collective-permute-done | bytes 331808 | tf_op jit(solution)/shard_map/ppermute | solution.py:70
  241.1 4.4 %collective-permute-done.16 = bf16[24,6912]{1,0:T(8,128)(2,1)S(1)} collective-permute-done((bf16[24,6912]{1,0:T(8,128)(2,1)}, bf16[24,6912]{1,0:T(8,128)(2,1)S(1)}, u32[]{:S(2)}, u32[]{:S(2)}) %collective-permute-start.16) | collective-permute-done | bytes 331808 | tf_op jit(solution)/shard_map/ppermute | solution.py:70
  245.5 1.2 convert_add_fusion
  247.3 0.8 fusion.43
  248.2 0.8 copy.80
  (156 shorter events, 16.5 us)
Async XLA Ops:
  7.2 22.2 %copy-start.15 = (bf16[1,256,768]{2,1,0:T(8,128)(2,1)S(1)}, bf16[1,256,768]{2,1,0:T(8,128)(2,1)}, u32[]{:S(2)}) copy-start(bf16[1,256,768]{2,1,0:T(8,128)(2,1)} %param.16) | copy-start | bytes 1179652
  7.2 81.3 %all-gather.3.cloned.1.call-start = ((), (), s32[]{:S(2)}) async-start(), calls=%async_computation.4 | async-start | bytes 11354112 | tf_op jit(solution)/shard_map/all_gather | solution.py:282
  16.8 0.7 copy-start.14
  21.0 34.1 %all-to-all-start = ((bf16[32,26,576]{2,1,0:T(8,128)(2,1)}), bf16[32,26,576]{2,1,0:T(8,128)(2,1)S(1)}, u32[]{:S(2)}, u32[]{:S(2)}) async-start(bf16[32,26,576]{2,1,0:T(8,128)(2,1)} %broadcast_in_dim.107), calls=%async_computation | async-start | bytes 2621440 | tf_op jit(solution)/shard_map/all_to_all | solution.py:298
  29.3 199.4 %reduce-scatter.2.cloned.1.call-start = ((), (), s32[]{:S(2)}) async-start(), calls=%async_computation.3 | async-start | bytes 10948608 | tf_op jit(solution)/shard_map/reduce_scatter | solution.py:365
  29.4 26.3 %collective-permute-start.2 = (bf16[256,768]{1,0:T(8,128)(2,1)S(1)}, bf16[256,768]{1,0:T(8,128)(2,1)S(1)}, u32[]{:S(2)}, u32[]{:S(2)}) collective-permute-start(bf16[256,768]{1,0:T(8,128)(2,1)S(1)} %bitcast.102), channel_id=1, source_target_pairs={{0,1},{1,2},{2,3},{3,0},{4,5},{5,6},{6,7},{7,4},{8,9},{9,10},{10,1... | collective-permute-start | bytes 1179656 | tf_op jit(solution)/shard_map/ppermute | solution.py:70
  29.9 25.8 %collective-permute-start.1 = (bf16[256,768]{1,0:T(8,128)(2,1)S(1)}, bf16[256,768]{1,0:T(8,128)(2,1)S(1)}, u32[]{:S(2)}, u32[]{:S(2)}) collective-permute-start(bf16[256,768]{1,0:T(8,128)(2,1)S(1)} %bitcast.103), channel_id=1, source_target_pairs={{0,2},{1,3},{2,0},{3,1},{4,6},{5,7},{6,4},{7,5},{8,10},{9,11},{10,... | collective-permute-start | bytes 1179656 | tf_op jit(solution)/shard_map/ppermute | solution.py:70
  32.3 23.4 %collective-permute-start = (bf16[256,768]{1,0:T(8,128)(2,1)S(1)}, bf16[256,768]{1,0:T(8,128)(2,1)S(1)}, u32[]{:S(2)}, u32[]{:S(2)}) collective-permute-start(bf16[256,768]{1,0:T(8,128)(2,1)S(1)} %bitcast.104), channel_id=1, source_target_pairs={{0,3},{1,0},{2,1},{3,2},{4,7},{5,4},{6,5},{7,6},{8,11},{9,8},{10,9... | collective-permute-start | bytes 1179656 | tf_op jit(solution)/shard_map/ppermute | solution.py:70
  55.6 1.0 copy-start.12
  55.7 2.3 copy-start.17
  55.7 2.3 copy-start.19
  55.7 2.3 copy-start.21
  65.6 6.4 %collective-permute-start.5 = (bf16[256,192]{1,0:T(8,128)(2,1)S(1)}, bf16[256,192]{1,0:T(8,128)(2,1)S(1)}, u32[]{:S(2)}, u32[]{:S(2)}) collective-permute-start(bf16[256,192]{1,0:T(8,128)(2,1)S(1)} %get-tuple-element.55), channel_id=1, source_target_pairs={{0,1},{1,2},{2,3},{3,0},{4,5},{5,6},{6,7},{7,4},{8,9},{9,10},{10,1... | collective-permute-start | bytes 294920 | tf_op jit(solution)/shard_map/ppermute | solution.py:70
  66.1 7.6 %collective-permute-start.4 = (bf16[256,192]{1,0:T(8,128)(2,1)S(1)}, bf16[256,192]{1,0:T(8,128)(2,1)S(1)}, u32[]{:S(2)}, u32[]{:S(2)}) collective-permute-start(bf16[256,192]{1,0:T(8,128)(2,1)S(1)} %get-tuple-element.56), channel_id=1, source_target_pairs={{0,2},{1,3},{2,0},{3,1},{4,6},{5,7},{6,4},{7,5},{8,10},{9,11},{10,... | collective-permute-start | bytes 294920 | tf_op jit(solution)/shard_map/ppermute | solution.py:70
  68.6 7.0 %collective-permute-start.3 = (bf16[256,192]{1,0:T(8,128)(2,1)S(1)}, bf16[256,192]{1,0:T(8,128)(2,1)S(1)}, u32[]{:S(2)}, u32[]{:S(2)}) collective-permute-start(bf16[256,192]{1,0:T(8,128)(2,1)S(1)} %get-tuple-element.57), channel_id=1, source_target_pairs={{0,3},{1,0},{2,1},{3,2},{4,7},{5,4},{6,5},{7,6},{8,11},{9,8},{10,9... | collective-permute-start | bytes 294920 | tf_op jit(solution)/shard_map/ppermute | solution.py:70
  101.5 2.9 %copy-start.5 = (bf16[32,24,768]{2,1,0:T(8,128)(2,1)S(1)}, bf16[32,24,768]{2,1,0:T(8,128)(2,1)}, u32[]{:S(2)}) copy-start(bf16[32,24,768]{2,1,0:T(8,128)(2,1)} %get-tuple-element.43) | copy-start | bytes 3538948
  101.5 2.9 %copy-start.6 = (bf16[32,24,768]{2,1,0:T(8,128)(2,1)S(1)}, bf16[32,24,768]{2,1,0:T(8,128)(2,1)}, u32[]{:S(2)}) copy-start(bf16[32,24,768]{2,1,0:T(8,128)(2,1)} %get-tuple-element.44) | copy-start | bytes 3538948
  101.5 2.9 %copy-start.8 = (bf16[32,24,768]{2,1,0:T(8,128)(2,1)S(1)}, bf16[32,24,768]{2,1,0:T(8,128)(2,1)}, u32[]{:S(2)}) copy-start(bf16[32,24,768]{2,1,0:T(8,128)(2,1)} %get-tuple-element.45) | copy-start | bytes 3538948
  101.6 2.9 %copy-start.10 = (bf16[32,24,768]{2,1,0:T(8,128)(2,1)S(1)}, bf16[32,24,768]{2,1,0:T(8,128)(2,1)}, u32[]{:S(2)}) copy-start(bf16[32,24,768]{2,1,0:T(8,128)(2,1)} %get-tuple-element.46) | copy-start | bytes 3538948
  104.2 6.0 %slice-start = ((s8[4718592]{0:T(1024)(128)(4,1)}), s8[4194304]{0:T(1024)(128)(4,1)S(1)}, s32[]{:S(2)}) async-start(s8[4718592]{0:T(1024)(128)(4,1)} %bitcast.83), calls=%async_computation.5 | async-start | bytes 8388608
  104.5 5.8 %slice-start.1 = ((s8[4718592]{0:T(1024)(128)(4,1)}), s8[524288]{0:T(1024)(128)(4,1)S(1)}, s32[]{:S(2)}) async-start(s8[4718592]{0:T(1024)(128)(4,1)} %bitcast.83), calls=%async_computation.6 | async-start | bytes 1048576
  110.3 1.7 copy-start.1
  116.0 4.6 %copy-start.7 = (bf16[32,24,768]{2,1,0:T(8,128)(2,1)S(1)}, bf16[32,24,768]{2,1,0:T(8,128)(2,1)}, u32[]{:S(2)}) copy-start(bf16[32,24,768]{2,1,0:T(8,128)(2,1)} %get-tuple-element.44) | copy-start | bytes 3538948
  116.0 4.6 %copy-start.9 = (bf16[32,24,768]{2,1,0:T(8,128)(2,1)S(1)}, bf16[32,24,768]{2,1,0:T(8,128)(2,1)}, u32[]{:S(2)}) copy-start(bf16[32,24,768]{2,1,0:T(8,128)(2,1)} %get-tuple-element.45) | copy-start | bytes 3538948
  116.0 4.6 %copy-start.11 = (bf16[32,24,768]{2,1,0:T(8,128)(2,1)S(1)}, bf16[32,24,768]{2,1,0:T(8,128)(2,1)}, u32[]{:S(2)}) copy-start(bf16[32,24,768]{2,1,0:T(8,128)(2,1)} %get-tuple-element.46) | copy-start | bytes 3538948
  127.5 4.0 %copy-start = (bf16[768,6912]{1,0:T(8,128)(2,1)}, bf16[768,6912]{1,0:T(8,128)(2,1)S(1)}, u32[]{:S(2)}) copy-start(bf16[768,6912]{1,0:T(8,128)(2,1)S(1)} %other_grads.1) | copy-start | bytes 31850500
  131.5 3.7 %copy-start.2 = (bf16[1,256,768]{2,1,0:T(8,128)(2,1)S(1)}, bf16[1,256,768]{2,1,0:T(8,128)(2,1)}, u32[]{:S(2)}) copy-start(bf16[1,256,768]{2,1,0:T(8,128)(2,1)} %param.31) | copy-start | bytes 1179652
  132.2 6.4 %collective-permute-start.8 = (bf16[256,192]{1,0:T(8,128)(2,1)S(1)}, bf16[256,192]{1,0:T(8,128)(2,1)S(1)}, u32[]{:S(2)}, u32[]{:S(2)}) collective-permute-start(bf16[256,192]{1,0:T(8,128)(2,1)S(1)} %get-tuple-element.59), channel_id=1, source_target_pairs={{0,1},{1,2},{2,3},{3,0},{4,5},{5,6},{6,7},{7,4},{8,9},{9,10},{10,1... | collective-permute-start | bytes 294920 | tf_op jit(solution)/shard_map/ppermute | solution.py:70
  132.8 7.9 %collective-permute-start.7 = (bf16[256,192]{1,0:T(8,128)(2,1)S(1)}, bf16[256,192]{1,0:T(8,128)(2,1)S(1)}, u32[]{:S(2)}, u32[]{:S(2)}) collective-permute-start(bf16[256,192]{1,0:T(8,128)(2,1)S(1)} %get-tuple-element.60), channel_id=1, source_target_pairs={{0,2},{1,3},{2,0},{3,1},{4,6},{5,7},{6,4},{7,5},{8,10},{9,11},{10,... | collective-permute-start | bytes 294920 | tf_op jit(solution)/shard_map/ppermute | solution.py:70
  135.1 7.4 %collective-permute-start.6 = (bf16[256,192]{1,0:T(8,128)(2,1)S(1)}, bf16[256,192]{1,0:T(8,128)(2,1)S(1)}, u32[]{:S(2)}, u32[]{:S(2)}) collective-permute-start(bf16[256,192]{1,0:T(8,128)(2,1)S(1)} %get-tuple-element.61), channel_id=1, source_target_pairs={{0,3},{1,0},{2,1},{3,2},{4,7},{5,4},{6,5},{7,6},{8,11},{9,8},{10,9... | collective-permute-start | bytes 294920 | tf_op jit(solution)/shard_map/ppermute | solution.py:70
  142.6 17.0 %copy-start.16 = (bf16[1,256,768]{2,1,0:T(8,128)(2,1)S(1)}, bf16[1,256,768]{2,1,0:T(8,128)(2,1)}, u32[]{:S(2)}) copy-start(bf16[1,256,768]{2,1,0:T(8,128)(2,1)} %param.16) | copy-start | bytes 1179652
  142.6 17.0 %copy-start.18 = (bf16[256,768]{1,0:T(8,128)(2,1)S(1)}, bf16[256,768]{1,0:T(8,128)(2,1)}, u32[]{:S(2)}) copy-start(bf16[256,768]{1,0:T(8,128)(2,1)} %copy-done.17) | copy-start | bytes 1179652
  142.6 17.0 %copy-start.20 = (bf16[256,768]{1,0:T(8,128)(2,1)S(1)}, bf16[256,768]{1,0:T(8,128)(2,1)}, u32[]{:S(2)}) copy-start(bf16[256,768]{1,0:T(8,128)(2,1)} %copy-done.19) | copy-start | bytes 1179652
  142.6 17.0 %copy-start.22 = (bf16[256,768]{1,0:T(8,128)(2,1)S(1)}, bf16[256,768]{1,0:T(8,128)(2,1)}, u32[]{:S(2)}) copy-start(bf16[256,768]{1,0:T(8,128)(2,1)} %copy-done.21) | copy-start | bytes 1179652
  160.7 1.4 copy-start.13
  163.4 33.6 %all-to-all-start.1 = ((bf16[32,24,588]{2,1,0:T(8,128)(2,1)}), bf16[32,24,588]{2,1,0:T(8,128)(2,1)S(1)}, u32[]{:S(2)}, u32[]{:S(2)}) async-start(bf16[32,24,588]{2,1,0:T(8,128)(2,1)} %pad_maximum_fusion.2), calls=%async_computation.1 | async-start | bytes 1966080 | tf_op jit(solution)/shard_map/all_to_all | solution.py:390
  168.8 25.9 %copy-start.3 = (f32[256,768]{1,0:T(8,128)S(1)}, f32[256,768]{1,0:T(8,128)}, u32[]{:S(2)}) copy-start(f32[256,768]{1,0:T(8,128)} %get-tuple-element.36) | copy-start | bytes 2359300
  171.6 1.1 copy-start.4
  172.8 12.0 %collective-permute-start.9 = (bf16[256,768]{1,0:T(8,128)(2,1)S(1)}, bf16[256,768]{1,0:T(8,128)(2,1)S(1)}, u32[]{:S(2)}, u32[]{:S(2)}) collective-permute-start(bf16[256,768]{1,0:T(8,128)(2,1)S(1)} %get-tuple-element.48), channel_id=1, source_target_pairs={{0,1},{1,2},{2,3},{3,0},{4,5},{5,6},{6,7},{7,4},{8,9},{9,10},{10,1... | collective-permute-start | bytes 1179656 | tf_op jit(solution)/shard_map/ppermute | solution.py:70
  173.7 13.6 %collective-permute-start.11 = (bf16[256,768]{1,0:T(8,128)(2,1)S(1)}, bf16[256,768]{1,0:T(8,128)(2,1)}, u32[]{:S(2)}, u32[]{:S(2)}) collective-permute-start(bf16[256,768]{1,0:T(8,128)(2,1)S(1)} %get-tuple-element.49), channel_id=1, source_target_pairs={{0,2},{1,3},{2,0},{3,1},{4,6},{5,7},{6,4},{7,5},{8,10},{9,11},{10,... | collective-permute-start | bytes 1179656 | tf_op jit(solution)/shard_map/ppermute | solution.py:70
  175.8 19.0 %collective-permute-start.10 = (bf16[256,768]{1,0:T(8,128)(2,1)S(1)}, bf16[256,768]{1,0:T(8,128)(2,1)}, u32[]{:S(2)}, u32[]{:S(2)}) collective-permute-start(bf16[256,768]{1,0:T(8,128)(2,1)S(1)} %get-tuple-element.50), channel_id=1, source_target_pairs={{0,3},{1,0},{2,1},{3,2},{4,7},{5,4},{6,5},{7,6},{8,11},{9,8},{10,9... | collective-permute-start | bytes 1179656 | tf_op jit(solution)/shard_map/ppermute | solution.py:70
  197.1 7.9 %collective-permute-start.14 = (bf16[24,588]{1,0:T(8,128)(2,1)S(1)}, bf16[24,588]{1,0:T(8,128)(2,1)S(1)}, u32[]{:S(2)}, u32[]{:S(2)}) collective-permute-start(bf16[24,588]{1,0:T(8,128)(2,1)S(1)} %reduce_sum.181), channel_id=1, source_target_pairs={{0,1},{1,2},{2,3},{3,0},{4,5},{5,6},{6,7},{7,4},{8,9},{9,10},{10,1... | collective-permute-start | bytes 84680 | tf_op jit(solution)/shard_map/ppermute | solution.py:70
  197.9 7.1 %collective-permute-start.13 = (bf16[24,588]{1,0:T(8,128)(2,1)S(1)}, bf16[24,588]{1,0:T(8,128)(2,1)S(1)}, u32[]{:S(2)}, u32[]{:S(2)}) collective-permute-start(bf16[24,588]{1,0:T(8,128)(2,1)S(1)} %reduce_sum.181), channel_id=1, source_target_pairs={{0,2},{1,3},{2,0},{3,1},{4,6},{5,7},{6,4},{7,5},{8,10},{9,11},{10,... | collective-permute-start | bytes 84680 | tf_op jit(solution)/shard_map/ppermute | solution.py:70
  199.9 5.1 %collective-permute-start.12 = (bf16[24,588]{1,0:T(8,128)(2,1)S(1)}, bf16[24,588]{1,0:T(8,128)(2,1)S(1)}, u32[]{:S(2)}, u32[]{:S(2)}) collective-permute-start(bf16[24,588]{1,0:T(8,128)(2,1)S(1)} %reduce_sum.181), channel_id=1, source_target_pairs={{0,3},{1,0},{2,1},{3,2},{4,7},{5,4},{6,5},{7,6},{8,11},{9,8},{10,9... | collective-permute-start | bytes 84680 | tf_op jit(solution)/shard_map/ppermute | solution.py:70
  228.7 12.5 %collective-permute-start.17 = (bf16[24,6912]{1,0:T(8,128)(2,1)}, bf16[24,6912]{1,0:T(8,128)(2,1)S(1)}, u32[]{:S(2)}, u32[]{:S(2)}) collective-permute-start(bf16[24,6912]{1,0:T(8,128)(2,1)} %reduce-scatter.2.cloned.1.call-done), channel_id=1, source_target_pairs={{0,2},{1,3},{2,0},{3,1},{4,6},{5,7},{6,4},{7,5},{8,10},{9,11},{10,... | collective-permute-start | bytes 995336 | tf_op jit(solution)/shard_map/ppermute | solution.py:70
  230.1 15.4 %collective-permute-start.16 = (bf16[24,6912]{1,0:T(8,128)(2,1)}, bf16[24,6912]{1,0:T(8,128)(2,1)S(1)}, u32[]{:S(2)}, u32[]{:S(2)}) collective-permute-start(bf16[24,6912]{1,0:T(8,128)(2,1)} %reduce-scatter.2.cloned.1.call-done), channel_id=1, source_target_pairs={{0,3},{1,0},{2,1},{3,2},{4,7},{5,4},{6,5},{7,6},{8,11},{9,8},{10,9... | collective-permute-start | bytes 995336 | tf_op jit(solution)/shard_map/ppermute | solution.py:70
  230.1 15.4 %collective-permute-start.15 = (bf16[24,6912]{1,0:T(8,128)(2,1)}, bf16[24,6912]{1,0:T(8,128)(2,1)S(1)}, u32[]{:S(2)}, u32[]{:S(2)}) collective-permute-start(bf16[24,6912]{1,0:T(8,128)(2,1)} %reduce-scatter.2.cloned.1.call-done), channel_id=1, source_target_pairs={{0,1},{1,2},{2,3},{3,0},{4,5},{5,6},{6,7},{7,4},{8,9},{9,10},{10,1... | collective-permute-start | bytes 995336 | tf_op jit(solution)/shard_map/ppermute | solution.py:70
Sparse Core Ops, SparseCore 0:
  17.7 70.7 all-gather.2
  131.6 97.0 reduce-scatter.1
where the time goes:
time: 257 us; the launch traced here: 256 us
  waiting for transfers between devices  104 us (40%)
  local copies, waits for them, and re-layouts  39.7 us (15%)
  starting transfers between devices  34 us (13%)
  Pallas kernels  30.7 us (12%)
  matrix products  19.9 us (8%)
  between operations  15.5 us (6%)
  other arithmetic  12 us (5%)
    ppermute x18, waiting for transfers between devices, to_x(): return lax.ppermute(values, 'sp', [(i, (i + step) % SP) for i in range(SP)])  47.7 us
    all_to_all x1, waiting for transfers between devices, per_device(): lax.all_to_all(jnp.broadcast_to(early[None], (32, 26, 3 * HW)), 'fsdp', s...  22 us
    reduce_scatter x1, waiting for transfers between devices, per_device(): lax.psum_scatter(packed_grads, 'fsdp', scatter_dimension=0, tiled=True)  21.5 us
    ppermute x18, starting transfers between devices, to_x(): return lax.ppermute(values, 'sp', [(i, (i + step) % SP) for i in range(SP)])  20.1 us
    pallas_call x1, Pallas kernels, attend_back(): pl.pallas_call(attend_back_kernel, out_shape=jax.ShapeDtypeStruct((LEN, 3...  16.9 us
    all_gather x1, waiting for transfers between devices, per_device(): packed = lax.all_gather(packed, 'fsdp', axis=0, tiled=False)  12.7 us
    unnamed x63, local copies, waits for them, and re-layouts  11.7 us
    dot_general x4, matrix products, by_transpose(): lax.dot_general(left_side, right_side, (((1,), (1,)), ((), ())), preferre...  9.58 us
  transfers between devices with their start and end apart: 22, of which 15 were waited for; matrix products, arithmetic and copies ran while one was open for 8% of the time, Pallas kernels for 10%

commit v1 on v0

v1 whole, which is shorter than its diff:
```python
import jax
import jax.numpy as jnp
import numpy as np
from jax import lax
from jax.experimental import pallas as pl
from jax.experimental.pallas import tpu as pltpu
from jax.sharding import PartitionSpec as P

D = 768
H = 12
DH = 64
FF = 3072
SP = 4
LOCAL = 256
LEN = 1024
HEADS = H // SP
HW = HEADS * DH
BLOCK = 256

EPSILON = 1e-06
SCALING = 0.125
MASKED = -1000000000.0
F32 = jnp.float32
BF16 = jnp.bfloat16


def normalize(values, gain_row, shift_row):
    average = jnp.mean(values, axis=-1, keepdims=True)
    centred = values - average
    inv_std = lax.rsqrt(jnp.mean(centred * centred, axis=-1, keepdims=True) + EPSILON)
    normed = centred * inv_std
    return (normed * gain_row + shift_row, normed, inv_std)


def normalize_back(upstream, normed, inv_std, gain_row):
    weighted = upstream * gain_row
    return inv_std * (
        weighted
        - jnp.mean(weighted, axis=-1, keepdims=True)
        - normed * jnp.mean(weighted * normed, axis=-1, keepdims=True)
    )


def dot(left_side, right_side):
    return jnp.dot(left_side, right_side, preferred_element_type=F32)


def rows_first(left_side, right_side):
    return lax.dot_general(
        left_side, right_side, (((0,), (0,)), ((), ())), preferred_element_type=F32
    )


def by_transpose(left_side, right_side):
    return lax.dot_general(
        left_side, right_side, (((1,), (1,)), ((), ())), preferred_element_type=F32
    )


ROOT = 0.7978845608028654
CUBE = 0.044715


def gate_and_slope(values):
    square = values * values
    bent = jnp.tanh(ROOT * values * (1.0 + CUBE * square))
    half = 0.5 * (1.0 + bent)
    slope = half + 0.5 * values * (1.0 - bent * bent) * (ROOT * (1.0 + 3.0 * CUBE * square))
    return values * half, slope


def column_sum(values):
    return jnp.sum(values.astype(F32), axis=0)


def to_x(values, step):
    return lax.ppermute(values, "sp", [(i, (i + step) % SP) for i in range(SP)])


def to_z(values, step):
    return lax.ppermute(values, "fsdp", [(i, (i + 8 * step) % 32) for i in range(32)])


ORDER = (1, 3, 2)


def rolled(values, start):
    count = values.shape[0]
    return lax.dynamic_slice_in_dim(
        jnp.concatenate([values, values], axis=0), start % count, count, axis=0
    )


def masked_keys(info_ref, shape, dim):
    at = lax.broadcasted_iota(jnp.int32, shape, dim)
    block = (info_ref[0] + lax.shift_right_logical(at, 8)) & 3
    return (block * LOCAL + (at & (LOCAL - 1))) < info_ref[1]


def attend_kernel(info_ref, qkv_ref, context_ref):
    valid = masked_keys(info_ref, (1, LEN), 1)

    @pl.loop(0, LEN // BLOCK)
    def _(step):
        rows = pl.ds(pl.multiple_of(step * BLOCK, BLOCK), BLOCK)
        outs = []
        for head in range(HEADS):
            cols = head * DH
            keys = qkv_ref[:, HW + cols : HW + cols + DH]
            vals = qkv_ref[:, 2 * HW + cols : 2 * HW + cols + DH]
            queries = qkv_ref[rows, cols : cols + DH] * jnp.asarray(SCALING, BF16)
            scores = jnp.where(valid, by_transpose(queries, keys), MASKED)
            weights = jnp.exp(scores - jnp.max(scores, axis=-1, keepdims=True))
            totals = jnp.sum(weights, axis=-1, keepdims=True)
            outs.append(dot(weights.astype(BF16), vals) * (1.0 / totals))
        context_ref[rows, :] = jnp.concatenate(outs, axis=1).astype(BF16)


def attend_back_kernel(info_ref, qkv_ref, grad_ref, out_ref, key_sum, value_sum):
    valid = masked_keys(info_ref, (LEN, 1), 0)
    key_sum[...] = jnp.zeros_like(key_sum)
    value_sum[...] = jnp.zeros_like(value_sum)

    @pl.loop(0, LEN // BLOCK)
    def _(step):
        rows = pl.ds(pl.multiple_of(step * BLOCK, BLOCK), BLOCK)
        outs = []
        for head in range(HEADS):
            cols = head * DH
            keys = qkv_ref[:, HW + cols : HW + cols + DH]
            vals = qkv_ref[:, 2 * HW + cols : 2 * HW + cols + DH]
            queries = qkv_ref[rows, cols : cols + DH] * jnp.asarray(SCALING, BF16)
            grads = grad_ref[rows, cols : cols + DH]
            scores = jnp.where(valid, by_transpose(keys, queries), MASKED)
            weights = jnp.exp(scores - jnp.max(scores, axis=0, keepdims=True))
            probs = weights * (1.0 / jnp.sum(weights, axis=0, keepdims=True))
            value_sum[head] += dot(probs.astype(BF16), grads)
            prob_grad = by_transpose(vals, grads)
            centre = jnp.sum(probs * prob_grad, axis=0, keepdims=True)
            score_grad = (probs * (prob_grad - centre)).astype(BF16)
            key_sum[head] += dot(score_grad, queries)
            outs.append(rows_first(score_grad, keys) * SCALING)
        out_ref[rows, :HW] = jnp.concatenate(outs, axis=1).astype(BF16)

    for part, total in ((1, key_sum), (2, value_sum)):
        out_ref[:, part * HW : (part + 1) * HW] = jnp.concatenate(
            [total[head] for head in range(HEADS)], axis=1
        ).astype(BF16)


PACKED = 2 * FF + D


def reorder_matrix():
    source = np.arange(D).reshape(8, 4, 24).transpose(1, 0, 2).reshape(D)
    matrix = np.zeros((D, D), np.float32)
    matrix[source, np.arange(D)] = 1.0
    return matrix


def pack_kernel(info_ref, *rest):
    sources, (packed_ref, early_ref), held = rest[:14], rest[14:16], rest[16:30]
    rows_ref, sems = rest[30:]
    fetches = [
        pltpu.make_async_copy(source, target, sems.at[at])
        for at, (source, target) in enumerate(zip(sources, held))
    ]
    for fetch in fetches:
        fetch.start()
    qkv_ref, context_ref, expand_ref, reduce_ref, order_ref = held[:5]
    vector_refs = held[5:]
    for fetch in fetches:
        fetch.wait()
    reduce_rows = reduce_ref[...].astype(F32)
    for part in range(4):
        packed_ref[:, part * D : (part + 1) * D] = reduce_rows[part * 24 : (part + 1) * 24].astype(BF16)
    moved = [dot(expand_ref[:, q * D : (q + 1) * D], order_ref[...]) for q in range(4)]
    for part in range(4):
        packed_ref[:, FF + part * D : FF + (part + 1) * D] = jnp.concatenate(
            [values[:, part * HW : (part + 1) * HW] for values in moved], axis=1
        ).astype(BF16)
    packed_ref[:, 2 * FF :] = context_ref[...]

    rows_ref[...] = jnp.zeros_like(rows_ref)
    for row in range(8):
        rows_ref[row : row + 1, :24] = vector_refs[row][...].astype(F32).reshape(1, 24)
    rows_ref[0:1, 128:224] = vector_refs[8][...].astype(F32).reshape(1, 96)
    for at in range(SP):

        @pl.when(info_ref[0] == at)
        def _(at=at):
            own = jnp.concatenate(
                [qkv_ref[:, part * D + at * HW : part * D + (at + 1) * HW] for part in range(3)],
                axis=1,
            )
            block = jnp.concatenate([own.astype(F32), rows_ref[...]], axis=0).astype(BF16)

            @pl.loop(0, 32)
            def _(owner):
                early_ref[owner] = block


def middle_kernel(
    info_ref, context_ref, own_ref, cotangent_ref, rows_ref, bias_ref, weights_ref,
    hidden_ref, grad_one_ref, context_grad_ref, sums_ref, bias_sum_ref, grads_ref,
    held, made, slopes, active, in_sems, out_sems,
):
    def piece(block):
        return slice(block * D, (block + 1) * D)

    copies = {}
    for block in (8, 4, 0, 5, 1, 6, 2, 7, 3):
        copies[block] = pltpu.make_async_copy(
            weights_ref.at[:, piece(block)], held.at[:, piece(block)], in_sems.at[block]
        )
        copies[block].start()

    def send(block):
        copy = pltpu.make_async_copy(
            made.at[:, piece(block)], grads_ref.at[:, piece(block)], out_sems.at[block]
        )
        copy.start()
        return copy

    context_add, gain_one, shift_one, reduce_add, gain_two, shift_two = (
        rows_ref[row : row + 1, :] for row in range(2, 8)
    )
    groups = [(z - info_ref[0]) & 3 for z in range(SP)]

    def by_plane(values):
        return jnp.concatenate(
            [values[(8 * z + m) * 24 : (8 * z + m + 1) * 24] for m in range(8) for z in range(4)],
            axis=0,
        ).astype(BF16)

    own = own_ref[...].astype(F32) + context_add
    copies[8].wait()
    for block in range(SP):
        own = own + dot(
            context_ref[groups[block]], held[block * HW : (block + 1) * HW, piece(8)]
        )
    first_out, normed_one, inv_one = normalize(own, gain_one, shift_one)
    first_low = first_out.astype(BF16)
    second_in = first_out + reduce_add
    for part in range(4):
        copies[4 + part].wait()
        expand = dot(first_low, held[:, piece(4 + part)]) + bias_ref[:, piece(part)]
        value, slope = gate_and_slope(expand)
        active[:, piece(part)] = value.astype(BF16)
        slopes[:, piece(part)] = slope
        copies[part].wait()
        second_in = second_in + dot(active[:, piece(part)], held[:, piece(part)])
    second_out, normed_two, inv_two = normalize(second_in, gain_two, shift_two)
    hidden_ref[...] = second_out.astype(BF16)

    cotangent = cotangent_ref[...].astype(F32)
    grad_two = normalize_back(cotangent, normed_two, inv_two, gain_two)
    reduced_grad = grad_two.astype(BF16)
    sums_ref[...] = jnp.zeros_like(sums_ref)
    sums_ref[3:4, :] = jnp.sum(reduced_grad.astype(F32), axis=0, keepdims=True)
    sums_ref[4:5, :] = jnp.sum(cotangent * normed_two, axis=0, keepdims=True)
    sums_ref[5:6, :] = jnp.sum(cotangent, axis=0, keepdims=True)
    first_grad = grad_two
    sent = []
    for part in range(4):
        active_grad = by_transpose(reduced_grad, held[:, piece(part)]).astype(BF16)
        expand_grad = (active_grad.astype(F32) * slopes[:, piece(part)]).astype(BF16)
        bias_sum_ref[part : part + 1, :] = jnp.sum(expand_grad.astype(F32), axis=0, keepdims=True)
        first_grad = first_grad + by_transpose(expand_grad, held[:, piece(4 + part)])
        made[:, piece(part)] = by_plane(rows_first(active[:, piece(part)], reduced_grad))
        sent.append(send(part))
        made[:, piece(4 + part)] = by_plane(rows_first(first_low, expand_grad))
        sent.append(send(4 + part))
    sums_ref[1:2, :] = jnp.sum(first_grad * normed_one, axis=0, keepdims=True)
    sums_ref[2:3, :] = jnp.sum(first_grad, axis=0, keepdims=True)
    grad_one = normalize_back(first_grad, normed_one, inv_one, gain_one)
    grad_one_ref[...] = grad_one
    branch_grad = grad_one.astype(BF16)
    sums_ref[0:1, :] = jnp.sum(branch_grad.astype(F32), axis=0, keepdims=True)
    made[:, piece(8)] = by_plane(
        jnp.concatenate([rows_first(context_ref[group], branch_grad) for group in groups], axis=0)
    )
    sent.append(send(8))
    for block in range(SP):
        context_grad_ref[groups[block]] = by_transpose(
            branch_grad, held[block * HW : (block + 1) * HW, piece(8)]
        ).astype(BF16)
    for copy in sent:
        copy.wait()


SMEM = pl.BlockSpec(memory_space=pltpu.SMEM)
VMEM = pl.BlockSpec(memory_space=pltpu.VMEM)
PARAMS = pltpu.CompilerParams(vmem_limit_bytes=40 * 1024 * 1024)


def attend(info, qkv):
    return pl.pallas_call(
        attend_kernel,
        out_shape=jax.ShapeDtypeStruct((LEN, HW), BF16),
        in_specs=[SMEM, VMEM],
        out_specs=VMEM,
        compiler_params=PARAMS,
        cost_estimate=pl.CostEstimate(
            flops=4 * HEADS * LEN * LEN * 256, bytes_accessed=LEN * HW * 8, transcendentals=0
        ),
        name="attend",
    )(info, qkv)


def attend_back(info, qkv, grads):
    return pl.pallas_call(
        attend_back_kernel,
        out_shape=jax.ShapeDtypeStruct((LEN, 3 * HW), BF16),
        in_specs=[SMEM, VMEM, VMEM],
        out_specs=VMEM,
        scratch_shapes=[pltpu.VMEM((HEADS, LEN, DH), F32), pltpu.VMEM((HEADS, LEN, DH), F32)],
        compiler_params=PARAMS,
        cost_estimate=pl.CostEstimate(
            flops=10 * HEADS * LEN * LEN * 256, bytes_accessed=LEN * HW * 14, transcendentals=0
        ),
        name="attend_back",
    )(info, qkv, grads)


def pack(info, qkv_weight, context_weight, expand_weight, reduce_weight, vectors):
    operands = (
        qkv_weight, context_weight, expand_weight, reduce_weight,
        jnp.asarray(reorder_matrix(), BF16), *vectors,
    )
    return pl.pallas_call(
        pack_kernel,
        out_shape=(
            jax.ShapeDtypeStruct((24, PACKED), BF16),
            jax.ShapeDtypeStruct((32, 32, 3 * HW), BF16),
        ),
        in_specs=[SMEM] + [pl.BlockSpec(memory_space=pltpu.HBM)] * len(operands),
        out_specs=(VMEM, VMEM),
        scratch_shapes=[pltpu.VMEM(operand.shape, BF16) for operand in operands]
        + [pltpu.VMEM((8, 3 * HW), F32), pltpu.SemaphoreType.DMA((len(operands),))],
        compiler_params=pltpu.CompilerParams(vmem_limit_bytes=60 * 1024 * 1024),
        name="pack",
    )(info, *operands)


def finish_kernel(a_ref, b_ref, c_ref, d_ref, order_ref, reduce_ref, expand_ref, context_ref):
    def total(start, width):
        parts = [ref[:, start : start + width].astype(F32) for ref in (a_ref, b_ref, c_ref, d_ref)]
        return (parts[0] + parts[1]) + (parts[2] + parts[3])

    for part in range(4):
        reduce_ref[part * 24 : (part + 1) * 24, :] = total(part * D, D)
    context_ref[...] = total(2 * FF, D)
    moved = [total(FF + part * D, D) for part in range(4)]
    for q in range(4):
        left = jnp.concatenate([values[:, q * HW : (q + 1) * HW] for values in moved], axis=1)
        result = jnp.zeros((24, D), F32)
        for _ in range(3):
            term = left.astype(BF16)
            result = result + by_transpose(term, order_ref[...])
            left = left - term.astype(F32)
        expand_ref[:, q * D : (q + 1) * D] = result


def finish(pieces):
    return pl.pallas_call(
        finish_kernel,
        out_shape=(
            jax.ShapeDtypeStruct((96, D), F32),
            jax.ShapeDtypeStruct((24, FF), F32),
            jax.ShapeDtypeStruct((24, D), F32),
        ),
        in_specs=[VMEM] * 5,
        out_specs=(VMEM,) * 3,
        compiler_params=PARAMS,
        name="finish",
    )(*pieces, jnp.asarray(reorder_matrix(), BF16))


def middle(info, context_tok, own, cotangent, rows, bias, weights):
    tall = (LOCAL, D)
    return pl.pallas_call(
        middle_kernel,
        out_shape=(
            jax.ShapeDtypeStruct(tall, BF16),
            jax.ShapeDtypeStruct(tall, F32),
            jax.ShapeDtypeStruct((SP, LOCAL, HW), BF16),
            jax.ShapeDtypeStruct((8, D), F32),
            jax.ShapeDtypeStruct((4, D), F32),
            jax.ShapeDtypeStruct((D, PACKED), BF16),
        ),
        in_specs=[SMEM] + [VMEM] * 5 + [pl.BlockSpec(memory_space=pl.ANY)],
        out_specs=(VMEM,) * 5 + (pl.BlockSpec(memory_space=pl.ANY),),
        scratch_shapes=[
            pltpu.VMEM((D, PACKED), BF16),
            pltpu.VMEM((D, PACKED), BF16),
            pltpu.VMEM((LOCAL, FF), F32),
            pltpu.VMEM((LOCAL, FF), BF16),
            pltpu.SemaphoreType.DMA((9,)),
            pltpu.SemaphoreType.DMA((9,)),
        ],
        compiler_params=pltpu.CompilerParams(vmem_limit_bytes=48 * 1024 * 1024),
        cost_estimate=pl.CostEstimate(
            flops=6 * LOCAL * D * PACKED, bytes_accessed=24 * 1024 * 1024, transcendentals=0
        ),
        name="middle",
    )(info, context_tok, own, cotangent, rows, bias, weights)


def from_x(values, x_at):
    pieces = [values] + [to_x(values, -step) for step in (1, 2, 3)]
    return rolled(jnp.stack(pieces), SP - x_at)


def per_device(
    hidden_in,
    lengths,
    qkv_weight,
    query_bias,
    value_bias,
    context_weight,
    context_bias,
    first_gain,
    first_shift,
    expand_weight,
    expand_bias,
    reduce_weight,
    reduce_bias,
    second_gain,
    second_shift,
    out_grad,
):
    x_at = lax.axis_index("sp")
    own = hidden_in[0]
    tokens = [own] + [None] * 3
    for step in ORDER:
        tokens[step] = to_x(own, -step)

    info = jnp.stack([x_at.astype(jnp.int32), lengths[0]])
    packed, early = pack(
        info, qkv_weight, context_weight, expand_weight, reduce_weight,
        (query_bias, value_bias, context_bias, first_gain, first_shift, reduce_bias,
         second_gain, second_shift, expand_bias),
    )
    packed = lax.all_gather(packed, "fsdp", axis=0, tiled=True)
    early = lax.all_to_all(early, "fsdp", split_axis=0, concat_axis=0, tiled=True)
    qkv_full = early[:, :24].reshape(D, 3 * HW)
    rows = jnp.swapaxes(early[:, 24:, :24], 0, 1).reshape(8, D).astype(F32)
    query_full, value_full = rows[0], rows[1]
    expand_add = jnp.swapaxes(early[:, 24, 128:224].reshape(32, 4, 24), 0, 1)
    expand_add = expand_add.reshape(1, FF).astype(F32)

    everyone = jnp.concatenate(tokens, axis=0)
    offsets = jnp.concatenate(
        [
            lax.dynamic_slice_in_dim(query_full, x_at * HW, HW),
            jnp.zeros((HW,), F32),
            lax.dynamic_slice_in_dim(value_full, x_at * HW, HW),
        ]
    )
    qkv = (dot(everyone, qkv_full) + offsets).astype(BF16)
    context = attend(info, qkv)

    groups = [context[:LOCAL]] + [None] * 3
    for step in ORDER:
        groups[SP - step] = to_x(context[step * LOCAL : (step + 1) * LOCAL], step)
    context_tok = jnp.stack(groups)

    hidden_out, grad_one, context_grad, row_sums, bias_sums, packed_grads = middle(
        info, context_tok, own, out_grad[0], rows, expand_add, packed
    )
    packed_grads = lax.psum_scatter(
        packed_grads,
        "fsdp",
        scatter_dimension=0,
        axis_index_groups=[[8 * z + m for m in range(8)] for z in range(4)],
        tiled=True,
    )
    z_at = lax.axis_index("fsdp") // 8

    def rows_of(step):
        return lax.dynamic_slice_in_dim(packed_grads, (z_at + step) % 4 * 24, 24, axis=0)

    z_sum = rows_of(0).astype(F32)
    for step in ORDER:
        z_sum = z_sum + to_z(rows_of(step), step).astype(F32)
    packed_grads = z_sum.astype(BF16)
    blocks = [context_grad[0]] + [None] * 3
    for step in ORDER:
        blocks[SP - step] = to_x(context_grad[step], step)
    grad_heads = jnp.concatenate(blocks, axis=0)

    qkv_grad = attend_back(info, qkv, grad_heads)

    partial = by_transpose(qkv_grad, qkv_full).astype(BF16)
    input_sum = grad_one + partial[:LOCAL].astype(F32)
    for step in ORDER:
        input_sum = input_sum + to_x(partial[step * LOCAL : (step + 1) * LOCAL], step).astype(F32)
    input_grad = input_sum.astype(BF16)[None]

    qkv_weight_grad = rows_first(everyone, qkv_grad)
    sums = column_sum(qkv_grad)
    two = jnp.zeros((2, D), F32)
    two = lax.dynamic_update_slice(two, jnp.stack([sums[:HW], sums[2 * HW :]]), (0, x_at * HW))
    late = jnp.concatenate([two, row_sums[:6], bias_sums], axis=0).T
    second_round = jnp.concatenate([qkv_weight_grad, late], axis=1)
    second_round = lax.all_to_all(
        second_round.astype(BF16).reshape(32, 24, 3 * HW + 12),
        "fsdp",
        split_axis=0,
        concat_axis=0,
        tiled=True,
    )
    second_round = jnp.sum(second_round.astype(F32), axis=0).astype(BF16)
    second_round = from_x(second_round, x_at).astype(F32)
    qkv_out = jnp.transpose(second_round[:, :, : 3 * HW].reshape(SP, 24, 3, HW), (1, 2, 0, 3))
    qkv_out = qkv_out.reshape(24, 3 * D)
    vector_out = jnp.sum(second_round[:, :, 3 * HW :], axis=0)
    eight = vector_out.T
    expand_bias_out = eight[8:].reshape(96)

    reduce_out, expand_out, context_out = finish(
        [packed_grads] + [to_x(packed_grads, step) for step in ORDER]
    )

    return (
        hidden_out[None],
        input_grad,
        qkv_out,
        eight[0],
        eight[1],
        context_out,
        eight[2],
        eight[3],
        eight[4],
        expand_out,
        expand_bias_out,
        reduce_out,
        eight[5],
        eight[6],
        eight[7],
    )


def solution(mesh):
    sequences = P("fsdp", "sp", None)
    matrix = P("fsdp", None)
    vector = P("fsdp")
    return jax.shard_map(
        per_device,
        mesh=mesh,
        in_specs=(
            sequences, vector, matrix, vector, vector, matrix, vector, vector, vector,
            matrix, vector, matrix, vector, vector, vector, sequences,
        ),
        out_specs=(
            sequences, sequences, matrix, vector, vector, matrix, vector, vector, vector,
            matrix, vector, matrix, vector, vector, vector,
        ),
        check_vma=False,
    )
```

time: 257 us -> 223 us (0.87)
  local copies, waits for them, and re-layouts: 39.7 us -> 9.24 us
  Pallas kernels: 30.7 us -> 49.5 us
  waiting for transfers between devices: 104 us -> 91.1 us
  matrix products: 19.9 us -> 7.24 us
  starting transfers between devices: 34 us -> 44 us
  other arithmetic: 12 us -> 5.91 us
    reduce_scatter x1, waiting for transfers between devices: 21.5 us -> 0.02 us  [per_device(): lax.psum_scatter(packed_grads, 'fsdp', scatter_dimension=0, axis_index_gr...]
    pallas_call x2 -> x3, Pallas kernels: 6.32 us -> 25.7 us  [the longest x1 16.1 us: middle(): pl.pallas_call(middle_kernel, out_shape=(jax.ShapeDtypeStruct(tall, BF16)...]
    slice x8 -> x6, local copies, waits for them, and re-layouts: 13.1 us -> 0.42 us  [the longest x3 0.26 us: per_device(): query_full, value_full = (rows[0], rows[1])]
    ppermute x0 -> x3, waiting for transfers between devices: none -> 12.4 us  [to_z(): lax.ppermute(values, 'fsdp', [(i, (i + 8 * step) % 32) for i in range(32)])]
    unnamed x63 -> x31, local copies, waits for them, and re-layouts: 11.7 us -> 2.24 us
    dot_general x4 -> x1, matrix products: 9.21 us -> 1.39 us  [dot(): return jnp.dot(left_side, right_side, preferred_element_type=F32)]
    dot_general x4 -> x1, matrix products: 9.58 us -> 2.63 us  [by_transpose(): lax.dot_general(left_side, right_side, (((1,), (1,)), ((), ())), preferre...]
    pad x9 -> x0, local copies, waits for them, and re-layouts: 5.97 us -> none  [the longest x6 3.99 us: per_device(): jnp.pad(part, (0, D - 24))[None]]
  transfers between devices with their start and end apart: 22 -> 25, of which waited for: 15 -> 16; matrix products, arithmetic and copies ran while one was open for 8% -> 8% of each run, Pallas kernels for 10% -> 11%
where the time goes in v1:
time: 223 us; the launch traced here: 222 us
  waiting for transfers between devices  91.1 us (41%)
  Pallas kernels  49.5 us (22%)
  starting transfers between devices  44 us (20%)
  between operations  15.1 us (7%)
  local copies, waits for them, and re-layouts  9.24 us (4%)
  matrix products  7.24 us (3%)
  other arithmetic  5.91 us (3%)
    ppermute x18, waiting for transfers between devices, to_x(): return lax.ppermute(values, 'sp', [(i, (i + step) % SP) for i in range(SP)])  43.5 us
    ppermute x18, starting transfers between devices, to_x(): return lax.ppermute(values, 'sp', [(i, (i + step) % SP) for i in range(SP)])  24.5 us
    all_to_all x1, waiting for transfers between devices, per_device(): lax.all_to_all(early, 'fsdp', split_axis=0, concat_axis=0, tiled=True)  20.6 us
    pallas_call x1, Pallas kernels, attend_back(): pl.pallas_call(attend_back_kernel, out_shape=jax.ShapeDtypeStruct((LEN, 3...  16.5 us
    pallas_call x1, Pallas kernels, middle(): pl.pallas_call(middle_kernel, out_shape=(jax.ShapeDtypeStruct(tall, BF16)...  16.1 us
    all_gather x1, waiting for transfers between devices, per_device(): packed = lax.all_gather(packed, 'fsdp', axis=0, tiled=True)  14.6 us
    ppermute x3, waiting for transfers between devices, to_z(): lax.ppermute(values, 'fsdp', [(i, (i + 8 * step) % 32) for i in range(32)])  12.4 us
    all_to_all x1, starting transfers between devices, per_device(): lax.all_to_all(early, 'fsdp', split_axis=0, concat_axis=0, tiled=True)  8.48 us
  transfers between devices with their start and end apart: 25, of which 16 were waited for; matrix products, arithmetic and copies ran while one was open for 8% of the time, Pallas kernels for 11%

profile of v1, /device:TPU:6, one launch (start us, length us, event | category | flops | bytes accessed | tf_op | source)
XLA Modules:
  0.0 222.1 jit_solution(158478292873087965)
XLA Ops:
  7.9 0.6 pad_add_fusion.info_ref
  8.5 4.7 %pack.1 = (bf16[24,6912]{1,0:T(8,128)(2,1)}, bf16[32,32,576]{2,1,0:T(8,128)(2,1)}) custom-call(s32[2]{0:T(128)} %pad_add_fusion.info_ref, bf16[24,2304]{1,0:T(8,128)(2,1)} %rest_0_.1, bf16[24,768]{1,0:T(8,128)(2,1)} %rest_1_.1, bf16[24,3072]{1,0:T(8,128)(2,1)} %rest_2_.1, bf16[96,768]{1,0:T(8,128)(2,1)} %rest_3_.1, ...), custom_call_target="tpu_custom_call" | custom-call | tf_op jit(solution)/shard_map/pack/pallas_call | solution.py:331
  13.2 8.5 %all-to-all-start = ((bf16[32,32,576]{2,1,0:T(8,128)(2,1)}), bf16[32,32,576]{2,1,0:T(8,128)(2,1)S(1)}, u32[]{:S(2)}, u32[]{:S(2)}) async-start(bf16[32,32,576]{2,1,0:T(8,128)(2,1)} %get-tuple-element.26), calls=%async_computation | async-start | bytes 2621440 | tf_op jit(solution)/shard_map/all_to_all | solution.py:446
  21.8 0.9 collective-permute-start
  22.7 1.1 collective-permute-start.1
  23.8 2.1 collective-permute-start.2
  25.9 20.6 %all-to-all-done = bf16[32,32,576]{2,1,0:T(8,128)(2,1)S(1)} async-done(((bf16[32,32,576]{2,1,0:T(8,128)(2,1)}), bf16[32,32,576]{2,1,0:T(8,128)(2,1)S(1)}, u32[]{:S(2)}, u32[]{:S(2)}) %all-to-all-start) | async-done | bytes 1179680 | tf_op jit(solution)/shard_map/all_to_all | solution.py:446
  47.1 0.8 copy-done.7
  47.9 1.4 add_convert_fusion.qkv_ref
  49.3 7.3 %attend.1 = bf16[1024,192]{1,0:T(8,128)(2,1)S(1)} custom-call(s32[2]{0:T(128)S(1)} %copy-done.1, bf16[1024,576]{1,0:T(8,128)(2,1)S(1)} %add_convert_fusion.qkv_ref), custom_call_target="tpu_custom_call" | custom-call | flops 3221225472 | bytes 1572864 | tf_op jit(solution)/shard_map/attend/pallas_call | solution.py:298
  56.7 0.9 collective-permute-start.3
  57.6 1.1 collective-permute-start.4
  58.7 2.1 collective-permute-start.5
  61.2 5.0 %collective-permute-done.3 = bf16[256,192]{1,0:T(8,128)(2,1)S(1)} collective-permute-done((bf16[256,192]{1,0:T(8,128)(2,1)S(1)}, bf16[256,192]{1,0:T(8,128)(2,1)S(1)}, u32[]{:S(2)}, u32[]{:S(2)}) %collective-permute-start.3) | collective-permute-done | bytes 98336 | tf_op jit(solution)/shard_map/ppermute | solution.py:77
  66.2 0.6 collective-permute-done.5
  66.8 0.1 pad_maximum_fusion.2.context_ref
  66.9 14.6 %all-gather.2.cloned.1.call-done.weights_ref = bf16[768,6912]{1,0:T(8,128)(2,1)} async-done(((bf16[24,6912]{1,0:T(8,128)(2,1)}), bf16[768,6912]{1,0:T(8,128)(2,1)}) %all-gather.2.cloned.1.call-update) | async-done | bytes 10616848 | tf_op jit(solution)/shard_map/all_gather | solution.py:445
  81.5 16.1 %middle.1 = (bf16[256,768]{1,0:T(8,128)(2,1)}, f32[256,768]{1,0:T(8,128)S(1)}, bf16[4,256,192]{2,1,0:T(8,128)(2,1)S(1)}, f32[8,768]{1,0:T(8,128)S(1)}, f32[4,768]{1,0:T(4,128)S(1)}, /*index=5*/bf16[768,6912]{1,0:T(8,128)(2,1)}) custom-call(s32[2]{0:T(128)S(1)} %copy-done.1, bf16[4,256,192]{2,1,0:T(8,128)(2,1)S(1)} %pad_maximum_fusion.2.context_ref, ...), custom_call_target="tpu_custom_call" | custom-call | flops 8153726976 | bytes 25165824 | tf_op jit(solution)/shard_map/middle/pallas_call | solution.py:382
  97.8 1.1 collective-permute-start.6
  98.9 1.2 collective-permute-start.7
  100.1 2.1 collective-permute-start.8
  102.1 5.6 %collective-permute-done.6 = bf16[256,192]{1,0:T(8,128)(2,1)S(1)} collective-permute-done((bf16[256,192]{1,0:T(8,128)(2,1)S(1)}, bf16[256,192]{1,0:T(8,128)(2,1)S(1)}, u32[]{:S(2)}, u32[]{:S(2)}) %collective-permute-start.6) | collective-permute-done | bytes 98336 | tf_op jit(solution)/shard_map/ppermute | solution.py:77
  107.7 0.6 collective-permute-done.8
  108.4 16.5 %attend_back.1 = bf16[1024,576]{1,0:T(8,128)(2,1)S(1)} custom-call(s32[2]{0:T(128)S(1)} %copy-done.1, bf16[1024,576]{1,0:T(8,128)(2,1)S(1)} %copy-done.5, bf16[1024,192]{1,0:T(8,128)(2,1)S(1)} %pad_maximum_fusion.3.grad_ref), custom_call_target="tpu_custom_call" | custom-call | flops 8053063680 | bytes 2752512 | tf_op jit(solution)/shard_map/attend_back/pallas_call | solution.py:312
  124.9 0.3 convert_reduce_fusion
  125.2 0.3 dynamic_update_slice.3
  125.5 0.2 copy.62
  125.7 0.2 copy-done.9
  125.9 3.2 %convolution_convert_fusion.1 = bf16[768,576]{0,1:T(8,128)(2,1)} fusion(bf16[1024,576]{1,0:T(8,128)(2,1)S(1)} %attend_back.1, bf16[256,768]{1,0:T(8,128)(2,1)} %copy-done.11, bf16[256,768]{1,0:T(8,128)(2,1)} %copy-done.10, bf16[256,768]{1,0:T(8,128)(2,1)S(1)} %copy-done.9, bf16[256,768]{1,0:T(8,128)(2,1)S(1)} %bitcast.56), kind=kOutput, calls=%fused_computation.4 | convolution fusion | flops 912703488 | bytes 3637248 | tf_op jit(solution)/shard_map/dot_general | solution.py:49
  129.1 1.5 copy.57
  130.7 1.1 pad_maximum_fusion.1
  131.8 5.5 %all-to-all-start.1 = ((bf16[32,24,588]{2,1,0:T(8,128)(2,1)}), bf16[32,24,588]{2,1,0:T(8,128)(2,1)S(1)}, u32[]{:S(2)}, u32[]{:S(2)}) async-start(bf16[32,24,588]{2,1,0:T(8,128)(2,1)} %pad_maximum_fusion.1), calls=%async_computation.1 | async-start | bytes 1966080 | tf_op jit(solution)/shard_map/all_to_all | solution.py:507
  137.2 2.6 %convolution_convert_fusion = bf16[1024,768]{1,0:T(8,128)(2,1)S(1)} fusion(bf16[1024,576]{1,0:T(8,128)(2,1)S(1)} %attend_back.1, bf16[768,576]{1,0:T(8,128)(2,1)} %bitcast.63), kind=kOutput, calls=%fused_computation.2 | convolution fusion | flops 906756096 | bytes 3637248 | tf_op jit(solution)/shard_map/dot_general | solution.py:55
  139.9 1.1 copy-done.6
  141.1 0.9 collective-permute-start.10
  142.0 3.3 %collective-permute-start.11 = (bf16[256,768]{1,0:T(8,128)(2,1)S(1)}, bf16[256,768]{1,0:T(8,128)(2,1)}, u32[]{:S(2)}, u32[]{:S(2)}) collective-permute-start(bf16[256,768]{1,0:T(8,128)(2,1)S(1)} %get-tuple-element.48), channel_id=1, source_target_pairs={{0,2},{1,3},{2,0},{3,1},{4,6},{5,7},{6,4},{7,5},{8,10},{9,11},{10,... | collective-permute-start | bytes 1179656 | tf_op jit(solution)/shard_map/ppermute | solution.py:77
  145.3 8.4 %collective-permute-done.10 = bf16[256,768]{1,0:T(8,128)(2,1)S(1)} collective-permute-done((bf16[256,768]{1,0:T(8,128)(2,1)S(1)}, bf16[256,768]{1,0:T(8,128)(2,1)S(1)}, u32[]{:S(2)}, u32[]{:S(2)}) %collective-permute-start.10) | collective-permute-done | bytes 393248 | tf_op jit(solution)/shard_map/ppermute | solution.py:77
  153.7 9.4 %collective-permute-done.11 = bf16[256,768]{1,0:T(8,128)(2,1)} collective-permute-done((bf16[256,768]{1,0:T(8,128)(2,1)S(1)}, bf16[256,768]{1,0:T(8,128)(2,1)}, u32[]{:S(2)}, u32[]{:S(2)}) %collective-permute-start.11) | collective-permute-done | bytes 393248 | tf_op jit(solution)/shard_map/ppermute | solution.py:77
  163.1 2.2 fusion
  165.3 0.2 reduce_sum.31
  165.5 0.6 collective-permute-start.12
  166.1 3.4 %collective-permute-start.13 = (bf16[24,588]{1,0:T(8,128)(2,1)S(1)}, bf16[24,588]{1,0:T(8,128)(2,1)S(1)}, u32[]{:S(2)}, u32[]{:S(2)}) collective-permute-start(bf16[24,588]{1,0:T(8,128)(2,1)S(1)} %reduce_sum.31), channel_id=1, source_target_pairs={{0,2},{1,3},{2,0},{3,1},{4,6},{5,7},{6,4},{7,5},{8,10},{9,11},{10,... | collective-permute-start | bytes 84680 | tf_op jit(solution)/shard_map/ppermute | solution.py:77
  169.4 1.5 collective-permute-done.12
  171.0 0.7 collective-permute-done.13
  171.6 1.7 collective-permute-done.14
  173.4 1.3 constant_dynamic-slice_fusion.2
  174.6 2.0 collective-permute-start.15
  176.6 1.6 collective-permute-start.16
  178.2 2.0 collective-permute-start.17
  180.2 5.6 %collective-permute-done.15 = bf16[24,6912]{1,0:T(8,128)(2,1)S(1)} collective-permute-done((bf16[24,6912]{1,0:T(8,128)(2,1)S(1)}, bf16[24,6912]{1,0:T(8,128)(2,1)S(1)}, u32[]{:S(2)}, u32[]{:S(2)}) %collective-permute-start.15) | collective-permute-done | bytes 331808 | tf_op jit(solution)/shard_map/ppermute | solution.py:81
  185.8 1.6 collective-permute-done.16
  187.4 5.2 %collective-permute-done.17 = bf16[24,6912]{1,0:T(8,128)(2,1)S(1)} collective-permute-done((bf16[24,6912]{1,0:T(8,128)(2,1)S(1)}, bf16[24,6912]{1,0:T(8,128)(2,1)S(1)}, u32[]{:S(2)}, u32[]{:S(2)}) %collective-permute-start.17) | collective-permute-done | bytes 331808 | tf_op jit(solution)/shard_map/ppermute | solution.py:81
  192.5 1.1 add_convert_fusion.2.a_ref
  193.7 1.4 collective-permute-start.18
  195.1 0.7 collective-permute-start.19
  195.8 1.7 collective-permute-start.20
  197.5 0.2 reshape.72
  197.7 0.2 copy.59
  197.9 0.9 reshape.73
  199.0 0.6 reshape.74
  199.6 0.8 slice_reduce_fusion.3
  200.4 4.1 %collective-permute-done.18.b_ref = bf16[24,6912]{1,0:T(8,128)(2,1)S(1)} collective-permute-done((bf16[24,6912]{1,0:T(8,128)(2,1)S(1)}, bf16[24,6912]{1,0:T(8,128)(2,1)S(1)}, u32[]{:S(2)}, u32[]{:S(2)}) %collective-permute-start.18) | collective-permute-done | bytes 331808 | tf_op jit(solution)/shard_map/ppermute | solution.py:77
  204.5 5.9 %collective-permute-done.19.c_ref = bf16[24,6912]{1,0:T(8,128)(2,1)S(1)} collective-permute-done((bf16[24,6912]{1,0:T(8,128)(2,1)S(1)}, bf16[24,6912]{1,0:T(8,128)(2,1)S(1)}, u32[]{:S(2)}, u32[]{:S(2)}) %collective-permute-start.19) | collective-permute-done | bytes 331808 | tf_op jit(solution)/shard_map/ppermute | solution.py:77
  210.4 4.9 %finish.1 = (f32[96,768]{1,0:T(8,128)}, f32[24,3072]{1,0:T(8,128)}, f32[24,768]{1,0:T(8,128)}) custom-call(bf16[24,6912]{1,0:T(8,128)(2,1)S(1)} %add_convert_fusion.2.a_ref, bf16[24,6912]{1,0:T(8,128)(2,1)S(1)} %collective-permute-done.18.b_ref, bf16[24,6912]{1,0:T(8,128)(2,1)S(1)} %collective-permute-done.19.c_ref, ...), custom_call_target="tpu_custom_call" | custom-call | tf_op jit(solution)/shard_map/finish/pallas_call | solution.py:366
  (72 shorter events, 1.7 us)
Async XLA Ops:
  7.2 74.4 %all-gather.2.cloned.1.call-start = ((), (), s32[]{:S(2)}) async-start(), calls=%async_computation.3 | async-start | bytes 10948608 | tf_op jit(solution)/shard_map/all_gather | solution.py:445
  13.2 8.6 %copy-start.3 = (bf16[1,256,768]{2,1,0:T(8,128)(2,1)S(1)}, bf16[1,256,768]{2,1,0:T(8,128)(2,1)}, u32[]{:S(2)}) copy-start(bf16[1,256,768]{2,1,0:T(8,128)(2,1)} %param.18) | copy-start | bytes 1179652
  13.2 33.2 %all-to-all-start = ((bf16[32,32,576]{2,1,0:T(8,128)(2,1)}), bf16[32,32,576]{2,1,0:T(8,128)(2,1)S(1)}, u32[]{:S(2)}, u32[]{:S(2)}) async-start(bf16[32,32,576]{2,1,0:T(8,128)(2,1)} %get-tuple-element.26), calls=%async_computation | async-start | bytes 2621440 | tf_op jit(solution)/shard_map/all_to_all | solution.py:446
  21.7 151.6 %reduce-scatter.2.cloned.1.call-start = ((), (), s32[]{:S(2)}) async-start(), calls=%async_computation.4 | async-start | bytes 11943936 | tf_op jit(solution)/shard_map/reduce_scatter | solution.py:472
  21.8 25.3 %collective-permute-start = (bf16[256,768]{1,0:T(8,128)(2,1)S(1)}, bf16[256,768]{1,0:T(8,128)(2,1)S(1)}, u32[]{:S(2)}, u32[]{:S(2)}) collective-permute-start(bf16[256,768]{1,0:T(8,128)(2,1)S(1)} %bitcast.51), channel_id=1, source_target_pairs={{0,3},{1,0},{2,1},{3,2},{4,7},{5,4},{6,5},{7,6},{8,11},{9,8},{10,9... | collective-permute-start | bytes 1179656 | tf_op jit(solution)/shard_map/ppermute | solution.py:77
  22.7 24.4 %collective-permute-start.1 = (bf16[256,768]{1,0:T(8,128)(2,1)S(1)}, bf16[256,768]{1,0:T(8,128)(2,1)S(1)}, u32[]{:S(2)}, u32[]{:S(2)}) collective-permute-start(bf16[256,768]{1,0:T(8,128)(2,1)S(1)} %bitcast.52), channel_id=1, source_target_pairs={{0,2},{1,3},{2,0},{3,1},{4,6},{5,7},{6,4},{7,5},{8,10},{9,11},{10,... | collective-permute-start | bytes 1179656 | tf_op jit(solution)/shard_map/ppermute | solution.py:77
  23.8 23.3 %collective-permute-start.2 = (bf16[256,768]{1,0:T(8,128)(2,1)S(1)}, bf16[256,768]{1,0:T(8,128)(2,1)S(1)}, u32[]{:S(2)}, u32[]{:S(2)}) collective-permute-start(bf16[256,768]{1,0:T(8,128)(2,1)S(1)} %bitcast.53), channel_id=1, source_target_pairs={{0,1},{1,2},{2,3},{3,0},{4,5},{5,6},{6,7},{7,4},{8,9},{9,10},{10,1... | collective-permute-start | bytes 1179656 | tf_op jit(solution)/shard_map/ppermute | solution.py:77
  46.9 1.0 copy-start.7
  47.1 2.2 copy-start.8
  47.1 2.2 copy-start.10
  47.1 2.2 copy-start.11
  47.9 1.4 copy-start.1
  49.3 7.3 %copy-start.4 = (bf16[1024,576]{1,0:T(8,128)(2,1)}, bf16[1024,576]{1,0:T(8,128)(2,1)S(1)}, u32[]{:S(2)}) copy-start(bf16[1024,576]{1,0:T(8,128)(2,1)S(1)} %add_convert_fusion.qkv_ref) | copy-start | bytes 3538948
  56.6 24.9 %copy-start.2 = (bf16[1,256,768]{2,1,0:T(8,128)(2,1)S(1)}, bf16[1,256,768]{2,1,0:T(8,128)(2,1)}, u32[]{:S(2)}) copy-start(bf16[1,256,768]{2,1,0:T(8,128)(2,1)} %param.33) | copy-start | bytes 1179652
  56.7 9.5 %collective-permute-start.3 = (bf16[256,192]{1,0:T(8,128)(2,1)S(1)}, bf16[256,192]{1,0:T(8,128)(2,1)S(1)}, u32[]{:S(2)}, u32[]{:S(2)}) collective-permute-start(bf16[256,192]{1,0:T(8,128)(2,1)S(1)} %get-tuple-element.60), channel_id=1, source_target_pairs={{0,3},{1,0},{2,1},{3,2},{4,7},{5,4},{6,5},{7,6},{8,11},{9,8},{10,9... | collective-permute-start | bytes 294920 | tf_op jit(solution)/shard_map/ppermute | solution.py:77
  57.6 8.6 %collective-permute-start.4 = (bf16[256,192]{1,0:T(8,128)(2,1)S(1)}, bf16[256,192]{1,0:T(8,128)(2,1)S(1)}, u32[]{:S(2)}, u32[]{:S(2)}) collective-permute-start(bf16[256,192]{1,0:T(8,128)(2,1)S(1)} %get-tuple-element.59), channel_id=1, source_target_pairs={{0,2},{1,3},{2,0},{3,1},{4,6},{5,7},{6,4},{7,5},{8,10},{9,11},{10,... | collective-permute-start | bytes 294920 | tf_op jit(solution)/shard_map/ppermute | solution.py:77
  58.7 8.1 %collective-permute-start.5 = (bf16[256,192]{1,0:T(8,128)(2,1)S(1)}, bf16[256,192]{1,0:T(8,128)(2,1)S(1)}, u32[]{:S(2)}, u32[]{:S(2)}) collective-permute-start(bf16[256,192]{1,0:T(8,128)(2,1)S(1)} %get-tuple-element.58), channel_id=1, source_target_pairs={{0,1},{1,2},{2,3},{3,0},{4,5},{5,6},{6,7},{7,4},{8,9},{9,10},{10,1... | collective-permute-start | bytes 294920 | tf_op jit(solution)/shard_map/ppermute | solution.py:77
  97.7 10.7 %copy-start.5 = (bf16[1024,576]{1,0:T(8,128)(2,1)S(1)}, bf16[1024,576]{1,0:T(8,128)(2,1)}, u32[]{:S(2)}) copy-start(bf16[1024,576]{1,0:T(8,128)(2,1)} %copy-done.4) | copy-start | bytes 3538948
  97.8 10.0 %collective-permute-start.6 = (bf16[256,192]{1,0:T(8,128)(2,1)S(1)}, bf16[256,192]{1,0:T(8,128)(2,1)S(1)}, u32[]{:S(2)}, u32[]{:S(2)}) collective-permute-start(bf16[256,192]{1,0:T(8,128)(2,1)S(1)} %get-tuple-element.56), channel_id=1, source_target_pairs={{0,3},{1,0},{2,1},{3,2},{4,7},{5,4},{6,5},{7,6},{8,11},{9,8},{10,9... | collective-permute-start | bytes 294920 | tf_op jit(solution)/shard_map/ppermute | solution.py:77
  98.9 8.8 %collective-permute-start.7 = (bf16[256,192]{1,0:T(8,128)(2,1)S(1)}, bf16[256,192]{1,0:T(8,128)(2,1)S(1)}, u32[]{:S(2)}, u32[]{:S(2)}) collective-permute-start(bf16[256,192]{1,0:T(8,128)(2,1)S(1)} %get-tuple-element.55), channel_id=1, source_target_pairs={{0,2},{1,3},{2,0},{3,1},{4,6},{5,7},{6,4},{7,5},{8,10},{9,11},{10,... | collective-permute-start | bytes 294920 | tf_op jit(solution)/shard_map/ppermute | solution.py:77
  100.1 8.3 %collective-permute-start.8 = (bf16[256,192]{1,0:T(8,128)(2,1)S(1)}, bf16[256,192]{1,0:T(8,128)(2,1)S(1)}, u32[]{:S(2)}, u32[]{:S(2)}) collective-permute-start(bf16[256,192]{1,0:T(8,128)(2,1)S(1)} %get-tuple-element.54), channel_id=1, source_target_pairs={{0,1},{1,2},{2,3},{3,0},{4,5},{5,6},{6,7},{7,4},{8,9},{9,10},{10,1... | collective-permute-start | bytes 294920 | tf_op jit(solution)/shard_map/ppermute | solution.py:77
  124.9 1.0 copy-start.9
  131.8 33.6 %all-to-all-start.1 = ((bf16[32,24,588]{2,1,0:T(8,128)(2,1)}), bf16[32,24,588]{2,1,0:T(8,128)(2,1)S(1)}, u32[]{:S(2)}, u32[]{:S(2)}) async-start(bf16[32,24,588]{2,1,0:T(8,128)(2,1)} %pad_maximum_fusion.1), calls=%async_computation.1 | async-start | bytes 1966080 | tf_op jit(solution)/shard_map/all_to_all | solution.py:507
  139.9 1.1 copy-start.6
  141.1 12.6 %collective-permute-start.10 = (bf16[256,768]{1,0:T(8,128)(2,1)S(1)}, bf16[256,768]{1,0:T(8,128)(2,1)S(1)}, u32[]{:S(2)}, u32[]{:S(2)}) collective-permute-start(bf16[256,768]{1,0:T(8,128)(2,1)S(1)} %get-tuple-element.49), channel_id=1, source_target_pairs={{0,3},{1,0},{2,1},{3,2},{4,7},{5,4},{6,5},{7,6},{8,11},{9,8},{10,9... | collective-permute-start | bytes 1179656 | tf_op jit(solution)/shard_map/ppermute | solution.py:77
  142.0 21.1 %collective-permute-start.11 = (bf16[256,768]{1,0:T(8,128)(2,1)S(1)}, bf16[256,768]{1,0:T(8,128)(2,1)}, u32[]{:S(2)}, u32[]{:S(2)}) collective-permute-start(bf16[256,768]{1,0:T(8,128)(2,1)S(1)} %get-tuple-element.48), channel_id=1, source_target_pairs={{0,2},{1,3},{2,0},{3,1},{4,6},{5,7},{6,4},{7,5},{8,10},{9,11},{10,... | collective-permute-start | bytes 1179656 | tf_op jit(solution)/shard_map/ppermute | solution.py:77
  145.3 17.8 %collective-permute-start.9 = (bf16[256,768]{1,0:T(8,128)(2,1)S(1)}, bf16[256,768]{1,0:T(8,128)(2,1)}, u32[]{:S(2)}, u32[]{:S(2)}) collective-permute-start(bf16[256,768]{1,0:T(8,128)(2,1)S(1)} %get-tuple-element.47), channel_id=1, source_target_pairs={{0,1},{1,2},{2,3},{3,0},{4,5},{5,6},{6,7},{7,4},{8,9},{9,10},{10,1... | collective-permute-start | bytes 1179656 | tf_op jit(solution)/shard_map/ppermute | solution.py:77
  165.5 5.5 %collective-permute-start.12 = (bf16[24,588]{1,0:T(8,128)(2,1)S(1)}, bf16[24,588]{1,0:T(8,128)(2,1)S(1)}, u32[]{:S(2)}, u32[]{:S(2)}) collective-permute-start(bf16[24,588]{1,0:T(8,128)(2,1)S(1)} %reduce_sum.31), channel_id=1, source_target_pairs={{0,3},{1,0},{2,1},{3,2},{4,7},{5,4},{6,5},{7,6},{8,11},{9,8},{10,9... | collective-permute-start | bytes 84680 | tf_op jit(solution)/shard_map/ppermute | solution.py:77
  166.1 5.6 %collective-permute-start.13 = (bf16[24,588]{1,0:T(8,128)(2,1)S(1)}, bf16[24,588]{1,0:T(8,128)(2,1)S(1)}, u32[]{:S(2)}, u32[]{:S(2)}) collective-permute-start(bf16[24,588]{1,0:T(8,128)(2,1)S(1)} %reduce_sum.31), channel_id=1, source_target_pairs={{0,2},{1,3},{2,0},{3,1},{4,6},{5,7},{6,4},{7,5},{8,10},{9,11},{10,... | collective-permute-start | bytes 84680 | tf_op jit(solution)/shard_map/ppermute | solution.py:77
  169.4 3.9 %collective-permute-start.14 = (bf16[24,588]{1,0:T(8,128)(2,1)S(1)}, bf16[24,588]{1,0:T(8,128)(2,1)S(1)}, u32[]{:S(2)}, u32[]{:S(2)}) collective-permute-start(bf16[24,588]{1,0:T(8,128)(2,1)S(1)} %reduce_sum.31), channel_id=1, source_target_pairs={{0,1},{1,2},{2,3},{3,0},{4,5},{5,6},{6,7},{7,4},{8,9},{9,10},{10,1... | collective-permute-start | bytes 84680 | tf_op jit(solution)/shard_map/ppermute | solution.py:77
  174.6 11.1 %collective-permute-start.15 = (bf16[24,6912]{1,0:T(8,128)(2,1)S(1)}, bf16[24,6912]{1,0:T(8,128)(2,1)S(1)}, u32[]{:S(2)}, u32[]{:S(2)}) collective-permute-start(bf16[24,6912]{1,0:T(8,128)(2,1)S(1)} %get-tuple-element.50), channel_id=1, source_target_pairs={{0,32},{4,36},{8,40},{12,44},{16,48},{20,52},{24,56},{28,60},{32,6... | collective-permute-start | bytes 995336 | tf_op jit(solution)/shard_map/ppermute | solution.py:81
  176.6 10.7 %collective-permute-start.16 = (bf16[24,6912]{1,0:T(8,128)(2,1)S(1)}, bf16[24,6912]{1,0:T(8,128)(2,1)S(1)}, u32[]{:S(2)}, u32[]{:S(2)}) collective-permute-start(bf16[24,6912]{1,0:T(8,128)(2,1)S(1)} %get-tuple-element.52), channel_id=1, source_target_pairs={{0,96},{4,100},{8,104},{12,108},{16,112},{20,116},{24,120},{28,124... | collective-permute-start | bytes 995336 | tf_op jit(solution)/shard_map/ppermute | solution.py:81
  178.2 14.3 %collective-permute-start.17 = (bf16[24,6912]{1,0:T(8,128)(2,1)S(1)}, bf16[24,6912]{1,0:T(8,128)(2,1)S(1)}, u32[]{:S(2)}, u32[]{:S(2)}) collective-permute-start(bf16[24,6912]{1,0:T(8,128)(2,1)S(1)} %get-tuple-element.51), channel_id=1, source_target_pairs={{0,64},{4,68},{8,72},{12,76},{16,80},{20,84},{24,88},{28,92},{32,9... | collective-permute-start | bytes 995336 | tf_op jit(solution)/shard_map/ppermute | solution.py:81
  193.7 16.7 %copy-start = (bf16[768,768]{1,0:T(8,128)(2,1)S(1)}, bf16[768,768]{1,0:T(8,128)(2,1)}, u32[]{:S(2)}) copy-start(bf16[768,768]{1,0:T(8,128)(2,1)} %constant.76.clone.rest_4_.order_ref) | copy-start | bytes 3538948
  193.7 10.8 %collective-permute-start.18 = (bf16[24,6912]{1,0:T(8,128)(2,1)S(1)}, bf16[24,6912]{1,0:T(8,128)(2,1)S(1)}, u32[]{:S(2)}, u32[]{:S(2)}) collective-permute-start(bf16[24,6912]{1,0:T(8,128)(2,1)S(1)} %add_convert_fusion.2.a_ref), channel_id=1, source_target_pairs={{0,1},{1,2},{2,3},{3,0},{4,5},{5,6},{6,7},{7,4},{8,9},{9,10},{10,1... | collective-permute-start | bytes 995336 | tf_op jit(solution)/shard_map/ppermute | solution.py:77
  195.1 15.3 %collective-permute-start.19 = (bf16[24,6912]{1,0:T(8,128)(2,1)S(1)}, bf16[24,6912]{1,0:T(8,128)(2,1)S(1)}, u32[]{:S(2)}, u32[]{:S(2)}) collective-permute-start(bf16[24,6912]{1,0:T(8,128)(2,1)S(1)} %add_convert_fusion.2.a_ref), channel_id=1, source_target_pairs={{0,3},{1,0},{2,1},{3,2},{4,7},{5,4},{6,5},{7,6},{8,11},{9,8},{10,9... | collective-permute-start | bytes 995336 | tf_op jit(solution)/shard_map/ppermute | solution.py:77
  195.8 14.6 %collective-permute-start.20 = (bf16[24,6912]{1,0:T(8,128)(2,1)S(1)}, bf16[24,6912]{1,0:T(8,128)(2,1)S(1)}, u32[]{:S(2)}, u32[]{:S(2)}) collective-permute-start(bf16[24,6912]{1,0:T(8,128)(2,1)S(1)} %add_convert_fusion.2.a_ref), channel_id=1, source_target_pairs={{0,2},{1,3},{2,0},{3,1},{4,6},{5,7},{6,4},{7,5},{8,10},{9,11},{10,... | collective-permute-start | bytes 995336 | tf_op jit(solution)/shard_map/ppermute | solution.py:77
Sparse Core Ops, SparseCore 0:
  13.4 68.1 all-gather.1
  97.8 73.0 reduce-scatter.1

commit v2 on v1

--- a/solution.py
+++ b/solution.py
@@ -67,10 +67,6 @@
     half = 0.5 * (1.0 + bent)
     slope = half + 0.5 * values * (1.0 - bent * bent) * (ROOT * (1.0 + 3.0 * CUBE * square))
     return values * half, slope
-
-
-def column_sum(values):
-    return jnp.sum(values.astype(F32), axis=0)
 
 
 def to_x(values, step):
@@ -116,7 +112,10 @@
         context_ref[rows, :] = jnp.concatenate(outs, axis=1).astype(BF16)
 
 
-def attend_back_kernel(info_ref, qkv_ref, grad_ref, out_ref, key_sum, value_sum):
+def attend_back_kernel(
+    info_ref, qkv_ref, grad_ref, tokens_ref, context_ref, sums_ref, bias_sum_ref,
+    out_ref, late_ref, key_sum, value_sum, stack,
+):
     valid = masked_keys(info_ref, (LEN, 1), 0)
     key_sum[...] = jnp.zeros_like(key_sum)
     value_sum[...] = jnp.zeros_like(value_sum)
@@ -147,8 +146,23 @@
             [total[head] for head in range(HEADS)], axis=1
         ).astype(BF16)
 
+    low = out_ref[...]
+    late_ref[:, D + 128 :] = rows_first(tokens_ref[...], low).astype(BF16)
+    late_ref[:, :D] = context_ref[...]
+    sums = jnp.sum(low.astype(F32), axis=0, keepdims=True)
+    stack[...] = jnp.zeros_like(stack)
+    for row, part in ((0, 0), (1, 2)):
+        own = sums[:, part * HW : (part + 1) * HW]
+        stack[row : row + 1, :] = jnp.concatenate(
+            [jnp.where(info_ref[0] == at, own, 0.0) for at in range(SP)], axis=1
+        )
+    stack[2:8, :] = sums_ref[0:6, :]
+    stack[8:12, :] = bias_sum_ref[...]
+    late_ref[:, D : D + 128] = stack[...].T.astype(BF16)
+
 
 PACKED = 2 * FF + D
+LATE = D + 128 + 3 * HW
 
 
 def reorder_matrix():
@@ -174,7 +188,11 @@
     reduce_rows = reduce_ref[...].astype(F32)
     for part in range(4):
         packed_ref[:, part * D : (part + 1) * D] = reduce_rows[part * 24 : (part + 1) * 24].astype(BF16)
-    moved = [dot(expand_ref[:, q * D : (q + 1) * D], order_ref[...]) for q in range(4)]
+    stacked = jnp.concatenate(
+        [expand_ref[:, q * D : (q + 1) * D].astype(F32) for q in range(4)], axis=0
+    )
+    stacked = dot(stacked.astype(BF16), order_ref[...])
+    moved = [stacked[q * 24 : (q + 1) * 24] for q in range(4)]
     for part in range(4):
         packed_ref[:, FF + part * D : FF + (part + 1) * D] = jnp.concatenate(
             [values[:, part * HW : (part + 1) * HW] for values in moved], axis=1
@@ -202,7 +220,7 @@
 
 def middle_kernel(
     info_ref, context_ref, own_ref, cotangent_ref, rows_ref, bias_ref, weights_ref,
-    hidden_ref, grad_one_ref, context_grad_ref, sums_ref, bias_sum_ref, grads_ref,
+    hidden_ref, grad_one_ref, context_grad_ref, sums_ref, bias_sum_ref, context_sum_ref, grads_ref,
     held, made, slopes, active, in_sems, out_sems,
 ):
     def piece(block):
@@ -277,10 +295,10 @@
     grad_one_ref[...] = grad_one
     branch_grad = grad_one.astype(BF16)
     sums_ref[0:1, :] = jnp.sum(branch_grad.astype(F32), axis=0, keepdims=True)
-    made[:, piece(8)] = by_plane(
-        jnp.concatenate([rows_first(context_ref[group], branch_grad) for group in groups], axis=0)
-    )
-    sent.append(send(8))
+    for block in range(SP):
+        context_sum_ref[block * HW : (block + 1) * HW, :] = rows_first(
+            context_ref[groups[block]], branch_grad
+        ).astype(BF16)
     for block in range(SP):
         context_grad_ref[groups[block]] = by_transpose(
             branch_grad, held[block * HW : (block + 1) * HW, piece(8)]
@@ -308,19 +326,26 @@
     )(info, qkv)
 
 
-def attend_back(info, qkv, grads):
+def attend_back(info, qkv, grads, tokens, context_sum, row_sums, bias_sums):
     return pl.pallas_call(
         attend_back_kernel,
-        out_shape=jax.ShapeDtypeStruct((LEN, 3 * HW), BF16),
-        in_specs=[SMEM, VMEM, VMEM],
-        out_specs=VMEM,
-        scratch_shapes=[pltpu.VMEM((HEADS, LEN, DH), F32), pltpu.VMEM((HEADS, LEN, DH), F32)],
+        out_shape=(
+            jax.ShapeDtypeStruct((LEN, 3 * HW), BF16),
+            jax.ShapeDtypeStruct((D, LATE), BF16),
+        ),
+        in_specs=[SMEM] + [VMEM] * 6,
+        out_specs=(VMEM, VMEM),
+        scratch_shapes=[
+            pltpu.VMEM((HEADS, LEN, DH), F32),
+            pltpu.VMEM((HEADS, LEN, DH), F32),
+            pltpu.VMEM((128, D), F32),
+        ],
         compiler_params=PARAMS,
         cost_estimate=pl.CostEstimate(
             flops=10 * HEADS * LEN * LEN * 256, bytes_accessed=LEN * HW * 14, transcendentals=0
         ),
         name="attend_back",
-    )(info, qkv, grads)
+    )(info, qkv, grads, tokens, context_sum, row_sums, bias_sums)
 
 
 def pack(info, qkv_weight, context_weight, expand_weight, reduce_weight, vectors):
@@ -343,23 +368,50 @@
     )(info, *operands)
 
 
-def finish_kernel(a_ref, b_ref, c_ref, d_ref, order_ref, reduce_ref, expand_ref, context_ref):
+def add_up_kernel(parts_ref, after_ref, out_ref):
+    total = parts_ref[0].astype(F32)
+    for owner in range(1, 32):
+        total = total + parts_ref[owner].astype(F32)
+    out_ref[...] = total.astype(BF16)
+
+
+def add_up(parts, after):
+    return pl.pallas_call(
+        add_up_kernel,
+        out_shape=jax.ShapeDtypeStruct(parts.shape[1:], BF16),
+        in_specs=[VMEM, pl.BlockSpec(memory_space=pl.ANY)],
+        out_specs=VMEM,
+        compiler_params=PARAMS,
+        cost_estimate=pl.CostEstimate(
+            flops=parts.size, bytes_accessed=2 * parts.size, transcendentals=0
+        ),
+        name="add_up",
+    )(parts, after)
+
+
+def finish_kernel(a_ref, b_ref, c_ref, d_ref, order_ref, reduce_ref, expand_ref):
     def total(start, width):
         parts = [ref[:, start : start + width].astype(F32) for ref in (a_ref, b_ref, c_ref, d_ref)]
         return (parts[0] + parts[1]) + (parts[2] + parts[3])
 
     for part in range(4):
         reduce_ref[part * 24 : (part + 1) * 24, :] = total(part * D, D)
-    context_ref[...] = total(2 * FF, D)
     moved = [total(FF + part * D, D) for part in range(4)]
+    left = jnp.concatenate(
+        [
+            jnp.concatenate([values[:, q * HW : (q + 1) * HW] for values in moved], axis=1)
+            for q in range(4)
+        ],
+        axis=0,
+    )
+    terms = []
+    for _ in range(3):
+        terms.append(left.astype(BF16))
+        left = left - terms[-1].astype(F32)
+    result = by_transpose(jnp.concatenate(terms, axis=0), order_ref[...])
+    result = (result[:96] + result[96:192]) + result[192:]
     for q in range(4):
-        left = jnp.concatenate([values[:, q * HW : (q + 1) * HW] for values in moved], axis=1)
-        result = jnp.zeros((24, D), F32)
-        for _ in range(3):
-            term = left.astype(BF16)
-            result = result + by_transpose(term, order_ref[...])
-            left = left - term.astype(F32)
-        expand_ref[:, q * D : (q + 1) * D] = result
+        expand_ref[:, q * D : (q + 1) * D] = result[q * 24 : (q + 1) * 24]
 
 
 def finish(pieces):
@@ -368,10 +420,9 @@
         out_shape=(
             jax.ShapeDtypeStruct((96, D), F32),
             jax.ShapeDtypeStruct((24, FF), F32),
-            jax.ShapeDtypeStruct((24, D), F32),
         ),
         in_specs=[VMEM] * 5,
-        out_specs=(VMEM,) * 3,
+        out_specs=(VMEM,) * 2,
         compiler_params=PARAMS,
         name="finish",
     )(*pieces, jnp.asarray(reorder_matrix(), BF16))
@@ -387,17 +438,18 @@
             jax.ShapeDtypeStruct((SP, LOCAL, HW), BF16),
             jax.ShapeDtypeStruct((8, D), F32),
             jax.ShapeDtypeStruct((4, D), F32),
-            jax.ShapeDtypeStruct((D, PACKED), BF16),
+            jax.ShapeDtypeStruct((D, D), BF16),
+            jax.ShapeDtypeStruct((D, 2 * FF), BF16),
         ),
         in_specs=[SMEM] + [VMEM] * 5 + [pl.BlockSpec(memory_space=pl.ANY)],
-        out_specs=(VMEM,) * 5 + (pl.BlockSpec(memory_space=pl.ANY),),
+        out_specs=(VMEM,) * 6 + (pl.BlockSpec(memory_space=pl.ANY),),
         scratch_shapes=[
             pltpu.VMEM((D, PACKED), BF16),
-            pltpu.VMEM((D, PACKED), BF16),
+            pltpu.VMEM((D, 2 * FF), BF16),
             pltpu.VMEM((LOCAL, FF), F32),
             pltpu.VMEM((LOCAL, FF), BF16),
             pltpu.SemaphoreType.DMA((9,)),
-            pltpu.SemaphoreType.DMA((9,)),
+            pltpu.SemaphoreType.DMA((8,)),
         ],
         compiler_params=pltpu.CompilerParams(vmem_limit_bytes=48 * 1024 * 1024),
         cost_estimate=pl.CostEstimate(
@@ -466,7 +518,7 @@
         groups[SP - step] = to_x(context[step * LOCAL : (step + 1) * LOCAL], step)
     context_tok = jnp.stack(groups)
 
-    hidden_out, grad_one, context_grad, row_sums, bias_sums, packed_grads = middle(
+    hidden_out, grad_one, context_grad, row_sums, bias_sums, context_sum, packed_grads = middle(
         info, context_tok, own, out_grad[0], rows, expand_add, packed
     )
     packed_grads = lax.psum_scatter(
@@ -481,16 +533,19 @@
     def rows_of(step):
         return lax.dynamic_slice_in_dim(packed_grads, (z_at + step) % 4 * 24, 24, axis=0)
 
-    z_sum = rows_of(0).astype(F32)
+    z_rows = [rows_of(step) for step in range(4)]
+    z_sum = z_rows[0].astype(F32)
     for step in ORDER:
-        z_sum = z_sum + to_z(rows_of(step), step).astype(F32)
+        z_sum = z_sum + to_z(z_rows[step], step).astype(F32)
     packed_grads = z_sum.astype(BF16)
     blocks = [context_grad[0]] + [None] * 3
     for step in ORDER:
         blocks[SP - step] = to_x(context_grad[step], step)
     grad_heads = jnp.concatenate(blocks, axis=0)
 
-    qkv_grad = attend_back(info, qkv, grad_heads)
+    qkv_grad, second_round = attend_back(
+        info, qkv, grad_heads, everyone, context_sum, row_sums, bias_sums
+    )
 
     partial = by_transpose(qkv_grad, qkv_full).astype(BF16)
     input_sum = grad_one + partial[:LOCAL].astype(F32)
@@ -498,28 +553,22 @@
         input_sum = input_sum + to_x(partial[step * LOCAL : (step + 1) * LOCAL], step).astype(F32)
     input_grad = input_sum.astype(BF16)[None]
 
-    qkv_weight_grad = rows_first(everyone, qkv_grad)
-    sums = column_sum(qkv_grad)
-    two = jnp.zeros((2, D), F32)
-    two = lax.dynamic_update_slice(two, jnp.stack([sums[:HW], sums[2 * HW :]]), (0, x_at * HW))
-    late = jnp.concatenate([two, row_sums[:6], bias_sums], axis=0).T
-    second_round = jnp.concatenate([qkv_weight_grad, late], axis=1)
     second_round = lax.all_to_all(
-        second_round.astype(BF16).reshape(32, 24, 3 * HW + 12),
+        second_round.reshape(32, 24, LATE),
         "fsdp",
         split_axis=0,
         concat_axis=0,
         tiled=True,
     )
-    second_round = jnp.sum(second_round.astype(F32), axis=0).astype(BF16)
+    second_round = add_up(second_round, z_rows[0])
     second_round = from_x(second_round, x_at).astype(F32)
-    qkv_out = jnp.transpose(second_round[:, :, : 3 * HW].reshape(SP, 24, 3, HW), (1, 2, 0, 3))
+    qkv_out = jnp.transpose(second_round[:, :, D + 128 :].reshape(SP, 24, 3, HW), (1, 2, 0, 3))
     qkv_out = qkv_out.reshape(24, 3 * D)
-    vector_out = jnp.sum(second_round[:, :, 3 * HW :], axis=0)
-    eight = vector_out.T
+    context_out = jnp.sum(second_round[:, :, :D], axis=0)
+    eight = jnp.sum(second_round[:, :, D : D + 12], axis=0).T
     expand_bias_out = eight[8:].reshape(96)
 
-    reduce_out, expand_out, context_out = finish(
+    reduce_out, expand_out = finish(
         [packed_grads] + [to_x(packed_grads, step) for step in ORDER]
     )
 

time: 223 us -> 239 us (1.072)
  waiting for transfers between devices: 91.1 us -> 104 us
  local copies, waits for them, and re-layouts: 9.24 us -> 12.4 us
    reduce_scatter x1, waiting for transfers between devices: 0.02 us -> 34.8 us  [per_device(): lax.psum_scatter(packed_grads, 'fsdp', scatter_dimension=0, axis_index_gr...]
    ppermute x18, waiting for transfers between devices: 43.5 us -> 25.8 us  [to_x(): return lax.ppermute(values, 'sp', [(i, (i + step) % SP) for i in range(SP)])]
    dot_general x1 -> x0, matrix products: 3.22 us -> none  [rows_first(): lax.dot_general(left_side, right_side, (((0,), (0,)), ((), ())), preferre...]
    ppermute x3, waiting for transfers between devices: 12.4 us -> 9.67 us  [to_z(): lax.ppermute(values, 'fsdp', [(i, (i + 8 * step) % 32) for i in range(32)])]
    pallas_call x1, Pallas kernels: 4.88 us -> 2.35 us  [finish(): pl.pallas_call(finish_kernel, out_shape=(jax.ShapeDtypeStruct((96, D), F3...]
    pallas_call x1 -> x2, Pallas kernels: 16.5 us -> 18.4 us  [the longest x1 18.1 us: attend_back(): pl.pallas_call(attend_back_kernel, out_shape=(jax.ShapeDtypeStruct((LEN,...]
  transfers between devices with their start and end apart: 25 -> 25, of which waited for: 16 -> 12; matrix products, arithmetic and copies ran while one was open for 8% -> 9% of each run, Pallas kernels for 11% -> 11%
where the time goes in v2:
time: 239 us; the launch traced here: 236 us
  waiting for transfers between devices  104 us (44%)
  Pallas kernels  48.2 us (20%)
  starting transfers between devices  43.1 us (18%)
  between operations  15.2 us (6%)
  local copies, waits for them, and re-layouts  12.4 us (5%)
  matrix products  6.6 us (3%)
  other arithmetic  6.44 us (3%)
    reduce_scatter x1, waiting for transfers between devices, per_device(): lax.psum_scatter(packed_grads, 'fsdp', scatter_dimension=0, axis_index_gr...  34.8 us
    ppermute x18, waiting for transfers between devices, to_x(): return lax.ppermute(values, 'sp', [(i, (i + step) % SP) for i in range(SP)])  25.8 us
    ppermute x18, starting transfers between devices, to_x(): return lax.ppermute(values, 'sp', [(i, (i + step) % SP) for i in range(SP)])  23.9 us
    all_to_all x1, waiting for transfers between devices, per_device(): lax.all_to_all(early, 'fsdp', split_axis=0, concat_axis=0, tiled=True)  20.6 us
    pallas_call x1, Pallas kernels, attend_back(): pl.pallas_call(attend_back_kernel, out_shape=(jax.ShapeDtypeStruct((LEN,...  18.1 us
    pallas_call x1, Pallas kernels, middle(): pl.pallas_call(middle_kernel, out_shape=(jax.ShapeDtypeStruct(tall, BF16)...  16 us
    all_gather x1, waiting for transfers between devices, per_device(): packed = lax.all_gather(packed, 'fsdp', axis=0, tiled=True)  13.5 us
    ppermute x3, waiting for transfers between devices, to_z(): lax.ppermute(values, 'fsdp', [(i, (i + 8 * step) % 32) for i in range(32)])  9.67 us
  transfers between devices with their start and end apart: 25, of which 12 were waited for; matrix products, arithmetic and copies ran while one was open for 9% of the time, Pallas kernels for 11%

profile of v2, /device:TPU:6, one launch (start us, length us, event | category | flops | bytes accessed | tf_op | source)
XLA Modules:
  0.0 236.5 jit_solution(5653731445386536404)
XLA Ops:
  7.9 0.6 pad_add_fusion.info_ref
  8.5 4.2 %pack.1 = (bf16[24,6912]{1,0:T(8,128)(2,1)}, bf16[32,32,576]{2,1,0:T(8,128)(2,1)}) custom-call(s32[2]{0:T(128)} %pad_add_fusion.info_ref, bf16[24,2304]{1,0:T(8,128)(2,1)} %rest_0_.1, bf16[24,768]{1,0:T(8,128)(2,1)} %rest_1_.1, bf16[24,3072]{1,0:T(8,128)(2,1)} %rest_2_.1, bf16[96,768]{1,0:T(8,128)(2,1)} %rest_3_.1, ...), custom_call_target="tpu_custom_call" | custom-call | tf_op jit(solution)/shard_map/pack/pallas_call | solution.py:356
  12.7 8.5 %all-to-all-start = ((bf16[32,32,576]{2,1,0:T(8,128)(2,1)}), bf16[32,32,576]{2,1,0:T(8,128)(2,1)S(1)}, u32[]{:S(2)}, u32[]{:S(2)}) async-start(bf16[32,32,576]{2,1,0:T(8,128)(2,1)} %get-tuple-element.28), calls=%async_computation | async-start | bytes 2621440 | tf_op jit(solution)/shard_map/all_to_all | solution.py:498
  21.2 0.9 collective-permute-start
  22.1 1.1 collective-permute-start.1
  23.2 2.1 collective-permute-start.2
  25.3 20.6 %all-to-all-done = bf16[32,32,576]{2,1,0:T(8,128)(2,1)S(1)} async-done(((bf16[32,32,576]{2,1,0:T(8,128)(2,1)}), bf16[32,32,576]{2,1,0:T(8,128)(2,1)S(1)}, u32[]{:S(2)}, u32[]{:S(2)}) %all-to-all-start) | async-done | bytes 1179680 | tf_op jit(solution)/shard_map/all_to_all | solution.py:498
  45.9 0.1 slice_reduce_fusion.3
  46.0 0.1 slice.96
  46.5 0.8 copy-done.10
  47.3 2.4 %add_convert_fusion.qkv_ref = bf16[1024,576]{1,0:T(8,128)(2,1)S(1)} fusion(bf16[768,576]{1,0:T(8,128)(2,1)S(1)} %bitcast.54, f32[576]{0:T(1024)S(1)} %pad_maximum_fusion.3, bf16[256,768]{1,0:T(8,128)(2,1)} %collective-permute-done.2, bf16[256,768]{1,0:T(8,128)(2,1)S(1)} %collective-permute-done.1, bf16[256,768]{1,0:T(8,128)(2,1)S(1)} %collective-permute-done, ...), kind=kOutput, calls=%fused_computation | convolution fusion | flops 913440768 | bytes 3639552 | tf_op jit(solution)/shard_map/dot_general | solution.py:45
  49.8 7.3 %attend.1 = bf16[1024,192]{1,0:T(8,128)(2,1)S(1)} custom-call(s32[2]{0:T(128)S(1)} %copy-done.3, bf16[1024,576]{1,0:T(8,128)(2,1)S(1)} %add_convert_fusion.qkv_ref), custom_call_target="tpu_custom_call" | custom-call | flops 3221225472 | bytes 1572864 | tf_op jit(solution)/shard_map/attend/pallas_call | solution.py:316
  57.2 0.9 collective-permute-start.3
  58.1 1.1 collective-permute-start.4
  59.2 2.1 collective-permute-start.5
  61.3 0.1 convert_element_type.58.rows_ref
  61.4 0.1 reshape.75
  61.5 0.1 reshape.74.bias_ref
  61.7 5.0 %collective-permute-done.3 = bf16[256,192]{1,0:T(8,128)(2,1)S(1)} collective-permute-done((bf16[256,192]{1,0:T(8,128)(2,1)S(1)}, bf16[256,192]{1,0:T(8,128)(2,1)S(1)}, u32[]{:S(2)}, u32[]{:S(2)}) %collective-permute-start.3) | collective-permute-done | bytes 98336 | tf_op jit(solution)/shard_map/ppermute | solution.py:73
  66.7 0.6 collective-permute-done.5
  67.2 0.1 pad_maximum_fusion.1.context_ref
  67.4 13.5 %all-gather.2.cloned.1.call-done.weights_ref = bf16[768,6912]{1,0:T(8,128)(2,1)} async-done(((bf16[24,6912]{1,0:T(8,128)(2,1)}), bf16[768,6912]{1,0:T(8,128)(2,1)}) %all-gather.2.cloned.1.call-update) | async-done | bytes 10616848 | tf_op jit(solution)/shard_map/all_gather | solution.py:497
  80.9 16.0 %middle.1 = (bf16[256,768]{1,0:T(8,128)(2,1)}, f32[256,768]{1,0:T(8,128)S(1)}, bf16[4,256,192]{2,1,0:T(8,128)(2,1)S(1)}, f32[8,768]{1,0:T(8,128)S(1)}, f32[4,768...) custom-call(s32[2]{0:T(128)S(1)} %copy-done.3, ...), custom_call_target="tpu_custom_call" | custom-call | flops 8153726976 | bytes 25165824 | tf_op jit(solution)/shard_map/middle/pallas_call | solution.py:433
  96.9 1.0 copy-done.8
  98.1 1.1 collective-permute-start.6
  99.2 1.2 collective-permute-start.7
  100.4 2.1 collective-permute-start.8
  102.5 1.1 pad_maximum_fusion.tokens_ref
  103.6 4.5 %collective-permute-done.6 = bf16[256,192]{1,0:T(8,128)(2,1)S(1)} collective-permute-done((bf16[256,192]{1,0:T(8,128)(2,1)S(1)}, bf16[256,192]{1,0:T(8,128)(2,1)S(1)}, u32[]{:S(2)}, u32[]{:S(2)}) %collective-permute-start.6) | collective-permute-done | bytes 98336 | tf_op jit(solution)/shard_map/ppermute | solution.py:73
  108.1 0.6 collective-permute-done.8
  108.6 0.1 pad_maximum_fusion.2.grad_ref
  108.7 18.1 %attend_back.1 = (bf16[1024,576]{1,0:T(8,128)(2,1)S(1)}, bf16[768,1472]{1,0:T(8,128)(2,1)S(1)}) custom-call(s32[2]{0:T(128)S(1)} %copy-done.3, bf16[1024,576]{1,0:T(8,128)(2,1)S(1)} %copy-done.7, bf16[1024,192]{1,0:T(8,128)(2,1)S(1)} %pad_maximum_fusion.2.grad_ref, bf16[1024,768]{1,0:T(8,128)(2,1)S(1)} %pad_maximum_fusion.tokens_ref, ...), custom_call_target="tpu_custom_call" | custom-call | flops 8053063680 | bytes 2752512 | tf_op jit(solution)/shard_map/attend_back/pallas_call | solution.py:330
  126.9 1.4 copy-done.1
  128.3 1.1 copy-done.5
  129.4 5.5 %all-to-all-start.1 = ((bf16[32,24,1472]{2,1,0:T(8,128)(2,1)}), bf16[32,24,1472]{2,1,0:T(8,128)(2,1)S(1)}, u32[]{:S(2)}, u32[]{:S(2)}) async-start(bf16[32,24,1472]{2,1,0:T(8,128)(2,1)} %bitcast.43), calls=%async_computation.1 | async-start | bytes 4718592 | tf_op jit(solution)/shard_map/all_to_all | solution.py:556
  134.8 4.2 %convolution_convert_fusion = bf16[1024,768]{1,0:T(8,128)(2,1)} fusion(bf16[1024,576]{1,0:T(8,128)(2,1)} %copy-done.5, bf16[768,576]{1,0:T(8,128)(2,1)} %bitcast.55), kind=kOutput, calls=%fused_computation.1 | convolution fusion | flops 906756096 | bytes 3637248 | tf_op jit(solution)/shard_map/dot_general | solution.py:55
  139.1 2.2 fusion.2
  141.3 0.9 collective-permute-start.10
  142.1 3.3 %collective-permute-start.11 = (bf16[256,768]{1,0:T(8,128)(2,1)}, bf16[256,768]{1,0:T(8,128)(2,1)}, u32[]{:S(2)}, u32[]{:S(2)}) collective-permute-start(bf16[256,768]{1,0:T(8,128)(2,1)} %get-tuple-element.54), channel_id=1, source_target_pairs={{0,2},{1,3},{2,0},{3,1},{4,6},{5,7},{6,4},{7,5},{8,10},{9,11},{10,... | collective-permute-start | bytes 1179656 | tf_op jit(solution)/shard_map/ppermute | solution.py:73
  145.4 34.8 %reduce-scatter.2.cloned.1.call-done = bf16[96,6144]{1,0:T(8,128)(2,1)} async-done(((bf16[768,6144]{1,0:T(8,128)(2,1)}), bf16[96,6144]{1,0:T(8,128)(2,1)}) %reduce-scatter.2.cloned.1.call-update) | async-done | bytes 1179664 | tf_op jit(solution)/shard_map/reduce_scatter | solution.py:524
  180.3 2.1 constant_dynamic-slice_fusion.2
  182.4 1.5 collective-permute-start.15
  183.9 1.7 collective-permute-start.16
  185.6 1.9 collective-permute-start.17
  187.5 2.3 fusion
  189.9 2.8 %collective-permute-done.15 = bf16[24,6144]{1,0:T(8,128)(2,1)} collective-permute-done((bf16[24,6144]{1,0:T(8,128)(2,1)}, bf16[24,6144]{1,0:T(8,128)(2,1)}, u32[]{:S(2)}, u32[]{:S(2)}) %collective-permute-start.15) | collective-permute-done | bytes 294944 | tf_op jit(solution)/shard_map/ppermute | solution.py:77
  192.6 1.5 collective-permute-done.16
  194.2 5.4 %collective-permute-done.17 = bf16[24,6144]{1,0:T(8,128)(2,1)} collective-permute-done((bf16[24,6144]{1,0:T(8,128)(2,1)}, bf16[24,6144]{1,0:T(8,128)(2,1)}, u32[]{:S(2)}, u32[]{:S(2)}) %collective-permute-start.17) | collective-permute-done | bytes 294944 | tf_op jit(solution)/shard_map/ppermute | solution.py:77
  199.5 1.4 add_convert_fusion.2
  200.9 0.6 collective-permute-start.18
  201.5 1.5 collective-permute-start.19
  203.0 1.5 collective-permute-start.20
  204.5 0.3 add_up.1
  204.8 1.2 collective-permute-start.12
  206.0 2.4 %collective-permute-start.13 = (bf16[24,1472]{1,0:T(8,128)(2,1)S(1)}, bf16[24,1472]{1,0:T(8,128)(2,1)S(1)}, u32[]{:S(2)}, u32[]{:S(2)}) collective-permute-start(bf16[24,1472]{1,0:T(8,128)(2,1)S(1)} %add_up.1), channel_id=1, source_target_pairs={{0,2},{1,3},{2,0},{3,1},{4,6},{5,7},{6,4},{7,5},{8,10},{9,11},{10,... | collective-permute-start | bytes 211976 | tf_op jit(solution)/shard_map/ppermute | solution.py:73
  208.4 10.8 %collective-permute-done.12 = bf16[24,1472]{1,0:T(8,128)(2,1)S(1)} collective-permute-done((bf16[24,1472]{1,0:T(8,128)(2,1)S(1)}, bf16[24,1472]{1,0:T(8,128)(2,1)S(1)}, u32[]{:S(2)}, u32[]{:S(2)}) %collective-permute-start.12) | collective-permute-done | bytes 70688 | tf_op jit(solution)/shard_map/ppermute | solution.py:73
  219.3 4.3 %collective-permute-done.14 = bf16[24,1472]{1,0:T(8,128)(2,1)S(1)} collective-permute-done((bf16[24,1472]{1,0:T(8,128)(2,1)S(1)}, bf16[24,1472]{1,0:T(8,128)(2,1)S(1)}, u32[]{:S(2)}, u32[]{:S(2)}) %collective-permute-start.14) | collective-permute-done | bytes 70688 | tf_op jit(solution)/shard_map/ppermute | solution.py:73
  223.7 0.2 reshape.71
  223.9 0.2 copy.52
  224.1 0.9 reshape.72
  225.2 0.6 reshape.73
  225.8 0.8 slice_reduce_fusion.4
  226.6 0.6 slice_reduce_fusion
  227.3 2.4 finish.1
  (69 shorter events, 1.0 us)
Async XLA Ops:
  7.2 73.7 %all-gather.2.cloned.1.call-start = ((), (), s32[]{:S(2)}) async-start(), calls=%async_computation.3 | async-start | bytes 10948608 | tf_op jit(solution)/shard_map/all_gather | solution.py:497
  12.6 8.6 %copy-start.2 = (bf16[1,256,768]{2,1,0:T(8,128)(2,1)S(1)}, bf16[1,256,768]{2,1,0:T(8,128)(2,1)}, u32[]{:S(2)}) copy-start(bf16[1,256,768]{2,1,0:T(8,128)(2,1)} %param.18) | copy-start | bytes 1179652
  12.7 33.2 %all-to-all-start = ((bf16[32,32,576]{2,1,0:T(8,128)(2,1)}), bf16[32,32,576]{2,1,0:T(8,128)(2,1)S(1)}, u32[]{:S(2)}, u32[]{:S(2)}) async-start(bf16[32,32,576]{2,1,0:T(8,128)(2,1)} %get-tuple-element.28), calls=%async_computation | async-start | bytes 2621440 | tf_op jit(solution)/shard_map/all_to_all | solution.py:498
  21.1 159.1 %reduce-scatter.2.cloned.1.call-start = ((), (), s32[]{:S(2)}) async-start(), calls=%async_computation.4 | async-start | bytes 10616832 | tf_op jit(solution)/shard_map/reduce_scatter | solution.py:524
  21.2 25.3 %collective-permute-start = (bf16[256,768]{1,0:T(8,128)(2,1)S(1)}, bf16[256,768]{1,0:T(8,128)(2,1)S(1)}, u32[]{:S(2)}, u32[]{:S(2)}) collective-permute-start(bf16[256,768]{1,0:T(8,128)(2,1)S(1)} %bitcast.44), channel_id=1, source_target_pairs={{0,3},{1,0},{2,1},{3,2},{4,7},{5,4},{6,5},{7,6},{8,11},{9,8},{10,9... | collective-permute-start | bytes 1179656 | tf_op jit(solution)/shard_map/ppermute | solution.py:73
  22.1 24.4 %collective-permute-start.1 = (bf16[256,768]{1,0:T(8,128)(2,1)S(1)}, bf16[256,768]{1,0:T(8,128)(2,1)S(1)}, u32[]{:S(2)}, u32[]{:S(2)}) collective-permute-start(bf16[256,768]{1,0:T(8,128)(2,1)S(1)} %bitcast.45), channel_id=1, source_target_pairs={{0,2},{1,3},{2,0},{3,1},{4,6},{5,7},{6,4},{7,5},{8,10},{9,11},{10,... | collective-permute-start | bytes 1179656 | tf_op jit(solution)/shard_map/ppermute | solution.py:73
  23.2 23.3 %collective-permute-start.2 = (bf16[256,768]{1,0:T(8,128)(2,1)S(1)}, bf16[256,768]{1,0:T(8,128)(2,1)}, u32[]{:S(2)}, u32[]{:S(2)}) collective-permute-start(bf16[256,768]{1,0:T(8,128)(2,1)S(1)} %bitcast.46), channel_id=1, source_target_pairs={{0,1},{1,2},{2,3},{3,0},{4,5},{5,6},{6,7},{7,4},{8,9},{9,10},{10,1... | collective-permute-start | bytes 1179656 | tf_op jit(solution)/shard_map/ppermute | solution.py:73
  46.3 1.0 copy-start.10
  46.5 3.3 %copy-start.11 = (bf16[256,768]{1,0:T(8,128)(2,1)}, bf16[256,768]{1,0:T(8,128)(2,1)S(1)}, u32[]{:S(2)}) copy-start(bf16[256,768]{1,0:T(8,128)(2,1)S(1)} %collective-permute-done) | copy-start | bytes 1179652
  46.5 3.3 %copy-start.13 = (bf16[256,768]{1,0:T(8,128)(2,1)}, bf16[256,768]{1,0:T(8,128)(2,1)S(1)}, u32[]{:S(2)}) copy-start(bf16[256,768]{1,0:T(8,128)(2,1)S(1)} %collective-permute-done.1) | copy-start | bytes 1179652
  47.3 2.4 %copy-start.3 = (s32[2]{0:T(128)S(1)}, s32[2]{0:T(128)}, u32[]{:S(2)}) copy-start(s32[2]{0:T(128)} %pad_add_fusion.info_ref) | copy-start | bytes 28
  49.8 7.3 %copy-start.6 = (bf16[1024,576]{1,0:T(8,128)(2,1)}, bf16[1024,576]{1,0:T(8,128)(2,1)S(1)}, u32[]{:S(2)}) copy-start(bf16[1024,576]{1,0:T(8,128)(2,1)S(1)} %add_convert_fusion.qkv_ref) | copy-start | bytes 3538948
  57.1 23.8 %copy-start.4 = (bf16[1,256,768]{2,1,0:T(8,128)(2,1)S(1)}, bf16[1,256,768]{2,1,0:T(8,128)(2,1)}, u32[]{:S(2)}) copy-start(bf16[1,256,768]{2,1,0:T(8,128)(2,1)} %param.33) | copy-start | bytes 1179652
  57.2 9.5 %collective-permute-start.3 = (bf16[256,192]{1,0:T(8,128)(2,1)S(1)}, bf16[256,192]{1,0:T(8,128)(2,1)S(1)}, u32[]{:S(2)}, u32[]{:S(2)}) collective-permute-start(bf16[256,192]{1,0:T(8,128)(2,1)S(1)} %get-tuple-element.66), channel_id=1, source_target_pairs={{0,3},{1,0},{2,1},{3,2},{4,7},{5,4},{6,5},{7,6},{8,11},{9,8},{10,9... | collective-permute-start | bytes 294920 | tf_op jit(solution)/shard_map/ppermute | solution.py:73
  58.1 8.6 %collective-permute-start.4 = (bf16[256,192]{1,0:T(8,128)(2,1)S(1)}, bf16[256,192]{1,0:T(8,128)(2,1)S(1)}, u32[]{:S(2)}, u32[]{:S(2)}) collective-permute-start(bf16[256,192]{1,0:T(8,128)(2,1)S(1)} %get-tuple-element.65), channel_id=1, source_target_pairs={{0,2},{1,3},{2,0},{3,1},{4,6},{5,7},{6,4},{7,5},{8,10},{9,11},{10,... | collective-permute-start | bytes 294920 | tf_op jit(solution)/shard_map/ppermute | solution.py:73
  59.2 8.1 %collective-permute-start.5 = (bf16[256,192]{1,0:T(8,128)(2,1)S(1)}, bf16[256,192]{1,0:T(8,128)(2,1)S(1)}, u32[]{:S(2)}, u32[]{:S(2)}) collective-permute-start(bf16[256,192]{1,0:T(8,128)(2,1)S(1)} %get-tuple-element.64), channel_id=1, source_target_pairs={{0,1},{1,2},{2,3},{3,0},{4,5},{5,6},{6,7},{7,4},{8,9},{9,10},{10,1... | collective-permute-start | bytes 294920 | tf_op jit(solution)/shard_map/ppermute | solution.py:73
  96.9 1.0 copy-start.8
  97.9 4.6 %copy-start.12 = (bf16[256,768]{1,0:T(8,128)(2,1)S(1)}, bf16[256,768]{1,0:T(8,128)(2,1)}, u32[]{:S(2)}) copy-start(bf16[256,768]{1,0:T(8,128)(2,1)} %copy-done.11) | copy-start | bytes 1179652
  97.9 4.6 %copy-start.14 = (bf16[256,768]{1,0:T(8,128)(2,1)S(1)}, bf16[256,768]{1,0:T(8,128)(2,1)}, u32[]{:S(2)}) copy-start(bf16[256,768]{1,0:T(8,128)(2,1)} %copy-done.13) | copy-start | bytes 1179652
  98.1 10.0 %collective-permute-start.6 = (bf16[256,192]{1,0:T(8,128)(2,1)S(1)}, bf16[256,192]{1,0:T(8,128)(2,1)S(1)}, u32[]{:S(2)}, u32[]{:S(2)}) collective-permute-start(bf16[256,192]{1,0:T(8,128)(2,1)S(1)} %get-tuple-element.62), channel_id=1, source_target_pairs={{0,3},{1,0},{2,1},{3,2},{4,7},{5,4},{6,5},{7,6},{8,11},{9,8},{10,9... | collective-permute-start | bytes 294920 | tf_op jit(solution)/shard_map/ppermute | solution.py:73
  99.2 8.8 %collective-permute-start.7 = (bf16[256,192]{1,0:T(8,128)(2,1)S(1)}, bf16[256,192]{1,0:T(8,128)(2,1)S(1)}, u32[]{:S(2)}, u32[]{:S(2)}) collective-permute-start(bf16[256,192]{1,0:T(8,128)(2,1)S(1)} %get-tuple-element.61), channel_id=1, source_target_pairs={{0,2},{1,3},{2,0},{3,1},{4,6},{5,7},{6,4},{7,5},{8,10},{9,11},{10,... | collective-permute-start | bytes 294920 | tf_op jit(solution)/shard_map/ppermute | solution.py:73
  100.4 8.3 %copy-start.7 = (bf16[1024,576]{1,0:T(8,128)(2,1)S(1)}, bf16[1024,576]{1,0:T(8,128)(2,1)}, u32[]{:S(2)}) copy-start(bf16[1024,576]{1,0:T(8,128)(2,1)} %copy-done.6) | copy-start | bytes 3538948
  100.4 8.4 %copy-start.9 = (bf16[768,768]{1,0:T(8,128)(2,1)S(1)}, bf16[768,768]{1,0:T(8,128)(2,1)}, u32[]{:S(2)}) copy-start(bf16[768,768]{1,0:T(8,128)(2,1)} %copy-done.8) | copy-start | bytes 3538948
  100.4 8.2 %collective-permute-start.8 = (bf16[256,192]{1,0:T(8,128)(2,1)S(1)}, bf16[256,192]{1,0:T(8,128)(2,1)S(1)}, u32[]{:S(2)}, u32[]{:S(2)}) collective-permute-start(bf16[256,192]{1,0:T(8,128)(2,1)S(1)} %get-tuple-element.60), channel_id=1, source_target_pairs={{0,1},{1,2},{2,3},{3,0},{4,5},{5,6},{6,7},{7,4},{8,9},{9,10},{10,1... | collective-permute-start | bytes 294920 | tf_op jit(solution)/shard_map/ppermute | solution.py:73
  126.9 1.4 copy-start.1
  128.3 1.1 copy-start.5
  129.4 75.1 %all-to-all-start.1 = ((bf16[32,24,1472]{2,1,0:T(8,128)(2,1)}), bf16[32,24,1472]{2,1,0:T(8,128)(2,1)S(1)}, u32[]{:S(2)}, u32[]{:S(2)}) async-start(bf16[32,24,1472]{2,1,0:T(8,128)(2,1)} %bitcast.43), calls=%async_computation.1 | async-start | bytes 4718592 | tf_op jit(solution)/shard_map/all_to_all | solution.py:556
  141.3 44.3 %collective-permute-start.10 = (bf16[256,768]{1,0:T(8,128)(2,1)}, bf16[256,768]{1,0:T(8,128)(2,1)}, u32[]{:S(2)}, u32[]{:S(2)}) collective-permute-start(bf16[256,768]{1,0:T(8,128)(2,1)} %get-tuple-element.55), channel_id=1, source_target_pairs={{0,3},{1,0},{2,1},{3,2},{4,7},{5,4},{6,5},{7,6},{8,11},{9,8},{10,9... | collective-permute-start | bytes 1179656 | tf_op jit(solution)/shard_map/ppermute | solution.py:73
  142.1 45.4 %collective-permute-start.11 = (bf16[256,768]{1,0:T(8,128)(2,1)}, bf16[256,768]{1,0:T(8,128)(2,1)}, u32[]{:S(2)}, u32[]{:S(2)}) collective-permute-start(bf16[256,768]{1,0:T(8,128)(2,1)} %get-tuple-element.54), channel_id=1, source_target_pairs={{0,2},{1,3},{2,0},{3,1},{4,6},{5,7},{6,4},{7,5},{8,10},{9,11},{10,... | collective-permute-start | bytes 1179656 | tf_op jit(solution)/shard_map/ppermute | solution.py:73
  145.4 42.1 %collective-permute-start.9 = (bf16[256,768]{1,0:T(8,128)(2,1)S(1)}, bf16[256,768]{1,0:T(8,128)(2,1)}, u32[]{:S(2)}, u32[]{:S(2)}) collective-permute-start(bf16[256,768]{1,0:T(8,128)(2,1)S(1)} %get-tuple-element.53), channel_id=1, source_target_pairs={{0,1},{1,2},{2,3},{3,0},{4,5},{5,6},{6,7},{7,4},{8,9},{9,10},{10,1... | collective-permute-start | bytes 1179656 | tf_op jit(solution)/shard_map/ppermute | solution.py:73
  182.4 10.3 %collective-permute-start.15 = (bf16[24,6144]{1,0:T(8,128)(2,1)}, bf16[24,6144]{1,0:T(8,128)(2,1)}, u32[]{:S(2)}, u32[]{:S(2)}) collective-permute-start(bf16[24,6144]{1,0:T(8,128)(2,1)} %get-tuple-element.56), channel_id=1, source_target_pairs={{0,32},{4,36},{8,40},{12,44},{16,48},{20,52},{24,56},{28,60},{32,6... | collective-permute-start | bytes 884744 | tf_op jit(solution)/shard_map/ppermute | solution.py:77
  183.9 10.3 %collective-permute-start.16 = (bf16[24,6144]{1,0:T(8,128)(2,1)}, bf16[24,6144]{1,0:T(8,128)(2,1)}, u32[]{:S(2)}, u32[]{:S(2)}) collective-permute-start(bf16[24,6144]{1,0:T(8,128)(2,1)} %get-tuple-element.58), channel_id=1, source_target_pairs={{0,96},{4,100},{8,104},{12,108},{16,112},{20,116},{24,120},{28,124... | collective-permute-start | bytes 884744 | tf_op jit(solution)/shard_map/ppermute | solution.py:77
  185.6 13.9 %collective-permute-start.17 = (bf16[24,6144]{1,0:T(8,128)(2,1)}, bf16[24,6144]{1,0:T(8,128)(2,1)}, u32[]{:S(2)}, u32[]{:S(2)}) collective-permute-start(bf16[24,6144]{1,0:T(8,128)(2,1)} %get-tuple-element.57), channel_id=1, source_target_pairs={{0,64},{4,68},{8,72},{12,76},{16,80},{20,84},{24,88},{28,92},{32,9... | collective-permute-start | bytes 884744 | tf_op jit(solution)/shard_map/ppermute | solution.py:77
  200.9 26.3 %collective-permute-start.18 = (bf16[24,6144]{1,0:T(8,128)(2,1)S(1)}, bf16[24,6144]{1,0:T(8,128)(2,1)S(1)}, u32[]{:S(2)}, u32[]{:S(2)}) collective-permute-start(bf16[24,6144]{1,0:T(8,128)(2,1)S(1)} %get-tuple-element.51.a_ref), channel_id=1, source_target_pairs={{0,1},{1,2},{2,3},{3,0},{4,5},{5,6},{6,7},{7,4},{8,9},{9,10},{10,1... | collective-permute-start | bytes 884744 | tf_op jit(solution)/shard_map/ppermute | solution.py:73
  201.5 25.7 %collective-permute-start.19 = (bf16[24,6144]{1,0:T(8,128)(2,1)S(1)}, bf16[24,6144]{1,0:T(8,128)(2,1)S(1)}, u32[]{:S(2)}, u32[]{:S(2)}) collective-permute-start(bf16[24,6144]{1,0:T(8,128)(2,1)S(1)} %get-tuple-element.51.a_ref), channel_id=1, source_target_pairs={{0,3},{1,0},{2,1},{3,2},{4,7},{5,4},{6,5},{7,6},{8,11},{9,8},{10,9... | collective-permute-start | bytes 884744 | tf_op jit(solution)/shard_map/ppermute | solution.py:73
  203.0 24.2 %collective-permute-start.20 = (bf16[24,6144]{1,0:T(8,128)(2,1)S(1)}, bf16[24,6144]{1,0:T(8,128)(2,1)}, u32[]{:S(2)}, u32[]{:S(2)}) collective-permute-start(bf16[24,6144]{1,0:T(8,128)(2,1)S(1)} %get-tuple-element.51.a_ref), channel_id=1, source_target_pairs={{0,2},{1,3},{2,0},{3,1},{4,6},{5,7},{6,4},{7,5},{8,10},{9,11},{10,... | collective-permute-start | bytes 884744 | tf_op jit(solution)/shard_map/ppermute | solution.py:73
  204.8 14.4 %collective-permute-start.12 = (bf16[24,1472]{1,0:T(8,128)(2,1)S(1)}, bf16[24,1472]{1,0:T(8,128)(2,1)S(1)}, u32[]{:S(2)}, u32[]{:S(2)}) collective-permute-start(bf16[24,1472]{1,0:T(8,128)(2,1)S(1)} %add_up.1), channel_id=1, source_target_pairs={{0,3},{1,0},{2,1},{3,2},{4,7},{5,4},{6,5},{7,6},{8,11},{9,8},{10,9... | collective-permute-start | bytes 211976 | tf_op jit(solution)/shard_map/ppermute | solution.py:73
  206.0 13.2 %collective-permute-start.13 = (bf16[24,1472]{1,0:T(8,128)(2,1)S(1)}, bf16[24,1472]{1,0:T(8,128)(2,1)S(1)}, u32[]{:S(2)}, u32[]{:S(2)}) collective-permute-start(bf16[24,1472]{1,0:T(8,128)(2,1)S(1)} %add_up.1), channel_id=1, source_target_pairs={{0,2},{1,3},{2,0},{3,1},{4,6},{5,7},{6,4},{7,5},{8,10},{9,11},{10,... | collective-permute-start | bytes 211976 | tf_op jit(solution)/shard_map/ppermute | solution.py:73
  219.2 4.4 %collective-permute-start.14 = (bf16[24,1472]{1,0:T(8,128)(2,1)S(1)}, bf16[24,1472]{1,0:T(8,128)(2,1)S(1)}, u32[]{:S(2)}, u32[]{:S(2)}) collective-permute-start(bf16[24,1472]{1,0:T(8,128)(2,1)S(1)} %add_up.1), channel_id=1, source_target_pairs={{0,1},{1,2},{2,3},{3,0},{4,5},{5,6},{6,7},{7,4},{8,9},{9,10},{10,1... | collective-permute-start | bytes 211976 | tf_op jit(solution)/shard_map/ppermute | solution.py:73
  223.7 3.5 %copy-start = (bf16[768,768]{1,0:T(8,128)(2,1)S(1)}, bf16[768,768]{1,0:T(8,128)(2,1)}, u32[]{:S(2)}) copy-start(bf16[768,768]{1,0:T(8,128)(2,1)} %constant.73.clone.rest_4_.order_ref) | copy-start | bytes 3538948
Sparse Core Ops, SparseCore 0:
  12.8 68.0 all-gather.1
  98.1 82.1 reduce-scatter.1

commit v3 on v2

--- a/solution.py
+++ b/solution.py
@@ -71,6 +71,10 @@
 
 def to_x(values, step):
     return lax.ppermute(values, "sp", [(i, (i + step) % SP) for i in range(SP)])
+
+
+def to_core(values):
+    return lax.ppermute(values, "fsdp", [(i, i ^ 1) for i in range(32)])
 
 
 def to_z(values, step):
@@ -113,8 +117,8 @@
 
 
 def attend_back_kernel(
-    info_ref, qkv_ref, grad_ref, tokens_ref, context_ref, sums_ref, bias_sum_ref,
-    out_ref, late_ref, key_sum, value_sum, stack,
+    info_ref, qkv_ref, grad_ref, tokens_ref, sums_ref, bias_sum_ref,
+    out_ref, mine_ref, other_ref, key_sum, value_sum, stack,
 ):
     valid = masked_keys(info_ref, (LEN, 1), 0)
     key_sum[...] = jnp.zeros_like(key_sum)
@@ -147,8 +151,6 @@
         ).astype(BF16)
 
     low = out_ref[...]
-    late_ref[:, D + 128 :] = rows_first(tokens_ref[...], low).astype(BF16)
-    late_ref[:, :D] = context_ref[...]
     sums = jnp.sum(low.astype(F32), axis=0, keepdims=True)
     stack[...] = jnp.zeros_like(stack)
     for row, part in ((0, 0), (1, 2)):
@@ -158,11 +160,25 @@
         )
     stack[2:8, :] = sums_ref[0:6, :]
     stack[8:12, :] = bias_sum_ref[...]
-    late_ref[:, D : D + 128] = stack[...].T.astype(BF16)
+    mine_ref[:, 128 + 3 * HW :] = jnp.zeros((D // 2, LATE - 128 - 3 * HW), BF16)
+    other_ref[:, 128 + 3 * HW :] = jnp.zeros((D // 2, LATE - 128 - 3 * HW), BF16)
+    for cols, full in (
+        (slice(0, 128), stack[...].T),
+        (slice(128, 128 + 3 * HW), rows_first(tokens_ref[...], low)),
+    ):
+        even, odd = (
+            jnp.concatenate(
+                [full[(2 * chip + at) * 24 : (2 * chip + at + 1) * 24] for chip in range(16)], axis=0
+            )
+            for at in range(2)
+        )
+        first = info_ref[2] == 0
+        mine_ref[:, cols] = jnp.where(first, even, odd).astype(BF16)
+        other_ref[:, cols] = jnp.where(first, odd, even).astype(BF16)
 
 
 PACKED = 2 * FF + D
-LATE = D + 128 + 3 * HW
+LATE = D
 
 
 def reorder_matrix():
@@ -220,7 +236,7 @@
 
 def middle_kernel(
     info_ref, context_ref, own_ref, cotangent_ref, rows_ref, bias_ref, weights_ref,
-    hidden_ref, grad_one_ref, context_grad_ref, sums_ref, bias_sum_ref, context_sum_ref, grads_ref,
+    hidden_ref, grad_one_ref, context_grad_ref, sums_ref, bias_sum_ref, grads_ref,
     held, made, slopes, active, in_sems, out_sems,
 ):
     def piece(block):
@@ -295,10 +311,10 @@
     grad_one_ref[...] = grad_one
     branch_grad = grad_one.astype(BF16)
     sums_ref[0:1, :] = jnp.sum(branch_grad.astype(F32), axis=0, keepdims=True)
-    for block in range(SP):
-        context_sum_ref[block * HW : (block + 1) * HW, :] = rows_first(
-            context_ref[groups[block]], branch_grad
-        ).astype(BF16)
+    made[:, piece(8)] = by_plane(
+        jnp.concatenate([rows_first(context_ref[group], branch_grad) for group in groups], axis=0)
+    )
+    sent.append(send(8))
     for block in range(SP):
         context_grad_ref[groups[block]] = by_transpose(
             branch_grad, held[block * HW : (block + 1) * HW, piece(8)]
@@ -326,15 +342,16 @@
     )(info, qkv)
 
 
-def attend_back(info, qkv, grads, tokens, context_sum, row_sums, bias_sums):
+def attend_back(info, qkv, grads, tokens, row_sums, bias_sums):
     return pl.pallas_call(
         attend_back_kernel,
         out_shape=(
             jax.ShapeDtypeStruct((LEN, 3 * HW), BF16),
-            jax.ShapeDtypeStruct((D, LATE), BF16),
-        ),
-        in_specs=[SMEM] + [VMEM] * 6,
-        out_specs=(VMEM, VMEM),
+            jax.ShapeDtypeStruct((D // 2, LATE), BF16),
+            jax.ShapeDtypeStruct((D // 2, LATE), BF16),
+        ),
+        in_specs=[SMEM] + [VMEM] * 5,
+        out_specs=(VMEM,) * 3,
         scratch_shapes=[
             pltpu.VMEM((HEADS, LEN, DH), F32),
             pltpu.VMEM((HEADS, LEN, DH), F32),
@@ -345,7 +362,7 @@
             flops=10 * HEADS * LEN * LEN * 256, bytes_accessed=LEN * HW * 14, transcendentals=0
         ),
         name="attend_back",
-    )(info, qkv, grads, tokens, context_sum, row_sums, bias_sums)
+    )(info, qkv, grads, tokens, row_sums, bias_sums)
 
 
 def pack(info, qkv_weight, context_weight, expand_weight, reduce_weight, vectors):
@@ -368,34 +385,14 @@
     )(info, *operands)
 
 
-def add_up_kernel(parts_ref, after_ref, out_ref):
-    total = parts_ref[0].astype(F32)
-    for owner in range(1, 32):
-        total = total + parts_ref[owner].astype(F32)
-    out_ref[...] = total.astype(BF16)
-
-
-def add_up(parts, after):
-    return pl.pallas_call(
-        add_up_kernel,
-        out_shape=jax.ShapeDtypeStruct(parts.shape[1:], BF16),
-        in_specs=[VMEM, pl.BlockSpec(memory_space=pl.ANY)],
-        out_specs=VMEM,
-        compiler_params=PARAMS,
-        cost_estimate=pl.CostEstimate(
-            flops=parts.size, bytes_accessed=2 * parts.size, transcendentals=0
-        ),
-        name="add_up",
-    )(parts, after)
-
-
-def finish_kernel(a_ref, b_ref, c_ref, d_ref, order_ref, reduce_ref, expand_ref):
+def finish_kernel(a_ref, b_ref, c_ref, d_ref, order_ref, reduce_ref, expand_ref, context_ref):
     def total(start, width):
         parts = [ref[:, start : start + width].astype(F32) for ref in (a_ref, b_ref, c_ref, d_ref)]
         return (parts[0] + parts[1]) + (parts[2] + parts[3])
 
     for part in range(4):
         reduce_ref[part * 24 : (part + 1) * 24, :] = total(part * D, D)
+    context_ref[...] = total(2 * FF, D)
     moved = [total(FF + part * D, D) for part in range(4)]
     left = jnp.concatenate(
         [
@@ -420,9 +417,10 @@
         out_shape=(
             jax.ShapeDtypeStruct((96, D), F32),
             jax.ShapeDtypeStruct((24, FF), F32),
+            jax.ShapeDtypeStruct((24, D), F32),
         ),
         in_specs=[VMEM] * 5,
-        out_specs=(VMEM,) * 2,
+        out_specs=(VMEM,) * 3,
         compiler_params=PARAMS,
         name="finish",
     )(*pieces, jnp.asarray(reorder_matrix(), BF16))
@@ -438,18 +436,17 @@
             jax.ShapeDtypeStruct((SP, LOCAL, HW), BF16),
             jax.ShapeDtypeStruct((8, D), F32),
             jax.ShapeDtypeStruct((4, D), F32),
-            jax.ShapeDtypeStruct((D, D), BF16),
-            jax.ShapeDtypeStruct((D, 2 * FF), BF16),
+            jax.ShapeDtypeStruct((D, PACKED), BF16),
         ),
         in_specs=[SMEM] + [VMEM] * 5 + [pl.BlockSpec(memory_space=pl.ANY)],
-        out_specs=(VMEM,) * 6 + (pl.BlockSpec(memory_space=pl.ANY),),
+        out_specs=(VMEM,) * 5 + (pl.BlockSpec(memory_space=pl.ANY),),
         scratch_shapes=[
             pltpu.VMEM((D, PACKED), BF16),
-            pltpu.VMEM((D, 2 * FF), BF16),
+            pltpu.VMEM((D, PACKED), BF16),
             pltpu.VMEM((LOCAL, FF), F32),
             pltpu.VMEM((LOCAL, FF), BF16),
             pltpu.SemaphoreType.DMA((9,)),
-            pltpu.SemaphoreType.DMA((8,)),
+            pltpu.SemaphoreType.DMA((9,)),
         ],
         compiler_params=pltpu.CompilerParams(vmem_limit_bytes=48 * 1024 * 1024),
         cost_estimate=pl.CostEstimate(
@@ -488,7 +485,8 @@
     for step in ORDER:
         tokens[step] = to_x(own, -step)
 
-    info = jnp.stack([x_at.astype(jnp.int32), lengths[0]])
+    core = lax.axis_index("fsdp") & 1
+    info = jnp.stack([x_at.astype(jnp.int32), lengths[0], core.astype(jnp.int32)])
     packed, early = pack(
         info, qkv_weight, context_weight, expand_weight, reduce_weight,
         (query_bias, value_bias, context_bias, first_gain, first_shift, reduce_bias,
@@ -518,7 +516,7 @@
         groups[SP - step] = to_x(context[step * LOCAL : (step + 1) * LOCAL], step)
     context_tok = jnp.stack(groups)
 
-    hidden_out, grad_one, context_grad, row_sums, bias_sums, context_sum, packed_grads = middle(
+    hidden_out, grad_one, context_grad, row_sums, bias_sums, packed_grads = middle(
         info, context_tok, own, out_grad[0], rows, expand_add, packed
     )
     packed_grads = lax.psum_scatter(
@@ -533,19 +531,17 @@
     def rows_of(step):
         return lax.dynamic_slice_in_dim(packed_grads, (z_at + step) % 4 * 24, 24, axis=0)
 
-    z_rows = [rows_of(step) for step in range(4)]
-    z_sum = z_rows[0].astype(F32)
+    z_sum = rows_of(0).astype(F32)
     for step in ORDER:
-        z_sum = z_sum + to_z(z_rows[step], step).astype(F32)
+        z_sum = z_sum + to_z(rows_of(step), step).astype(F32)
     packed_grads = z_sum.astype(BF16)
     blocks = [context_grad[0]] + [None] * 3
     for step in ORDER:
         blocks[SP - step] = to_x(context_grad[step], step)
     grad_heads = jnp.concatenate(blocks, axis=0)
 
-    qkv_grad, second_round = attend_back(
-        info, qkv, grad_heads, everyone, context_sum, row_sums, bias_sums
-    )
+    qkv_grad, mine, other = attend_back(info, qkv, grad_heads, everyone, row_sums, bias_sums)
+    second_round = (mine.astype(F32) + to_core(other).astype(F32)).astype(BF16)
 
     partial = by_transpose(qkv_grad, qkv_full).astype(BF16)
     input_sum = grad_one + partial[:LOCAL].astype(F32)
@@ -554,21 +550,21 @@
     input_grad = input_sum.astype(BF16)[None]
 
     second_round = lax.all_to_all(
-        second_round.reshape(32, 24, LATE),
+        second_round.reshape(16, 24, LATE),
         "fsdp",
         split_axis=0,
         concat_axis=0,
+        axis_index_groups=[[2 * chip + at for chip in range(16)] for at in range(2)],
         tiled=True,
     )
-    second_round = add_up(second_round, z_rows[0])
+    second_round = jnp.sum(second_round.astype(F32), axis=0).astype(BF16)
     second_round = from_x(second_round, x_at).astype(F32)
-    qkv_out = jnp.transpose(second_round[:, :, D + 128 :].reshape(SP, 24, 3, HW), (1, 2, 0, 3))
+    qkv_out = jnp.transpose(second_round[:, :, 128 : 128 + 3 * HW].reshape(SP, 24, 3, HW), (1, 2, 0, 3))
     qkv_out = qkv_out.reshape(24, 3 * D)
-    context_out = jnp.sum(second_round[:, :, :D], axis=0)
-    eight = jnp.sum(second_round[:, :, D : D + 12], axis=0).T
+    eight = jnp.sum(second_round[:, :, :12], axis=0).T
     expand_bias_out = eight[8:].reshape(96)
 
-    reduce_out, expand_out = finish(
+    reduce_out, expand_out, context_out = finish(
         [packed_grads] + [to_x(packed_grads, step) for step in ORDER]
     )
 

time: 239 us -> 214 us (0.90)
  waiting for transfers between devices: 104 us -> 90.2 us
  local copies, waits for them, and re-layouts: 12.4 us -> 6.75 us
  matrix products: 6.6 us -> 2.81 us
    reduce_scatter x1, waiting for transfers between devices: 34.8 us -> 3.55 us  [per_device(): lax.psum_scatter(packed_grads, 'fsdp', scatter_dimension=0, axis_index_gr...]
    ppermute x18, waiting for transfers between devices: 25.8 us -> 36.8 us  [to_x(): return lax.ppermute(values, 'sp', [(i, (i + step) % SP) for i in range(SP)])]
    ppermute x3, waiting for transfers between devices: 9.67 us -> 13.3 us  [to_z(): lax.ppermute(values, 'fsdp', [(i, (i + 8 * step) % 32) for i in range(32)])]
    unnamed x37 -> x31, local copies, waits for them, and re-layouts: 4.4 us -> 0.85 us
    dot_general x1, matrix products: 4.21 us -> 1.42 us  [by_transpose(): lax.dot_general(left_side, right_side, (((1,), (1,)), ((), ())), preferre...]
  transfers between devices with their start and end apart: 25 -> 26, of which waited for: 12 -> 17; matrix products, arithmetic and copies ran while one was open for 9% -> 6% of each run, Pallas kernels for 11% -> 12%
where the time goes in v3:
time: 214 us; the launch traced here: 212 us
  waiting for transfers between devices  90.2 us (42%)
  Pallas kernels  47.3 us (22%)
  starting transfers between devices  43.5 us (20%)
  between operations  15.2 us (7%)
  local copies, waits for them, and re-layouts  6.75 us (3%)
  other arithmetic  6.37 us (3%)
  matrix products  2.81 us (1%)
    ppermute x18, waiting for transfers between devices, to_x(): return lax.ppermute(values, 'sp', [(i, (i + step) % SP) for i in range(SP)])  36.8 us
    ppermute x18, starting transfers between devices, to_x(): return lax.ppermute(values, 'sp', [(i, (i + step) % SP) for i in range(SP)])  24.5 us
    all_to_all x1, waiting for transfers between devices, per_device(): lax.all_to_all(early, 'fsdp', split_axis=0, concat_axis=0, tiled=True)  20.6 us
    pallas_call x1, Pallas kernels, attend_back(): pl.pallas_call(attend_back_kernel, out_shape=(jax.ShapeDtypeStruct((LEN,...  18.1 us
    pallas_call x1, Pallas kernels, middle(): pl.pallas_call(middle_kernel, out_shape=(jax.ShapeDtypeStruct(tall, BF16)...  16.3 us
    all_gather x1, waiting for transfers between devices, per_device(): packed = lax.all_gather(packed, 'fsdp', axis=0, tiled=True)  14.1 us
    ppermute x3, waiting for transfers between devices, to_z(): lax.ppermute(values, 'fsdp', [(i, (i + 8 * step) % 32) for i in range(32)])  13.3 us
    all_to_all x1, starting transfers between devices, per_device(): lax.all_to_all(early, 'fsdp', split_axis=0, concat_axis=0, tiled=True)  8.48 us
  transfers between devices with their start and end apart: 26, of which 17 were waited for; matrix products, arithmetic and copies ran while one was open for 6% of the time, Pallas kernels for 12%

profile of v3, /device:TPU:6, one launch (start us, length us, event | category | flops | bytes accessed | tf_op | source)
XLA Modules:
  0.0 212.1 jit_solution(6710382636468175465)
XLA Ops:
  7.9 0.6 pad_add_fusion.info_ref
  8.5 4.2 %pack.1 = (bf16[24,6912]{1,0:T(8,128)(2,1)}, bf16[32,32,576]{2,1,0:T(8,128)(2,1)}) custom-call(s32[3]{0:T(128)} %pad_add_fusion.info_ref, bf16[24,2304]{1,0:T(8,128)(2,1)} %rest_0_.1, bf16[24,768]{1,0:T(8,128)(2,1)} %rest_1_.1, bf16[24,3072]{1,0:T(8,128)(2,1)} %rest_2_.1, bf16[96,768]{1,0:T(8,128)(2,1)} %rest_3_.1, ...), custom_call_target="tpu_custom_call" | custom-call | tf_op jit(solution)/shard_map/pack/pallas_call | solution.py:373
  12.7 8.5 %all-to-all-start = ((bf16[32,32,576]{2,1,0:T(8,128)(2,1)}), bf16[32,32,576]{2,1,0:T(8,128)(2,1)S(1)}, u32[]{:S(2)}, u32[]{:S(2)}) async-start(bf16[32,32,576]{2,1,0:T(8,128)(2,1)} %get-tuple-element.29), calls=%async_computation | async-start | bytes 2621440 | tf_op jit(solution)/shard_map/all_to_all | solution.py:496
  21.2 0.9 collective-permute-start
  22.1 1.1 collective-permute-start.1
  23.2 2.1 collective-permute-start.2
  25.3 20.6 %all-to-all-done = bf16[32,32,576]{2,1,0:T(8,128)(2,1)S(1)} async-done(((bf16[32,32,576]{2,1,0:T(8,128)(2,1)}), bf16[32,32,576]{2,1,0:T(8,128)(2,1)S(1)}, u32[]{:S(2)}, u32[]{:S(2)}) %all-to-all-start) | async-done | bytes 1179680 | tf_op jit(solution)/shard_map/all_to_all | solution.py:496
  46.0 0.1 slice.93
  46.5 0.8 copy-done.6
  47.3 1.4 add_convert_fusion.qkv_ref
  48.7 7.3 %attend.1 = bf16[1024,192]{1,0:T(8,128)(2,1)S(1)} custom-call(s32[3]{0:T(128)S(1)} %copy-done.2, bf16[1024,576]{1,0:T(8,128)(2,1)S(1)} %add_convert_fusion.qkv_ref), custom_call_target="tpu_custom_call" | custom-call | flops 3221225472 | bytes 1572864 | tf_op jit(solution)/shard_map/attend/pallas_call | solution.py:332
  56.1 0.5 collective-permute-start.5
  56.7 1.5 collective-permute-start.3
  58.2 1.4 collective-permute-start.4
  59.6 0.1 convert_element_type.69.rows_ref
  59.8 0.1 reshape.75
  59.9 0.1 reshape.74.bias_ref
  60.0 2.4 %collective-permute-done.5 = bf16[256,192]{1,0:T(8,128)(2,1)S(1)} collective-permute-done((bf16[256,192]{1,0:T(8,128)(2,1)S(1)}, bf16[256,192]{1,0:T(8,128)(2,1)S(1)}, u32[]{:S(2)}, u32[]{:S(2)}) %collective-permute-start.5) | collective-permute-done | bytes 98336 | tf_op jit(solution)/shard_map/ppermute | solution.py:73
  62.4 3.4 %collective-permute-done.3 = bf16[256,192]{1,0:T(8,128)(2,1)S(1)} collective-permute-done((bf16[256,192]{1,0:T(8,128)(2,1)S(1)}, bf16[256,192]{1,0:T(8,128)(2,1)S(1)}, u32[]{:S(2)}, u32[]{:S(2)}) %collective-permute-start.3) | collective-permute-done | bytes 98336 | tf_op jit(solution)/shard_map/ppermute | solution.py:73
  65.8 1.0 pad_maximum_fusion.1.context_ref
  66.9 14.1 %all-gather.2.cloned.1.call-done.weights_ref = bf16[768,6912]{1,0:T(8,128)(2,1)} async-done(((bf16[24,6912]{1,0:T(8,128)(2,1)}), bf16[768,6912]{1,0:T(8,128)(2,1)}) %all-gather.2.cloned.1.call-update) | async-done | bytes 10616848 | tf_op jit(solution)/shard_map/all_gather | solution.py:495
  81.0 16.3 %middle.1 = (bf16[256,768]{1,0:T(8,128)(2,1)}, f32[256,768]{1,0:T(8,128)S(1)}, bf16[4,256,192]{2,1,0:T(8,128)(2,1)S(1)}, f32[8,768]{1,0:T(8,128)S(1)}, f32[4,768]{1,0:T(4,128)S(1)}, /*index=5*/bf16[768,6912]{1,0:T(8,128)(2,1)}) custom-call(s32[3]{0:T(128)S(1)} %copy-done.2, bf16[4,256,192]{2,1,0:T(8,128)(2,1)S(1)} %pad_maximum_fusion.1.context_ref, ...), custom_call_target="tpu_custom_call" | custom-call | flops 8153726976 | bytes 25165824 | tf_op jit(solution)/shard_map/middle/pallas_call | solution.py:431
  97.3 1.1 collective-permute-start.6
  98.5 1.2 collective-permute-start.7
  99.6 2.1 collective-permute-start.8
  101.7 0.1 pad_maximum_fusion.tokens_ref
  101.8 5.5 %collective-permute-done.6 = bf16[256,192]{1,0:T(8,128)(2,1)S(1)} collective-permute-done((bf16[256,192]{1,0:T(8,128)(2,1)S(1)}, bf16[256,192]{1,0:T(8,128)(2,1)S(1)}, u32[]{:S(2)}, u32[]{:S(2)}) %collective-permute-start.6) | collective-permute-done | bytes 98336 | tf_op jit(solution)/shard_map/ppermute | solution.py:73
  107.3 0.6 collective-permute-done.8
  108.0 18.1 %attend_back.1 = (bf16[1024,576]{1,0:T(8,128)(2,1)S(1)}, bf16[384,768]{1,0:T(8,128)(2,1)S(1)}, bf16[384,768]{1,0:T(8,128)(2,1)S(1)}) custom-call(s32[3]{0:T(128)S(1)} %copy-done.2, bf16[1024,576]{1,0:T(8,128)(2,1)S(1)} %copy-done.5, bf16[1024,192]{1,0:T(8,128)(2,1)S(1)} %pad_maximum_fusion.2.grad_ref, bf16[1024,768]{1,0:T(8,128)(2,1)S(1)} %pad_maximum_fusion.tokens_ref, ...), custom_call_target="tpu_custom_call" | custom-call | flops 8053063680 | bytes 2752512 | tf_op jit(solution)/shard_map/attend_back/pallas_call | solution.py:346
  126.2 1.4 convolution_convert_fusion
  127.7 1.0 fusion.2
  128.6 0.8 collective-permute-start.10
  129.5 3.4 %collective-permute-start.11 = (bf16[256,768]{1,0:T(8,128)(2,1)}, bf16[256,768]{1,0:T(8,128)(2,1)}, u32[]{:S(2)}, u32[]{:S(2)}) collective-permute-start(bf16[256,768]{1,0:T(8,128)(2,1)} %get-tuple-element.54), channel_id=1, source_target_pairs={{0,2},{1,3},{2,0},{3,1},{4,6},{5,7},{6,4},{7,5},{8,10},{9,11},{10,... | collective-permute-start | bytes 1179656 | tf_op jit(solution)/shard_map/ppermute | solution.py:73
  132.9 1.0 add_convert_fusion.1
  133.9 5.1 %all-to-all-start.1 = ((bf16[16,24,768]{2,1,0:T(8,128)(2,1)}), bf16[16,24,768]{2,1,0:T(8,128)(2,1)S(1)}, u32[]{:S(2)}, u32[]{:S(2)}) async-start(bf16[16,24,768]{2,1,0:T(8,128)(2,1)} %bitcast.19), calls=%async_computation.1 | async-start | bytes 1179648 | tf_op jit(solution)/shard_map/all_to_all | solution.py:552
  139.0 2.6 %collective-permute-done.10 = bf16[256,768]{1,0:T(8,128)(2,1)} collective-permute-done((bf16[256,768]{1,0:T(8,128)(2,1)}, bf16[256,768]{1,0:T(8,128)(2,1)}, u32[]{:S(2)}, u32[]{:S(2)}) %collective-permute-start.10) | collective-permute-done | bytes 393248 | tf_op jit(solution)/shard_map/ppermute | solution.py:73
  141.7 9.3 %collective-permute-done.11 = bf16[256,768]{1,0:T(8,128)(2,1)} collective-permute-done((bf16[256,768]{1,0:T(8,128)(2,1)}, bf16[256,768]{1,0:T(8,128)(2,1)}, u32[]{:S(2)}, u32[]{:S(2)}) %collective-permute-start.11) | collective-permute-done | bytes 393248 | tf_op jit(solution)/shard_map/ppermute | solution.py:73
  151.0 2.2 %fusion = bf16[1,256,768]{2,1,0:T(8,128)(2,1)} fusion(bf16[256,768]{1,0:T(8,128)(2,1)} %collective-permute-done.11, bf16[256,768]{1,0:T(8,128)(2,1)} %collective-permute-done.10, bf16[256,768]{1,0:T(8,128)(2,1)} %collective-permute-done.9, f32[256,768]{1,0:T(8,128)S(1)} %get-tuple-element.32, bf16[1024,768]{1,0:T(8,128)(2,1)S(1)} %convolution_convert_fusion), kind=kLoop, calls=%fused_computation.8 | loop fusion | flops 1769472 | bytes 2752512 | tf_op jit(solution)/shard_map/broadcast_in_dim | solution.py:550
  153.2 1.9 all-to-all-done.1
  155.2 2.0 collective-permute-start.13
  157.2 0.3 collective-permute-start.14
  157.5 2.5 %collective-permute-start.15 = (bf16[24,768]{1,0:T(8,128)(2,1)S(1)}, bf16[24,768]{1,0:T(8,128)(2,1)S(1)}, u32[]{:S(2)}, u32[]{:S(2)}) collective-permute-start(bf16[24,768]{1,0:T(8,128)(2,1)S(1)} %reduce_sum.21), channel_id=1, source_target_pairs={{0,1},{1,2},{2,3},{3,0},{4,5},{5,6},{6,7},{7,4},{8,9},{9,10},{10,1... | collective-permute-start | bytes 110600 | tf_op jit(solution)/shard_map/ppermute | solution.py:73
  160.0 0.5 collective-permute-done.13
  160.5 2.2 %collective-permute-done.14 = bf16[24,768]{1,0:T(8,128)(2,1)S(1)} collective-permute-done((bf16[24,768]{1,0:T(8,128)(2,1)S(1)}, bf16[24,768]{1,0:T(8,128)(2,1)S(1)}, u32[]{:S(2)}, u32[]{:S(2)}) %collective-permute-start.14) | collective-permute-done | bytes 36896 | tf_op jit(solution)/shard_map/ppermute | solution.py:73
  162.7 3.6 %reduce-scatter.2.cloned.1.call-done = bf16[96,6912]{1,0:T(8,128)(2,1)} async-done(((bf16[768,6912]{1,0:T(8,128)(2,1)}), bf16[96,6912]{1,0:T(8,128)(2,1)}) %reduce-scatter.2.cloned.1.call-update) | async-done | bytes 1327120 | tf_op jit(solution)/shard_map/reduce_scatter | solution.py:522
  166.2 1.2 constant_dynamic-slice_fusion.2
  167.5 1.6 collective-permute-start.16
  169.1 1.7 collective-permute-start.17
  170.9 1.9 collective-permute-start.18
  172.8 5.6 %collective-permute-done.16 = bf16[24,6912]{1,0:T(8,128)(2,1)S(1)} collective-permute-done((bf16[24,6912]{1,0:T(8,128)(2,1)S(1)}, bf16[24,6912]{1,0:T(8,128)(2,1)S(1)}, u32[]{:S(2)}, u32[]{:S(2)}) %collective-permute-start.16) | collective-permute-done | bytes 331808 | tf_op jit(solution)/shard_map/ppermute | solution.py:81
  178.3 6.1 %collective-permute-done.17 = bf16[24,6912]{1,0:T(8,128)(2,1)S(1)} collective-permute-done((bf16[24,6912]{1,0:T(8,128)(2,1)S(1)}, bf16[24,6912]{1,0:T(8,128)(2,1)S(1)}, u32[]{:S(2)}, u32[]{:S(2)}) %collective-permute-start.17) | collective-permute-done | bytes 331808 | tf_op jit(solution)/shard_map/ppermute | solution.py:81
  184.5 1.5 collective-permute-done.18
  186.0 1.1 add_convert_fusion.3.a_ref
  187.2 0.6 collective-permute-start.19
  187.8 1.5 collective-permute-start.20
  189.3 1.5 collective-permute-start.21
  190.8 0.2 reshape.71
  191.0 0.2 copy.51
  191.2 0.9 reshape.72
  192.2 0.6 reshape.73
  192.8 0.8 slice_reduce_fusion.3
  193.6 4.4 %collective-permute-done.19.b_ref = bf16[24,6912]{1,0:T(8,128)(2,1)S(1)} collective-permute-done((bf16[24,6912]{1,0:T(8,128)(2,1)S(1)}, bf16[24,6912]{1,0:T(8,128)(2,1)S(1)}, u32[]{:S(2)}, u32[]{:S(2)}) %collective-permute-start.19) | collective-permute-done | bytes 331808 | tf_op jit(solution)/shard_map/ppermute | solution.py:73
  198.0 5.9 %collective-permute-done.20.c_ref = bf16[24,6912]{1,0:T(8,128)(2,1)S(1)} collective-permute-done((bf16[24,6912]{1,0:T(8,128)(2,1)S(1)}, bf16[24,6912]{1,0:T(8,128)(2,1)S(1)}, u32[]{:S(2)}, u32[]{:S(2)}) %collective-permute-start.20) | collective-permute-done | bytes 331808 | tf_op jit(solution)/shard_map/ppermute | solution.py:73
  203.9 1.4 finish.1
  (65 shorter events, 1.3 us)
Async XLA Ops:
  7.2 73.8 %all-gather.2.cloned.1.call-start = ((), (), s32[]{:S(2)}) async-start(), calls=%async_computation.3 | async-start | bytes 10948608 | tf_op jit(solution)/shard_map/all_gather | solution.py:495
  12.6 8.6 %copy-start.1 = (bf16[1,256,768]{2,1,0:T(8,128)(2,1)S(1)}, bf16[1,256,768]{2,1,0:T(8,128)(2,1)}, u32[]{:S(2)}) copy-start(bf16[1,256,768]{2,1,0:T(8,128)(2,1)} %param.18) | copy-start | bytes 1179652
  12.7 33.2 %all-to-all-start = ((bf16[32,32,576]{2,1,0:T(8,128)(2,1)}), bf16[32,32,576]{2,1,0:T(8,128)(2,1)S(1)}, u32[]{:S(2)}, u32[]{:S(2)}) async-start(bf16[32,32,576]{2,1,0:T(8,128)(2,1)} %get-tuple-element.29), calls=%async_computation | async-start | bytes 2621440 | tf_op jit(solution)/shard_map/all_to_all | solution.py:496
  21.2 145.1 %reduce-scatter.2.cloned.1.call-start = ((), (), s32[]{:S(2)}) async-start(), calls=%async_computation.4 | async-start | bytes 11943936 | tf_op jit(solution)/shard_map/reduce_scatter | solution.py:522
  21.2 25.3 %collective-permute-start = (bf16[256,768]{1,0:T(8,128)(2,1)S(1)}, bf16[256,768]{1,0:T(8,128)(2,1)S(1)}, u32[]{:S(2)}, u32[]{:S(2)}) collective-permute-start(bf16[256,768]{1,0:T(8,128)(2,1)S(1)} %bitcast.44), channel_id=1, source_target_pairs={{0,3},{1,0},{2,1},{3,2},{4,7},{5,4},{6,5},{7,6},{8,11},{9,8},{10,9... | collective-permute-start | bytes 1179656 | tf_op jit(solution)/shard_map/ppermute | solution.py:73
  22.1 24.4 %collective-permute-start.1 = (bf16[256,768]{1,0:T(8,128)(2,1)S(1)}, bf16[256,768]{1,0:T(8,128)(2,1)S(1)}, u32[]{:S(2)}, u32[]{:S(2)}) collective-permute-start(bf16[256,768]{1,0:T(8,128)(2,1)S(1)} %bitcast.45), channel_id=1, source_target_pairs={{0,2},{1,3},{2,0},{3,1},{4,6},{5,7},{6,4},{7,5},{8,10},{9,11},{10,... | collective-permute-start | bytes 1179656 | tf_op jit(solution)/shard_map/ppermute | solution.py:73
  23.2 23.3 %collective-permute-start.2 = (bf16[256,768]{1,0:T(8,128)(2,1)S(1)}, bf16[256,768]{1,0:T(8,128)(2,1)S(1)}, u32[]{:S(2)}, u32[]{:S(2)}) collective-permute-start(bf16[256,768]{1,0:T(8,128)(2,1)S(1)} %bitcast.46), channel_id=1, source_target_pairs={{0,1},{1,2},{2,3},{3,0},{4,5},{5,6},{6,7},{7,4},{8,9},{9,10},{10,1... | collective-permute-start | bytes 1179656 | tf_op jit(solution)/shard_map/ppermute | solution.py:73
  46.3 1.0 copy-start.6
  46.5 2.2 %copy-start.8 = (bf16[256,768]{1,0:T(8,128)(2,1)}, bf16[256,768]{1,0:T(8,128)(2,1)S(1)}, u32[]{:S(2)}) copy-start(bf16[256,768]{1,0:T(8,128)(2,1)S(1)} %collective-permute-done.1) | copy-start | bytes 1179652
  46.5 2.2 %copy-start.10 = (bf16[256,768]{1,0:T(8,128)(2,1)}, bf16[256,768]{1,0:T(8,128)(2,1)S(1)}, u32[]{:S(2)}) copy-start(bf16[256,768]{1,0:T(8,128)(2,1)S(1)} %collective-permute-done.2) | copy-start | bytes 1179652
  47.3 1.4 copy-start.2
  48.7 7.3 %copy-start.4 = (bf16[1024,576]{1,0:T(8,128)(2,1)}, bf16[1024,576]{1,0:T(8,128)(2,1)S(1)}, u32[]{:S(2)}) copy-start(bf16[1024,576]{1,0:T(8,128)(2,1)S(1)} %add_convert_fusion.qkv_ref) | copy-start | bytes 3538948
  56.1 24.9 %copy-start.3 = (bf16[1,256,768]{2,1,0:T(8,128)(2,1)S(1)}, bf16[1,256,768]{2,1,0:T(8,128)(2,1)}, u32[]{:S(2)}) copy-start(bf16[1,256,768]{2,1,0:T(8,128)(2,1)} %param.33) | copy-start | bytes 1179652
  56.1 6.3 %collective-permute-start.5 = (bf16[256,192]{1,0:T(8,128)(2,1)S(1)}, bf16[256,192]{1,0:T(8,128)(2,1)S(1)}, u32[]{:S(2)}, u32[]{:S(2)}) collective-permute-start(bf16[256,192]{1,0:T(8,128)(2,1)S(1)} %get-tuple-element.64), channel_id=1, source_target_pairs={{0,1},{1,2},{2,3},{3,0},{4,5},{5,6},{6,7},{7,4},{8,9},{9,10},{10,1... | collective-permute-start | bytes 294920 | tf_op jit(solution)/shard_map/ppermute | solution.py:73
  56.7 9.2 %collective-permute-start.3 = (bf16[256,192]{1,0:T(8,128)(2,1)S(1)}, bf16[256,192]{1,0:T(8,128)(2,1)S(1)}, u32[]{:S(2)}, u32[]{:S(2)}) collective-permute-start(bf16[256,192]{1,0:T(8,128)(2,1)S(1)} %get-tuple-element.66), channel_id=1, source_target_pairs={{0,3},{1,0},{2,1},{3,2},{4,7},{5,4},{6,5},{7,6},{8,11},{9,8},{10,9... | collective-permute-start | bytes 294920 | tf_op jit(solution)/shard_map/ppermute | solution.py:73
  58.2 7.6 %collective-permute-start.4 = (bf16[256,192]{1,0:T(8,128)(2,1)S(1)}, bf16[256,192]{1,0:T(8,128)(2,1)}, u32[]{:S(2)}, u32[]{:S(2)}) collective-permute-start(bf16[256,192]{1,0:T(8,128)(2,1)S(1)} %get-tuple-element.65), channel_id=1, source_target_pairs={{0,2},{1,3},{2,0},{3,1},{4,6},{5,7},{6,4},{7,5},{8,10},{9,11},{10,... | collective-permute-start | bytes 294920 | tf_op jit(solution)/shard_map/ppermute | solution.py:73
  97.2 4.5 %copy-start.9 = (bf16[256,768]{1,0:T(8,128)(2,1)S(1)}, bf16[256,768]{1,0:T(8,128)(2,1)}, u32[]{:S(2)}) copy-start(bf16[256,768]{1,0:T(8,128)(2,1)} %copy-done.8) | copy-start | bytes 1179652
  97.2 4.5 %copy-start.11 = (bf16[256,768]{1,0:T(8,128)(2,1)S(1)}, bf16[256,768]{1,0:T(8,128)(2,1)}, u32[]{:S(2)}) copy-start(bf16[256,768]{1,0:T(8,128)(2,1)} %copy-done.10) | copy-start | bytes 1179652
  97.3 10.0 %collective-permute-start.6 = (bf16[256,192]{1,0:T(8,128)(2,1)S(1)}, bf16[256,192]{1,0:T(8,128)(2,1)S(1)}, u32[]{:S(2)}, u32[]{:S(2)}) collective-permute-start(bf16[256,192]{1,0:T(8,128)(2,1)S(1)} %get-tuple-element.62), channel_id=1, source_target_pairs={{0,3},{1,0},{2,1},{3,2},{4,7},{5,4},{6,5},{7,6},{8,11},{9,8},{10,9... | collective-permute-start | bytes 294920 | tf_op jit(solution)/shard_map/ppermute | solution.py:73
  98.5 8.8 %collective-permute-start.7 = (bf16[256,192]{1,0:T(8,128)(2,1)S(1)}, bf16[256,192]{1,0:T(8,128)(2,1)S(1)}, u32[]{:S(2)}, u32[]{:S(2)}) collective-permute-start(bf16[256,192]{1,0:T(8,128)(2,1)S(1)} %get-tuple-element.61), channel_id=1, source_target_pairs={{0,2},{1,3},{2,0},{3,1},{4,6},{5,7},{6,4},{7,5},{8,10},{9,11},{10,... | collective-permute-start | bytes 294920 | tf_op jit(solution)/shard_map/ppermute | solution.py:73
  99.6 8.3 %copy-start.5 = (bf16[1024,576]{1,0:T(8,128)(2,1)S(1)}, bf16[1024,576]{1,0:T(8,128)(2,1)}, u32[]{:S(2)}) copy-start(bf16[1024,576]{1,0:T(8,128)(2,1)} %copy-done.4) | copy-start | bytes 3538948
  99.6 8.2 %collective-permute-start.8 = (bf16[256,192]{1,0:T(8,128)(2,1)S(1)}, bf16[256,192]{1,0:T(8,128)(2,1)S(1)}, u32[]{:S(2)}, u32[]{:S(2)}) collective-permute-start(bf16[256,192]{1,0:T(8,128)(2,1)S(1)} %get-tuple-element.60), channel_id=1, source_target_pairs={{0,1},{1,2},{2,3},{3,0},{4,5},{5,6},{6,7},{7,4},{8,9},{9,10},{10,1... | collective-permute-start | bytes 294920 | tf_op jit(solution)/shard_map/ppermute | solution.py:73
  108.0 18.3 %copy-start.7 = (bf16[32,24,576]{2,1,0:T(8,128)(2,1)S(1)}, bf16[32,24,576]{2,1,0:T(8,128)(2,1)}, u32[]{:S(2)}) copy-start(bf16[32,24,576]{2,1,0:T(8,128)(2,1)} %copy-done.6) | copy-start | bytes 2654212
  126.1 6.8 %collective-permute-start.12 = (bf16[384,768]{1,0:T(8,128)(2,1)S(1)}, bf16[384,768]{1,0:T(8,128)(2,1)S(1)}, u32[]{:S(2)}, u32[]{:S(2)}) collective-permute-start(bf16[384,768]{1,0:T(8,128)(2,1)S(1)} %get-tuple-element.38), channel_id=1, source_target_pairs={{0,4},{4,0},{8,12},{12,8},{16,20},{20,16},{24,28},{28,24},{32,36},... | collective-permute-start | bytes 1769480 | tf_op jit(solution)/shard_map/ppermute | solution.py:77
  128.6 13.0 %collective-permute-start.10 = (bf16[256,768]{1,0:T(8,128)(2,1)}, bf16[256,768]{1,0:T(8,128)(2,1)}, u32[]{:S(2)}, u32[]{:S(2)}) collective-permute-start(bf16[256,768]{1,0:T(8,128)(2,1)} %get-tuple-element.55), channel_id=1, source_target_pairs={{0,3},{1,0},{2,1},{3,2},{4,7},{5,4},{6,5},{7,6},{8,11},{9,8},{10,9... | collective-permute-start | bytes 1179656 | tf_op jit(solution)/shard_map/ppermute | solution.py:73
  129.5 21.5 %collective-permute-start.11 = (bf16[256,768]{1,0:T(8,128)(2,1)}, bf16[256,768]{1,0:T(8,128)(2,1)}, u32[]{:S(2)}, u32[]{:S(2)}) collective-permute-start(bf16[256,768]{1,0:T(8,128)(2,1)} %get-tuple-element.54), channel_id=1, source_target_pairs={{0,2},{1,3},{2,0},{3,1},{4,6},{5,7},{6,4},{7,5},{8,10},{9,11},{10,... | collective-permute-start | bytes 1179656 | tf_op jit(solution)/shard_map/ppermute | solution.py:73
  132.9 18.1 %collective-permute-start.9 = (bf16[256,768]{1,0:T(8,128)(2,1)S(1)}, bf16[256,768]{1,0:T(8,128)(2,1)}, u32[]{:S(2)}, u32[]{:S(2)}) collective-permute-start(bf16[256,768]{1,0:T(8,128)(2,1)S(1)} %get-tuple-element.53), channel_id=1, source_target_pairs={{0,1},{1,2},{2,3},{3,0},{4,5},{5,6},{6,7},{7,4},{8,9},{9,10},{10,1... | collective-permute-start | bytes 1179656 | tf_op jit(solution)/shard_map/ppermute | solution.py:73
  133.9 21.3 %all-to-all-start.1 = ((bf16[16,24,768]{2,1,0:T(8,128)(2,1)}), bf16[16,24,768]{2,1,0:T(8,128)(2,1)S(1)}, u32[]{:S(2)}, u32[]{:S(2)}) async-start(bf16[16,24,768]{2,1,0:T(8,128)(2,1)} %bitcast.19), calls=%async_computation.1 | async-start | bytes 1179648 | tf_op jit(solution)/shard_map/all_to_all | solution.py:552
  155.2 5.2 %collective-permute-start.13 = (bf16[24,768]{1,0:T(8,128)(2,1)S(1)}, bf16[24,768]{1,0:T(8,128)(2,1)S(1)}, u32[]{:S(2)}, u32[]{:S(2)}) collective-permute-start(bf16[24,768]{1,0:T(8,128)(2,1)S(1)} %reduce_sum.21), channel_id=1, source_target_pairs={{0,3},{1,0},{2,1},{3,2},{4,7},{5,4},{6,5},{7,6},{8,11},{9,8},{10,9... | collective-permute-start | bytes 110600 | tf_op jit(solution)/shard_map/ppermute | solution.py:73
  157.2 5.5 %collective-permute-start.14 = (bf16[24,768]{1,0:T(8,128)(2,1)S(1)}, bf16[24,768]{1,0:T(8,128)(2,1)S(1)}, u32[]{:S(2)}, u32[]{:S(2)}) collective-permute-start(bf16[24,768]{1,0:T(8,128)(2,1)S(1)} %reduce_sum.21), channel_id=1, source_target_pairs={{0,2},{1,3},{2,0},{3,1},{4,6},{5,7},{6,4},{7,5},{8,10},{9,11},{10,... | collective-permute-start | bytes 110600 | tf_op jit(solution)/shard_map/ppermute | solution.py:73
  157.5 5.2 %collective-permute-start.15 = (bf16[24,768]{1,0:T(8,128)(2,1)S(1)}, bf16[24,768]{1,0:T(8,128)(2,1)S(1)}, u32[]{:S(2)}, u32[]{:S(2)}) collective-permute-start(bf16[24,768]{1,0:T(8,128)(2,1)S(1)} %reduce_sum.21), channel_id=1, source_target_pairs={{0,1},{1,2},{2,3},{3,0},{4,5},{5,6},{6,7},{7,4},{8,9},{9,10},{10,1... | collective-permute-start | bytes 110600 | tf_op jit(solution)/shard_map/ppermute | solution.py:73
  167.5 10.9 %collective-permute-start.16 = (bf16[24,6912]{1,0:T(8,128)(2,1)S(1)}, bf16[24,6912]{1,0:T(8,128)(2,1)S(1)}, u32[]{:S(2)}, u32[]{:S(2)}) collective-permute-start(bf16[24,6912]{1,0:T(8,128)(2,1)S(1)} %get-tuple-element.56), channel_id=1, source_target_pairs={{0,32},{4,36},{8,40},{12,44},{16,48},{20,52},{24,56},{28,60},{32,6... | collective-permute-start | bytes 995336 | tf_op jit(solution)/shard_map/ppermute | solution.py:81
  169.1 15.4 %collective-permute-start.17 = (bf16[24,6912]{1,0:T(8,128)(2,1)S(1)}, bf16[24,6912]{1,0:T(8,128)(2,1)S(1)}, u32[]{:S(2)}, u32[]{:S(2)}) collective-permute-start(bf16[24,6912]{1,0:T(8,128)(2,1)S(1)} %get-tuple-element.58), channel_id=1, source_target_pairs={{0,96},{4,100},{8,104},{12,108},{16,112},{20,116},{24,120},{28,124... | collective-permute-start | bytes 995336 | tf_op jit(solution)/shard_map/ppermute | solution.py:81
  170.9 15.2 %collective-permute-start.18 = (bf16[24,6912]{1,0:T(8,128)(2,1)S(1)}, bf16[24,6912]{1,0:T(8,128)(2,1)S(1)}, u32[]{:S(2)}, u32[]{:S(2)}) collective-permute-start(bf16[24,6912]{1,0:T(8,128)(2,1)S(1)} %get-tuple-element.57), channel_id=1, source_target_pairs={{0,64},{4,68},{8,72},{12,76},{16,80},{20,84},{24,88},{28,92},{32,9... | collective-permute-start | bytes 995336 | tf_op jit(solution)/shard_map/ppermute | solution.py:81
  187.2 16.7 %copy-start = (bf16[768,768]{1,0:T(8,128)(2,1)S(1)}, bf16[768,768]{1,0:T(8,128)(2,1)}, u32[]{:S(2)}) copy-start(bf16[768,768]{1,0:T(8,128)(2,1)} %constant.75.clone.rest_4_.order_ref) | copy-start | bytes 3538948
  187.2 10.8 %collective-permute-start.19 = (bf16[24,6912]{1,0:T(8,128)(2,1)S(1)}, bf16[24,6912]{1,0:T(8,128)(2,1)S(1)}, u32[]{:S(2)}, u32[]{:S(2)}) collective-permute-start(bf16[24,6912]{1,0:T(8,128)(2,1)S(1)} %add_convert_fusion.3.a_ref), channel_id=1, source_target_pairs={{0,1},{1,2},{2,3},{3,0},{4,5},{5,6},{6,7},{7,4},{8,9},{9,10},{10,1... | collective-permute-start | bytes 995336 | tf_op jit(solution)/shard_map/ppermute | solution.py:73
  187.8 16.1 %collective-permute-start.20 = (bf16[24,6912]{1,0:T(8,128)(2,1)S(1)}, bf16[24,6912]{1,0:T(8,128)(2,1)S(1)}, u32[]{:S(2)}, u32[]{:S(2)}) collective-permute-start(bf16[24,6912]{1,0:T(8,128)(2,1)S(1)} %add_convert_fusion.3.a_ref), channel_id=1, source_target_pairs={{0,3},{1,0},{2,1},{3,2},{4,7},{5,4},{6,5},{7,6},{8,11},{9,8},{10,9... | collective-permute-start | bytes 995336 | tf_op jit(solution)/shard_map/ppermute | solution.py:73
  189.3 14.6 %collective-permute-start.21 = (bf16[24,6912]{1,0:T(8,128)(2,1)S(1)}, bf16[24,6912]{1,0:T(8,128)(2,1)S(1)}, u32[]{:S(2)}, u32[]{:S(2)}) collective-permute-start(bf16[24,6912]{1,0:T(8,128)(2,1)S(1)} %add_convert_fusion.3.a_ref), channel_id=1, source_target_pairs={{0,2},{1,3},{2,0},{3,1},{4,6},{5,7},{6,4},{7,5},{8,10},{9,11},{10,... | collective-permute-start | bytes 995336 | tf_op jit(solution)/shard_map/ppermute | solution.py:73
Sparse Core Ops, SparseCore 0:
  12.8 68.1 all-gather.1
  97.4 68.8 reduce-scatter.1

commit v4 on v3

--- a/solution.py
+++ b/solution.py
@@ -188,19 +188,21 @@
     return matrix
 
 
-def pack_kernel(info_ref, *rest):
-    sources, (packed_ref, early_ref), held = rest[:14], rest[14:16], rest[16:30]
-    rows_ref, sems = rest[30:]
-    fetches = [
+def fetch(sources, held, sems):
+    copies = [
         pltpu.make_async_copy(source, target, sems.at[at])
         for at, (source, target) in enumerate(zip(sources, held))
     ]
-    for fetch in fetches:
-        fetch.start()
-    qkv_ref, context_ref, expand_ref, reduce_ref, order_ref = held[:5]
-    vector_refs = held[5:]
-    for fetch in fetches:
-        fetch.wait()
+    for copy in copies:
+        copy.start()
+    for copy in copies:
+        copy.wait()
+
+
+def pack_kernel(*refs):
+    packed_ref, held, sems = refs[4], refs[5:9], refs[9]
+    fetch(refs[:4], held, sems)
+    context_ref, expand_ref, reduce_ref, order_ref = held
     reduce_rows = reduce_ref[...].astype(F32)
     for part in range(4):
         packed_ref[:, part * D : (part + 1) * D] = reduce_rows[part * 24 : (part + 1) * 24].astype(BF16)
@@ -215,6 +217,11 @@
         ).astype(BF16)
     packed_ref[:, 2 * FF :] = context_ref[...]
 
+
+def early_kernel(info_ref, after_ref, *refs):
+    early_ref, held, (rows_ref, sems) = refs[10], refs[11:21], refs[21:]
+    fetch(refs[:10], held, sems)
+    qkv_ref, vector_refs = held[0], held[1:]
     rows_ref[...] = jnp.zeros_like(rows_ref)
     for row in range(8):
         rows_ref[row : row + 1, :24] = vector_refs[row][...].astype(F32).reshape(1, 24)
@@ -365,35 +372,52 @@
     )(info, qkv, grads, tokens, row_sums, bias_sums)
 
 
-def pack(info, qkv_weight, context_weight, expand_weight, reduce_weight, vectors):
-    operands = (
-        qkv_weight, context_weight, expand_weight, reduce_weight,
-        jnp.asarray(reorder_matrix(), BF16), *vectors,
-    )
+HBM = pl.BlockSpec(memory_space=pltpu.HBM)
+WIDE = pltpu.CompilerParams(vmem_limit_bytes=60 * 1024 * 1024)
+
+
+def pack(context_weight, expand_weight, reduce_weight):
+    operands = (context_weight, expand_weight, reduce_weight, jnp.asarray(reorder_matrix(), BF16))
     return pl.pallas_call(
         pack_kernel,
-        out_shape=(
-            jax.ShapeDtypeStruct((24, PACKED), BF16),
-            jax.ShapeDtypeStruct((32, 32, 3 * HW), BF16),
-        ),
-        in_specs=[SMEM] + [pl.BlockSpec(memory_space=pltpu.HBM)] * len(operands),
-        out_specs=(VMEM, VMEM),
+        out_shape=jax.ShapeDtypeStruct((24, PACKED), BF16),
+        in_specs=[HBM] * len(operands),
+        out_specs=VMEM,
+        scratch_shapes=[pltpu.VMEM(operand.shape, BF16) for operand in operands]
+        + [pltpu.SemaphoreType.DMA((len(operands),))],
+        compiler_params=WIDE,
+        name="pack",
+    )(*operands)
+
+
+def early_pack(info, after, qkv_weight, vectors):
+    operands = (qkv_weight, *vectors)
+    return pl.pallas_call(
+        early_kernel,
+        out_shape=jax.ShapeDtypeStruct((32, 32, 3 * HW), BF16),
+        in_specs=[SMEM] + [HBM] * (1 + len(operands)),
+        out_specs=VMEM,
         scratch_shapes=[pltpu.VMEM(operand.shape, BF16) for operand in operands]
         + [pltpu.VMEM((8, 3 * HW), F32), pltpu.SemaphoreType.DMA((len(operands),))],
-        compiler_params=pltpu.CompilerParams(vmem_limit_bytes=60 * 1024 * 1024),
-        name="pack",
-    )(info, *operands)
-
-
-def finish_kernel(a_ref, b_ref, c_ref, d_ref, order_ref, reduce_ref, expand_ref, context_ref):
+        compiler_params=WIDE,
+        name="early_pack",
+    )(info, after, *operands)
+
+
+def finish_reduce_kernel(a_ref, b_ref, c_ref, d_ref, reduce_ref):
+    for part in range(4):
+        cols = slice(part * D, (part + 1) * D)
+        parts = [ref[:, cols].astype(F32) for ref in (a_ref, b_ref, c_ref, d_ref)]
+        reduce_ref[part * 24 : (part + 1) * 24, :] = (parts[0] + parts[1]) + (parts[2] + parts[3])
+
+
+def finish_kernel(a_ref, b_ref, c_ref, d_ref, order_ref, expand_ref, context_ref):
     def total(start, width):
         parts = [ref[:, start : start + width].astype(F32) for ref in (a_ref, b_ref, c_ref, d_ref)]
         return (parts[0] + parts[1]) + (parts[2] + parts[3])
 
-    for part in range(4):
-        reduce_ref[part * 24 : (part + 1) * 24, :] = total(part * D, D)
-    context_ref[...] = total(2 * FF, D)
-    moved = [total(FF + part * D, D) for part in range(4)]
+    context_ref[...] = total(FF, D)
+    moved = [total(part * D, D) for part in range(4)]
     left = jnp.concatenate(
         [
             jnp.concatenate([values[:, q * HW : (q + 1) * HW] for values in moved], axis=1)
@@ -411,16 +435,26 @@
         expand_ref[:, q * D : (q + 1) * D] = result[q * 24 : (q + 1) * 24]
 
 
+def finish_reduce(pieces):
+    return pl.pallas_call(
+        finish_reduce_kernel,
+        out_shape=jax.ShapeDtypeStruct((96, D), F32),
+        in_specs=[VMEM] * 4,
+        out_specs=VMEM,
+        compiler_params=PARAMS,
+        name="finish_reduce",
+    )(*pieces)
+
+
 def finish(pieces):
     return pl.pallas_call(
         finish_kernel,
         out_shape=(
-            jax.ShapeDtypeStruct((96, D), F32),
             jax.ShapeDtypeStruct((24, FF), F32),
             jax.ShapeDtypeStruct((24, D), F32),
         ),
         in_specs=[VMEM] * 5,
-        out_specs=(VMEM,) * 3,
+        out_specs=(VMEM,) * 2,
         compiler_params=PARAMS,
         name="finish",
     )(*pieces, jnp.asarray(reorder_matrix(), BF16))
@@ -487,8 +521,9 @@
 
     core = lax.axis_index("fsdp") & 1
     info = jnp.stack([x_at.astype(jnp.int32), lengths[0], core.astype(jnp.int32)])
-    packed, early = pack(
-        info, qkv_weight, context_weight, expand_weight, reduce_weight,
+    packed = pack(context_weight, expand_weight, reduce_weight)
+    early = early_pack(
+        info, packed, qkv_weight,
         (query_bias, value_bias, context_bias, first_gain, first_shift, reduce_bias,
          second_gain, second_shift, expand_bias),
     )
@@ -528,13 +563,19 @@
     )
     z_at = lax.axis_index("fsdp") // 8
 
-    def rows_of(step):
-        return lax.dynamic_slice_in_dim(packed_grads, (z_at + step) % 4 * 24, 24, axis=0)
-
-    z_sum = rows_of(0).astype(F32)
-    for step in ORDER:
-        z_sum = z_sum + to_z(rows_of(step), step).astype(F32)
-    packed_grads = z_sum.astype(BF16)
+    def spread(start, width):
+        rows = [
+            lax.dynamic_slice(packed_grads, ((z_at + step) % 4 * 24, start), (24, width))
+            for step in range(4)
+        ]
+        total = rows[0].astype(F32)
+        for step in ORDER:
+            total = total + to_z(rows[step], step).astype(F32)
+        total = total.astype(BF16)
+        return [total] + [to_x(total, step) for step in ORDER]
+
+    reduce_parts = spread(0, FF)
+    other_parts = spread(FF, FF + D)
     blocks = [context_grad[0]] + [None] * 3
     for step in ORDER:
         blocks[SP - step] = to_x(context_grad[step], step)
@@ -564,9 +605,8 @@
     eight = jnp.sum(second_round[:, :, :12], axis=0).T
     expand_bias_out = eight[8:].reshape(96)
 
-    reduce_out, expand_out, context_out = finish(
-        [packed_grads] + [to_x(packed_grads, step) for step in ORDER]
-    )
+    reduce_out = finish_reduce(reduce_parts)
+    expand_out, context_out = finish(other_parts)
 
     return (
         hidden_out[None],

time: 214 us -> 207 us (0.967)
  waiting for transfers between devices: 90.2 us -> 73.2 us
  starting transfers between devices: 43.5 us -> 50.7 us
    ppermute x3 -> x6, waiting for transfers between devices: 13.3 us -> 4.01 us  [to_z(): lax.ppermute(values, 'fsdp', [(i, (i + 8 * step) % 32) for i in range(32)])]
    ppermute x18 -> x21, waiting for transfers between devices: 36.8 us -> 30.5 us  [to_x(): return lax.ppermute(values, 'sp', [(i, (i + step) % SP) for i in range(SP)])]
    ppermute x3 -> x6, starting transfers between devices: 5.26 us -> 8.98 us  [to_z(): lax.ppermute(values, 'fsdp', [(i, (i + 8 * step) % 32) for i in range(32)])]
    ppermute x18 -> x21, starting transfers between devices: 24.5 us -> 28.1 us  [to_x(): return lax.ppermute(values, 'sp', [(i, (i + step) % SP) for i in range(SP)])]
    all_gather x1, waiting for transfers between devices: 14.1 us -> 11.8 us  [per_device(): packed = lax.all_gather(packed, 'fsdp', axis=0, tiled=True)]
    pallas_call x2 -> x4, Pallas kernels: 5.6 us -> 7.73 us  [the longest x1 3.01 us: early_pack(): pl.pallas_call(early_kernel, out_shape=jax.ShapeDtypeStruct((32, 32, 3 *...]
  transfers between devices with their start and end apart: 26 -> 32, of which waited for: 17 -> 17; matrix products, arithmetic and copies ran while one was open for 6% -> 8% of each run, Pallas kernels for 12% -> 14%
where the time goes in v4:
time: 207 us; the launch traced here: 206 us
  waiting for transfers between devices  73.2 us (35%)
  starting transfers between devices  50.7 us (24%)
  Pallas kernels  49.3 us (24%)
  between operations  15.2 us (7%)
  local copies, waits for them, and re-layouts  7.72 us (4%)
  other arithmetic  7.22 us (3%)
  matrix products  2.81 us (1%)
    ppermute x21, waiting for transfers between devices, to_x(): return lax.ppermute(values, 'sp', [(i, (i + step) % SP) for i in range(SP)])  30.5 us
    ppermute x21, starting transfers between devices, to_x(): return lax.ppermute(values, 'sp', [(i, (i + step) % SP) for i in range(SP)])  28.1 us
    all_to_all x1, waiting for transfers between devices, per_device(): lax.all_to_all(early, 'fsdp', split_axis=0, concat_axis=0, tiled=True)  21.4 us
    pallas_call x1, Pallas kernels, attend_back(): pl.pallas_call(attend_back_kernel, out_shape=(jax.ShapeDtypeStruct((LEN,...  18.1 us
    pallas_call x1, Pallas kernels, middle(): pl.pallas_call(middle_kernel, out_shape=(jax.ShapeDtypeStruct(tall, BF16)...  16.1 us
    all_gather x1, waiting for transfers between devices, per_device(): packed = lax.all_gather(packed, 'fsdp', axis=0, tiled=True)  11.8 us
    ppermute x6, starting transfers between devices, to_z(): lax.ppermute(values, 'fsdp', [(i, (i + 8 * step) % 32) for i in range(32)])  8.98 us
    all_to_all x1, starting transfers between devices, per_device(): lax.all_to_all(early, 'fsdp', split_axis=0, concat_axis=0, tiled=True)  8.48 us
  transfers between devices with their start and end apart: 32, of which 17 were waited for; matrix products, arithmetic and copies ran while one was open for 8% of the time, Pallas kernels for 14%

profile of v4, /device:TPU:6, one launch (start us, length us, event | category | flops | bytes accessed | tf_op | source)
XLA Modules:
  0.0 206.2 jit_solution(1390660332840916882)
XLA Ops:
  7.2 2.6 %pack.1.after_ref = bf16[24,6912]{1,0:T(8,128)(2,1)} custom-call(bf16[24,768]{1,0:T(8,128)(2,1)} %refs_0_.2, bf16[24,3072]{1,0:T(8,128)(2,1)} %refs_1_.2, bf16[96,768]{1,0:T(8,128)(2,1)} %refs_2_.2, bf16[768,768]{1,0:T(8,128)(2,1)} %constant.85.clone.refs_3_.order_ref), custom_call_target="tpu_custom_call" | custom-call | tf_op jit(solution)/shard_map/pack/pallas_call | solution.py:381
  10.5 0.6 pad_add_fusion.info_ref
  11.1 3.0 %early_pack.1 = bf16[32,32,576]{2,1,0:T(8,128)(2,1)} custom-call(s32[3]{0:T(128)} %pad_add_fusion.info_ref, bf16[24,6912]{1,0:T(8,128)(2,1)} %pack.1.after_ref, bf16[24,2304]{1,0:T(8,128)(2,1)} %refs_0_.3, bf16[24]{0:T(256)(128)(2,1)} %refs_1_.3, bf16[24]{0:T(256)(128)(2,1)} %refs_2_.3, bf16[24]{0:T(256)(128)(2,1)} %refs_3_.2, bf16[24]{0:T(256)(128)(2,1)} %refs_4_.1, ...), custom_call_target="tpu_custom_call" | custom-call | tf_op jit(solution)/shard_map/early_pack/pallas_call | solution.py:395
  14.2 8.5 %all-to-all-start = ((bf16[32,32,576]{2,1,0:T(8,128)(2,1)}), bf16[32,32,576]{2,1,0:T(8,128)(2,1)S(1)}, u32[]{:S(2)}, u32[]{:S(2)}) async-start(bf16[32,32,576]{2,1,0:T(8,128)(2,1)} %early_pack.1), calls=%async_computation | async-start | bytes 2621440 | tf_op jit(solution)/shard_map/all_to_all | solution.py:531
  22.7 0.9 collective-permute-start
  23.6 1.1 collective-permute-start.1
  24.7 2.1 %collective-permute-start.2 = (bf16[256,768]{1,0:T(8,128)(2,1)S(1)}, bf16[256,768]{1,0:T(8,128)(2,1)S(1)}, u32[]{:S(2)}, u32[]{:S(2)}) collective-permute-start(bf16[256,768]{1,0:T(8,128)(2,1)S(1)} %bitcast.46), channel_id=1, source_target_pairs={{0,1},{1,2},{2,3},{3,0},{4,5},{5,6},{6,7},{7,4},{8,9},{9,10},{10,1... | collective-permute-start | bytes 1179656 | tf_op jit(solution)/shard_map/ppermute | solution.py:73
  26.8 21.4 %all-to-all-done = bf16[32,32,576]{2,1,0:T(8,128)(2,1)S(1)} async-done(((bf16[32,32,576]{2,1,0:T(8,128)(2,1)}), bf16[32,32,576]{2,1,0:T(8,128)(2,1)S(1)}, u32[]{:S(2)}, u32[]{:S(2)}) %all-to-all-start) | async-done | bytes 1179680 | tf_op jit(solution)/shard_map/all_to_all | solution.py:531
  48.8 0.7 copy-done.6
  49.6 1.4 add_convert_fusion.qkv_ref
  51.0 7.3 %attend.1 = bf16[1024,192]{1,0:T(8,128)(2,1)S(1)} custom-call(s32[3]{0:T(128)S(1)} %copy-done.2, bf16[1024,576]{1,0:T(8,128)(2,1)S(1)} %add_convert_fusion.qkv_ref), custom_call_target="tpu_custom_call" | custom-call | flops 3221225472 | bytes 1572864 | tf_op jit(solution)/shard_map/attend/pallas_call | solution.py:339
  58.4 0.6 collective-permute-start.5
  59.0 1.5 collective-permute-start.3
  60.5 1.4 collective-permute-start.4
  62.3 2.4 %collective-permute-done.5 = bf16[256,192]{1,0:T(8,128)(2,1)S(1)} collective-permute-done((bf16[256,192]{1,0:T(8,128)(2,1)S(1)}, bf16[256,192]{1,0:T(8,128)(2,1)S(1)}, u32[]{:S(2)}, u32[]{:S(2)}) %collective-permute-start.5) | collective-permute-done | bytes 98336 | tf_op jit(solution)/shard_map/ppermute | solution.py:73
  64.7 3.4 %collective-permute-done.3 = bf16[256,192]{1,0:T(8,128)(2,1)S(1)} collective-permute-done((bf16[256,192]{1,0:T(8,128)(2,1)S(1)}, bf16[256,192]{1,0:T(8,128)(2,1)S(1)}, u32[]{:S(2)}, u32[]{:S(2)}) %collective-permute-start.3) | collective-permute-done | bytes 98336 | tf_op jit(solution)/shard_map/ppermute | solution.py:73
  68.1 1.0 pad_maximum_fusion.1.context_ref
  69.1 11.8 %all-gather.2.cloned.1.call-done.weights_ref = bf16[768,6912]{1,0:T(8,128)(2,1)} async-done(((bf16[24,6912]{1,0:T(8,128)(2,1)}), bf16[768,6912]{1,0:T(8,128)(2,1)}) %all-gather.2.cloned.1.call-update) | async-done | bytes 10616848 | tf_op jit(solution)/shard_map/all_gather | solution.py:530
  80.9 16.1 %middle.1 = (bf16[256,768]{1,0:T(8,128)(2,1)}, f32[256,768]{1,0:T(8,128)S(1)}, bf16[4,256,192]{2,1,0:T(8,128)(2,1)S(1)}, f32[8,768]{1,0:T(8,128)S(1)}, f32[4,768]{1,0:T(4,128)S(1)}, /*index=5*/bf16[768,6912]{1,0:T(8,128)(2,1)}) custom-call(s32[3]{0:T(128)S(1)} %copy-done.2, bf16[4,256,192]{2,1,0:T(8,128)(2,1)S(1)} %pad_maximum_fusion.1.context_ref, ...), custom_call_target="tpu_custom_call" | custom-call | flops 8153726976 | bytes 25165824 | tf_op jit(solution)/shard_map/middle/pallas_call | solution.py:465
  97.2 1.1 collective-permute-start.6
  98.3 1.2 collective-permute-start.7
  99.4 2.1 %collective-permute-start.8 = (bf16[256,192]{1,0:T(8,128)(2,1)S(1)}, bf16[256,192]{1,0:T(8,128)(2,1)S(1)}, u32[]{:S(2)}, u32[]{:S(2)}) collective-permute-start(bf16[256,192]{1,0:T(8,128)(2,1)S(1)} %get-tuple-element.57), channel_id=1, source_target_pairs={{0,1},{1,2},{2,3},{3,0},{4,5},{5,6},{6,7},{7,4},{8,9},{9,10},{10,1... | collective-permute-start | bytes 294920 | tf_op jit(solution)/shard_map/ppermute | solution.py:73
  101.6 5.5 %collective-permute-done.6 = bf16[256,192]{1,0:T(8,128)(2,1)S(1)} collective-permute-done((bf16[256,192]{1,0:T(8,128)(2,1)S(1)}, bf16[256,192]{1,0:T(8,128)(2,1)S(1)}, u32[]{:S(2)}, u32[]{:S(2)}) %collective-permute-start.6) | collective-permute-done | bytes 98336 | tf_op jit(solution)/shard_map/ppermute | solution.py:73
  107.1 0.6 collective-permute-done.8
  107.8 18.1 %attend_back.1 = (bf16[1024,576]{1,0:T(8,128)(2,1)S(1)}, bf16[384,768]{1,0:T(8,128)(2,1)S(1)}, bf16[384,768]{1,0:T(8,128)(2,1)S(1)}) custom-call(s32[3]{0:T(128)S(1)} %copy-done.2, bf16[1024,576]{1,0:T(8,128)(2,1)S(1)} %copy-done.5, bf16[1024,192]{1,0:T(8,128)(2,1)S(1)} %pad_maximum_fusion.2.grad_ref, bf16[1024,768]{1,0:T(8,128)(2,1)S(1)} %pad_maximum_fusion.tokens_ref, ...), custom_call_target="tpu_custom_call" | custom-call | flops 8053063680 | bytes 2752512 | tf_op jit(solution)/shard_map/attend_back/pallas_call | solution.py:353
  126.1 1.4 convolution_convert_fusion
  127.5 1.0 fusion.2
  128.5 0.8 collective-permute-start.10
  129.3 3.4 %collective-permute-start.11 = (bf16[256,768]{1,0:T(8,128)(2,1)}, bf16[256,768]{1,0:T(8,128)(2,1)}, u32[]{:S(2)}, u32[]{:S(2)}) collective-permute-start(bf16[256,768]{1,0:T(8,128)(2,1)} %get-tuple-element.48), channel_id=1, source_target_pairs={{0,2},{1,3},{2,0},{3,1},{4,6},{5,7},{6,4},{7,5},{8,10},{9,11},{10,... | collective-permute-start | bytes 1179656 | tf_op jit(solution)/shard_map/ppermute | solution.py:73
  132.7 1.0 add_convert_fusion.1
  133.7 5.1 %all-to-all-start.1 = ((bf16[16,24,768]{2,1,0:T(8,128)(2,1)}), bf16[16,24,768]{2,1,0:T(8,128)(2,1)S(1)}, u32[]{:S(2)}, u32[]{:S(2)}) async-start(bf16[16,24,768]{2,1,0:T(8,128)(2,1)} %bitcast.19), calls=%async_computation.1 | async-start | bytes 1179648 | tf_op jit(solution)/shard_map/all_to_all | solution.py:593
  138.9 2.6 %collective-permute-done.10 = bf16[256,768]{1,0:T(8,128)(2,1)} collective-permute-done((bf16[256,768]{1,0:T(8,128)(2,1)}, bf16[256,768]{1,0:T(8,128)(2,1)}, u32[]{:S(2)}, u32[]{:S(2)}) %collective-permute-start.10) | collective-permute-done | bytes 393248 | tf_op jit(solution)/shard_map/ppermute | solution.py:73
  141.5 9.3 %collective-permute-done.11 = bf16[256,768]{1,0:T(8,128)(2,1)} collective-permute-done((bf16[256,768]{1,0:T(8,128)(2,1)}, bf16[256,768]{1,0:T(8,128)(2,1)}, u32[]{:S(2)}, u32[]{:S(2)}) %collective-permute-start.11) | collective-permute-done | bytes 393248 | tf_op jit(solution)/shard_map/ppermute | solution.py:73
  150.8 2.2 %fusion = bf16[1,256,768]{2,1,0:T(8,128)(2,1)} fusion(bf16[256,768]{1,0:T(8,128)(2,1)} %collective-permute-done.11, bf16[256,768]{1,0:T(8,128)(2,1)} %collective-permute-done.10, bf16[256,768]{1,0:T(8,128)(2,1)} %collective-permute-done.9, f32[256,768]{1,0:T(8,128)S(1)} %get-tuple-element.27, bf16[1024,768]{1,0:T(8,128)(2,1)S(1)} %convolution_convert_fusion), kind=kLoop, calls=%fused_computation.7 | loop fusion | flops 1769472 | bytes 2752512 | tf_op jit(solution)/shard_map/broadcast_in_dim | solution.py:591
  153.0 1.9 all-to-all-done.1
  155.1 2.0 collective-permute-start.13
  157.3 2.5 %collective-permute-start.15 = (bf16[24,768]{1,0:T(8,128)(2,1)S(1)}, bf16[24,768]{1,0:T(8,128)(2,1)S(1)}, u32[]{:S(2)}, u32[]{:S(2)}) collective-permute-start(bf16[24,768]{1,0:T(8,128)(2,1)S(1)} %reduce_sum.21), channel_id=1, source_target_pairs={{0,1},{1,2},{2,3},{3,0},{4,5},{5,6},{6,7},{7,4},{8,9},{9,10},{10,1... | collective-permute-start | bytes 110600 | tf_op jit(solution)/shard_map/ppermute | solution.py:73
  159.8 0.5 collective-permute-done.13
  160.3 2.2 %collective-permute-done.14 = bf16[24,768]{1,0:T(8,128)(2,1)S(1)} collective-permute-done((bf16[24,768]{1,0:T(8,128)(2,1)S(1)}, bf16[24,768]{1,0:T(8,128)(2,1)S(1)}, u32[]{:S(2)}, u32[]{:S(2)}) %collective-permute-start.14) | collective-permute-done | bytes 36896 | tf_op jit(solution)/shard_map/ppermute | solution.py:73
  162.6 3.5 %reduce-scatter.2.cloned.1.call-done = bf16[96,6912]{1,0:T(8,128)(2,1)} async-done(((bf16[768,6912]{1,0:T(8,128)(2,1)}), bf16[96,6912]{1,0:T(8,128)(2,1)}) %reduce-scatter.2.cloned.1.call-update) | async-done | bytes 1327120 | tf_op jit(solution)/shard_map/reduce_scatter | solution.py:557
  166.1 1.1 constant_dynamic-slice_fusion.2
  167.2 1.6 collective-permute-start.22
  168.8 1.7 collective-permute-start.23
  170.5 1.9 collective-permute-start.24
  172.4 1.1 constant_dynamic-slice_fusion.7
  173.6 0.7 collective-permute-start.16
  174.3 2.6 %collective-permute-start.17 = (bf16[24,3840]{1,0:T(8,128)(2,1)S(1)}, bf16[24,3840]{1,0:T(8,128)(2,1)S(1)}, u32[]{:S(2)}, u32[]{:S(2)}) collective-permute-start(bf16[24,3840]{1,0:T(8,128)(2,1)S(1)} %get-tuple-element.55), channel_id=1, source_target_pairs={{0,96},{4,100},{8,104},{12,108},{16,112},{20,116},{24,120},{28,124... | collective-permute-start | bytes 552968 | tf_op jit(solution)/shard_map/ppermute | solution.py:81
  177.3 1.9 collective-permute-done.24
  179.2 1.0 add_convert_fusion.4.a_ref
  180.2 0.6 collective-permute-start.25
  180.8 1.5 collective-permute-start.26
  182.3 0.7 collective-permute-done.16
  183.0 1.4 collective-permute-start.27
  184.4 1.4 collective-permute-done.18
  185.8 1.0 add_convert_fusion.3.a_ref
  186.9 0.7 collective-permute-start.19
  187.6 1.4 collective-permute-start.20
  189.0 1.5 collective-permute-start.21
  190.8 0.9 reshape.72
  191.9 0.6 reshape.73
  192.5 0.8 slice_reduce_fusion.3
  193.3 0.8 finish_reduce.1
  194.4 3.6 %collective-permute-done.20.c_ref = bf16[24,3840]{1,0:T(8,128)(2,1)S(1)} collective-permute-done((bf16[24,3840]{1,0:T(8,128)(2,1)S(1)}, bf16[24,3840]{1,0:T(8,128)(2,1)S(1)}, u32[]{:S(2)}, u32[]{:S(2)}) %collective-permute-start.20) | collective-permute-done | bytes 184352 | tf_op jit(solution)/shard_map/ppermute | solution.py:73
  198.1 1.3 finish.1
  (81 shorter events, 3.2 us)
Async XLA Ops:
  7.2 73.7 %all-gather.2.cloned.1.call-start = ((), (), s32[]{:S(2)}) async-start(), calls=%async_computation.3 | async-start | bytes 10948608 | tf_op jit(solution)/shard_map/all_gather | solution.py:530
  14.1 8.5 %copy-start.1 = (bf16[1,256,768]{2,1,0:T(8,128)(2,1)S(1)}, bf16[1,256,768]{2,1,0:T(8,128)(2,1)}, u32[]{:S(2)}) copy-start(bf16[1,256,768]{2,1,0:T(8,128)(2,1)} %param.18) | copy-start | bytes 1179652
  14.2 34.1 %all-to-all-start = ((bf16[32,32,576]{2,1,0:T(8,128)(2,1)}), bf16[32,32,576]{2,1,0:T(8,128)(2,1)S(1)}, u32[]{:S(2)}, u32[]{:S(2)}) async-start(bf16[32,32,576]{2,1,0:T(8,128)(2,1)} %early_pack.1), calls=%async_computation | async-start | bytes 2621440 | tf_op jit(solution)/shard_map/all_to_all | solution.py:531
  22.6 143.5 %reduce-scatter.2.cloned.1.call-start = ((), (), s32[]{:S(2)}) async-start(), calls=%async_computation.4 | async-start | bytes 11943936 | tf_op jit(solution)/shard_map/reduce_scatter | solution.py:557
  22.7 26.1 %collective-permute-start = (bf16[256,768]{1,0:T(8,128)(2,1)S(1)}, bf16[256,768]{1,0:T(8,128)(2,1)S(1)}, u32[]{:S(2)}, u32[]{:S(2)}) collective-permute-start(bf16[256,768]{1,0:T(8,128)(2,1)S(1)} %bitcast.44), channel_id=1, source_target_pairs={{0,3},{1,0},{2,1},{3,2},{4,7},{5,4},{6,5},{7,6},{8,11},{9,8},{10,9... | collective-permute-start | bytes 1179656 | tf_op jit(solution)/shard_map/ppermute | solution.py:73
  23.6 25.2 %collective-permute-start.1 = (bf16[256,768]{1,0:T(8,128)(2,1)S(1)}, bf16[256,768]{1,0:T(8,128)(2,1)S(1)}, u32[]{:S(2)}, u32[]{:S(2)}) collective-permute-start(bf16[256,768]{1,0:T(8,128)(2,1)S(1)} %bitcast.45), channel_id=1, source_target_pairs={{0,2},{1,3},{2,0},{3,1},{4,6},{5,7},{6,4},{7,5},{8,10},{9,11},{10,... | collective-permute-start | bytes 1179656 | tf_op jit(solution)/shard_map/ppermute | solution.py:73
  24.7 24.1 %collective-permute-start.2 = (bf16[256,768]{1,0:T(8,128)(2,1)S(1)}, bf16[256,768]{1,0:T(8,128)(2,1)S(1)}, u32[]{:S(2)}, u32[]{:S(2)}) collective-permute-start(bf16[256,768]{1,0:T(8,128)(2,1)S(1)} %bitcast.46), channel_id=1, source_target_pairs={{0,1},{1,2},{2,3},{3,0},{4,5},{5,6},{6,7},{7,4},{8,9},{9,10},{10,1... | collective-permute-start | bytes 1179656 | tf_op jit(solution)/shard_map/ppermute | solution.py:73
  48.6 1.0 copy-start.6
  48.8 2.2 %copy-start.8 = (bf16[256,768]{1,0:T(8,128)(2,1)}, bf16[256,768]{1,0:T(8,128)(2,1)S(1)}, u32[]{:S(2)}) copy-start(bf16[256,768]{1,0:T(8,128)(2,1)S(1)} %collective-permute-done.1) | copy-start | bytes 1179652
  48.8 2.2 %copy-start.10 = (bf16[256,768]{1,0:T(8,128)(2,1)}, bf16[256,768]{1,0:T(8,128)(2,1)S(1)}, u32[]{:S(2)}) copy-start(bf16[256,768]{1,0:T(8,128)(2,1)S(1)} %collective-permute-done.2) | copy-start | bytes 1179652
  49.6 1.4 copy-start.2
  51.0 7.3 %copy-start.4 = (bf16[1024,576]{1,0:T(8,128)(2,1)}, bf16[1024,576]{1,0:T(8,128)(2,1)S(1)}, u32[]{:S(2)}) copy-start(bf16[1024,576]{1,0:T(8,128)(2,1)S(1)} %add_convert_fusion.qkv_ref) | copy-start | bytes 3538948
  58.3 22.6 %copy-start.3 = (bf16[1,256,768]{2,1,0:T(8,128)(2,1)S(1)}, bf16[1,256,768]{2,1,0:T(8,128)(2,1)}, u32[]{:S(2)}) copy-start(bf16[1,256,768]{2,1,0:T(8,128)(2,1)} %param.33) | copy-start | bytes 1179652
  58.4 6.3 %collective-permute-start.5 = (bf16[256,192]{1,0:T(8,128)(2,1)S(1)}, bf16[256,192]{1,0:T(8,128)(2,1)S(1)}, u32[]{:S(2)}, u32[]{:S(2)}) collective-permute-start(bf16[256,192]{1,0:T(8,128)(2,1)S(1)} %get-tuple-element.61), channel_id=1, source_target_pairs={{0,1},{1,2},{2,3},{3,0},{4,5},{5,6},{6,7},{7,4},{8,9},{9,10},{10,1... | collective-permute-start | bytes 294920 | tf_op jit(solution)/shard_map/ppermute | solution.py:73
  59.0 9.2 %collective-permute-start.3 = (bf16[256,192]{1,0:T(8,128)(2,1)S(1)}, bf16[256,192]{1,0:T(8,128)(2,1)S(1)}, u32[]{:S(2)}, u32[]{:S(2)}) collective-permute-start(bf16[256,192]{1,0:T(8,128)(2,1)S(1)} %get-tuple-element.63), channel_id=1, source_target_pairs={{0,3},{1,0},{2,1},{3,2},{4,7},{5,4},{6,5},{7,6},{8,11},{9,8},{10,9... | collective-permute-start | bytes 294920 | tf_op jit(solution)/shard_map/ppermute | solution.py:73
  60.5 7.6 %collective-permute-start.4 = (bf16[256,192]{1,0:T(8,128)(2,1)S(1)}, bf16[256,192]{1,0:T(8,128)(2,1)}, u32[]{:S(2)}, u32[]{:S(2)}) collective-permute-start(bf16[256,192]{1,0:T(8,128)(2,1)S(1)} %get-tuple-element.62), channel_id=1, source_target_pairs={{0,2},{1,3},{2,0},{3,1},{4,6},{5,7},{6,4},{7,5},{8,10},{9,11},{10,... | collective-permute-start | bytes 294920 | tf_op jit(solution)/shard_map/ppermute | solution.py:73
  97.1 4.5 %copy-start.9 = (bf16[256,768]{1,0:T(8,128)(2,1)S(1)}, bf16[256,768]{1,0:T(8,128)(2,1)}, u32[]{:S(2)}) copy-start(bf16[256,768]{1,0:T(8,128)(2,1)} %copy-done.8) | copy-start | bytes 1179652
  97.1 4.4 %copy-start.11 = (bf16[256,768]{1,0:T(8,128)(2,1)S(1)}, bf16[256,768]{1,0:T(8,128)(2,1)}, u32[]{:S(2)}) copy-start(bf16[256,768]{1,0:T(8,128)(2,1)} %copy-done.10) | copy-start | bytes 1179652
  97.2 10.0 %collective-permute-start.6 = (bf16[256,192]{1,0:T(8,128)(2,1)S(1)}, bf16[256,192]{1,0:T(8,128)(2,1)S(1)}, u32[]{:S(2)}, u32[]{:S(2)}) collective-permute-start(bf16[256,192]{1,0:T(8,128)(2,1)S(1)} %get-tuple-element.59), channel_id=1, source_target_pairs={{0,3},{1,0},{2,1},{3,2},{4,7},{5,4},{6,5},{7,6},{8,11},{9,8},{10,9... | collective-permute-start | bytes 294920 | tf_op jit(solution)/shard_map/ppermute | solution.py:73
  98.3 8.8 %collective-permute-start.7 = (bf16[256,192]{1,0:T(8,128)(2,1)S(1)}, bf16[256,192]{1,0:T(8,128)(2,1)S(1)}, u32[]{:S(2)}, u32[]{:S(2)}) collective-permute-start(bf16[256,192]{1,0:T(8,128)(2,1)S(1)} %get-tuple-element.58), channel_id=1, source_target_pairs={{0,2},{1,3},{2,0},{3,1},{4,6},{5,7},{6,4},{7,5},{8,10},{9,11},{10,... | collective-permute-start | bytes 294920 | tf_op jit(solution)/shard_map/ppermute | solution.py:73
  99.4 8.4 %copy-start.5 = (bf16[1024,576]{1,0:T(8,128)(2,1)S(1)}, bf16[1024,576]{1,0:T(8,128)(2,1)}, u32[]{:S(2)}) copy-start(bf16[1024,576]{1,0:T(8,128)(2,1)} %copy-done.4) | copy-start | bytes 3538948
  99.4 8.3 %collective-permute-start.8 = (bf16[256,192]{1,0:T(8,128)(2,1)S(1)}, bf16[256,192]{1,0:T(8,128)(2,1)S(1)}, u32[]{:S(2)}, u32[]{:S(2)}) collective-permute-start(bf16[256,192]{1,0:T(8,128)(2,1)S(1)} %get-tuple-element.57), channel_id=1, source_target_pairs={{0,1},{1,2},{2,3},{3,0},{4,5},{5,6},{6,7},{7,4},{8,9},{9,10},{10,1... | collective-permute-start | bytes 294920 | tf_op jit(solution)/shard_map/ppermute | solution.py:73
  107.8 18.3 %copy-start.7 = (bf16[32,24,576]{2,1,0:T(8,128)(2,1)S(1)}, bf16[32,24,576]{2,1,0:T(8,128)(2,1)}, u32[]{:S(2)}) copy-start(bf16[32,24,576]{2,1,0:T(8,128)(2,1)} %copy-done.6) | copy-start | bytes 2654212
  126.0 6.8 %collective-permute-start.12 = (bf16[384,768]{1,0:T(8,128)(2,1)S(1)}, bf16[384,768]{1,0:T(8,128)(2,1)S(1)}, u32[]{:S(2)}, u32[]{:S(2)}) collective-permute-start(bf16[384,768]{1,0:T(8,128)(2,1)S(1)} %get-tuple-element.33), channel_id=1, source_target_pairs={{0,4},{4,0},{8,12},{12,8},{16,20},{20,16},{24,28},{28,24},{32,36},... | collective-permute-start | bytes 1769480 | tf_op jit(solution)/shard_map/ppermute | solution.py:77
  128.5 13.0 %collective-permute-start.10 = (bf16[256,768]{1,0:T(8,128)(2,1)}, bf16[256,768]{1,0:T(8,128)(2,1)}, u32[]{:S(2)}, u32[]{:S(2)}) collective-permute-start(bf16[256,768]{1,0:T(8,128)(2,1)} %get-tuple-element.49), channel_id=1, source_target_pairs={{0,3},{1,0},{2,1},{3,2},{4,7},{5,4},{6,5},{7,6},{8,11},{9,8},{10,9... | collective-permute-start | bytes 1179656 | tf_op jit(solution)/shard_map/ppermute | solution.py:73
  129.3 21.5 %collective-permute-start.11 = (bf16[256,768]{1,0:T(8,128)(2,1)}, bf16[256,768]{1,0:T(8,128)(2,1)}, u32[]{:S(2)}, u32[]{:S(2)}) collective-permute-start(bf16[256,768]{1,0:T(8,128)(2,1)} %get-tuple-element.48), channel_id=1, source_target_pairs={{0,2},{1,3},{2,0},{3,1},{4,6},{5,7},{6,4},{7,5},{8,10},{9,11},{10,... | collective-permute-start | bytes 1179656 | tf_op jit(solution)/shard_map/ppermute | solution.py:73
  132.7 18.1 %collective-permute-start.9 = (bf16[256,768]{1,0:T(8,128)(2,1)S(1)}, bf16[256,768]{1,0:T(8,128)(2,1)}, u32[]{:S(2)}, u32[]{:S(2)}) collective-permute-start(bf16[256,768]{1,0:T(8,128)(2,1)S(1)} %get-tuple-element.47), channel_id=1, source_target_pairs={{0,1},{1,2},{2,3},{3,0},{4,5},{5,6},{6,7},{7,4},{8,9},{9,10},{10,1... | collective-permute-start | bytes 1179656 | tf_op jit(solution)/shard_map/ppermute | solution.py:73
  133.7 21.3 %all-to-all-start.1 = ((bf16[16,24,768]{2,1,0:T(8,128)(2,1)}), bf16[16,24,768]{2,1,0:T(8,128)(2,1)S(1)}, u32[]{:S(2)}, u32[]{:S(2)}) async-start(bf16[16,24,768]{2,1,0:T(8,128)(2,1)} %bitcast.19), calls=%async_computation.1 | async-start | bytes 1179648 | tf_op jit(solution)/shard_map/all_to_all | solution.py:593
  155.1 5.2 %collective-permute-start.13 = (bf16[24,768]{1,0:T(8,128)(2,1)S(1)}, bf16[24,768]{1,0:T(8,128)(2,1)S(1)}, u32[]{:S(2)}, u32[]{:S(2)}) collective-permute-start(bf16[24,768]{1,0:T(8,128)(2,1)S(1)} %reduce_sum.21), channel_id=1, source_target_pairs={{0,3},{1,0},{2,1},{3,2},{4,7},{5,4},{6,5},{7,6},{8,11},{9,8},{10,9... | collective-permute-start | bytes 110600 | tf_op jit(solution)/shard_map/ppermute | solution.py:73
  157.0 5.5 %collective-permute-start.14 = (bf16[24,768]{1,0:T(8,128)(2,1)S(1)}, bf16[24,768]{1,0:T(8,128)(2,1)S(1)}, u32[]{:S(2)}, u32[]{:S(2)}) collective-permute-start(bf16[24,768]{1,0:T(8,128)(2,1)S(1)} %reduce_sum.21), channel_id=1, source_target_pairs={{0,2},{1,3},{2,0},{3,1},{4,6},{5,7},{6,4},{7,5},{8,10},{9,11},{10,... | collective-permute-start | bytes 110600 | tf_op jit(solution)/shard_map/ppermute | solution.py:73
  157.3 5.2 %collective-permute-start.15 = (bf16[24,768]{1,0:T(8,128)(2,1)S(1)}, bf16[24,768]{1,0:T(8,128)(2,1)S(1)}, u32[]{:S(2)}, u32[]{:S(2)}) collective-permute-start(bf16[24,768]{1,0:T(8,128)(2,1)S(1)} %reduce_sum.21), channel_id=1, source_target_pairs={{0,1},{1,2},{2,3},{3,0},{4,5},{5,6},{6,7},{7,4},{8,9},{9,10},{10,1... | collective-permute-start | bytes 110600 | tf_op jit(solution)/shard_map/ppermute | solution.py:73
  167.2 9.7 %collective-permute-start.22 = (bf16[24,3072]{1,0:T(8,128)(2,1)S(1)}, bf16[24,3072]{1,0:T(8,128)(2,1)S(1)}, u32[]{:S(2)}, u32[]{:S(2)}) collective-permute-start(bf16[24,3072]{1,0:T(8,128)(2,1)S(1)} %get-tuple-element.50), channel_id=1, source_target_pairs={{0,32},{4,36},{8,40},{12,44},{16,48},{20,52},{24,56},{28,60},{32,6... | collective-permute-start | bytes 442376 | tf_op jit(solution)/shard_map/ppermute | solution.py:81
  168.8 8.5 %collective-permute-start.23 = (bf16[24,3072]{1,0:T(8,128)(2,1)S(1)}, bf16[24,3072]{1,0:T(8,128)(2,1)S(1)}, u32[]{:S(2)}, u32[]{:S(2)}) collective-permute-start(bf16[24,3072]{1,0:T(8,128)(2,1)S(1)} %get-tuple-element.52), channel_id=1, source_target_pairs={{0,96},{4,100},{8,104},{12,108},{16,112},{20,116},{24,120},{28,124... | collective-permute-start | bytes 442376 | tf_op jit(solution)/shard_map/ppermute | solution.py:81
  170.5 8.6 %collective-permute-start.24 = (bf16[24,3072]{1,0:T(8,128)(2,1)S(1)}, bf16[24,3072]{1,0:T(8,128)(2,1)S(1)}, u32[]{:S(2)}, u32[]{:S(2)}) collective-permute-start(bf16[24,3072]{1,0:T(8,128)(2,1)S(1)} %get-tuple-element.51), channel_id=1, source_target_pairs={{0,64},{4,68},{8,72},{12,76},{16,80},{20,84},{24,88},{28,92},{32,9... | collective-permute-start | bytes 442376 | tf_op jit(solution)/shard_map/ppermute | solution.py:81
  173.6 9.4 %collective-permute-start.16 = (bf16[24,3840]{1,0:T(8,128)(2,1)S(1)}, bf16[24,3840]{1,0:T(8,128)(2,1)S(1)}, u32[]{:S(2)}, u32[]{:S(2)}) collective-permute-start(bf16[24,3840]{1,0:T(8,128)(2,1)S(1)} %get-tuple-element.53), channel_id=1, source_target_pairs={{0,32},{4,36},{8,40},{12,44},{16,48},{20,52},{24,56},{28,60},{32,6... | collective-permute-start | bytes 552968 | tf_op jit(solution)/shard_map/ppermute | solution.py:81
  174.3 10.1 %collective-permute-start.17 = (bf16[24,3840]{1,0:T(8,128)(2,1)S(1)}, bf16[24,3840]{1,0:T(8,128)(2,1)S(1)}, u32[]{:S(2)}, u32[]{:S(2)}) collective-permute-start(bf16[24,3840]{1,0:T(8,128)(2,1)S(1)} %get-tuple-element.55), channel_id=1, source_target_pairs={{0,96},{4,100},{8,104},{12,108},{16,112},{20,116},{24,120},{28,124... | collective-permute-start | bytes 552968 | tf_op jit(solution)/shard_map/ppermute | solution.py:81
  176.9 9.0 %collective-permute-start.18 = (bf16[24,3840]{1,0:T(8,128)(2,1)S(1)}, bf16[24,3840]{1,0:T(8,128)(2,1)S(1)}, u32[]{:S(2)}, u32[]{:S(2)}) collective-permute-start(bf16[24,3840]{1,0:T(8,128)(2,1)S(1)} %get-tuple-element.54), channel_id=1, source_target_pairs={{0,64},{4,68},{8,72},{12,76},{16,80},{20,84},{24,88},{28,92},{32,9... | collective-permute-start | bytes 552968 | tf_op jit(solution)/shard_map/ppermute | solution.py:81
  180.2 8.8 %collective-permute-start.25 = (bf16[24,3072]{1,0:T(8,128)(2,1)S(1)}, bf16[24,3072]{1,0:T(8,128)(2,1)S(1)}, u32[]{:S(2)}, u32[]{:S(2)}) collective-permute-start(bf16[24,3072]{1,0:T(8,128)(2,1)S(1)} %add_convert_fusion.4.a_ref), channel_id=1, source_target_pairs={{0,1},{1,2},{2,3},{3,0},{4,5},{5,6},{6,7},{7,4},{8,9},{9,10},{10,1... | collective-permute-start | bytes 442376 | tf_op jit(solution)/shard_map/ppermute | solution.py:73
  180.8 12.5 %collective-permute-start.26 = (bf16[24,3072]{1,0:T(8,128)(2,1)S(1)}, bf16[24,3072]{1,0:T(8,128)(2,1)S(1)}, u32[]{:S(2)}, u32[]{:S(2)}) collective-permute-start(bf16[24,3072]{1,0:T(8,128)(2,1)S(1)} %add_convert_fusion.4.a_ref), channel_id=1, source_target_pairs={{0,3},{1,0},{2,1},{3,2},{4,7},{5,4},{6,5},{7,6},{8,11},{9,8},{10,9... | collective-permute-start | bytes 442376 | tf_op jit(solution)/shard_map/ppermute | solution.py:73
  183.0 10.3 %collective-permute-start.27 = (bf16[24,3072]{1,0:T(8,128)(2,1)S(1)}, bf16[24,3072]{1,0:T(8,128)(2,1)S(1)}, u32[]{:S(2)}, u32[]{:S(2)}) collective-permute-start(bf16[24,3072]{1,0:T(8,128)(2,1)S(1)} %add_convert_fusion.4.a_ref), channel_id=1, source_target_pairs={{0,2},{1,3},{2,0},{3,1},{4,6},{5,7},{6,4},{7,5},{8,10},{9,11},{10,... | collective-permute-start | bytes 442376 | tf_op jit(solution)/shard_map/ppermute | solution.py:73
  186.9 7.6 %collective-permute-start.19 = (bf16[24,3840]{1,0:T(8,128)(2,1)S(1)}, bf16[24,3840]{1,0:T(8,128)(2,1)S(1)}, u32[]{:S(2)}, u32[]{:S(2)}) collective-permute-start(bf16[24,3840]{1,0:T(8,128)(2,1)S(1)} %add_convert_fusion.3.a_ref), channel_id=1, source_target_pairs={{0,1},{1,2},{2,3},{3,0},{4,5},{5,6},{6,7},{7,4},{8,9},{9,10},{10,1... | collective-permute-start | bytes 552968 | tf_op jit(solution)/shard_map/ppermute | solution.py:73
  187.6 10.5 %collective-permute-start.20 = (bf16[24,3840]{1,0:T(8,128)(2,1)S(1)}, bf16[24,3840]{1,0:T(8,128)(2,1)S(1)}, u32[]{:S(2)}, u32[]{:S(2)}) collective-permute-start(bf16[24,3840]{1,0:T(8,128)(2,1)S(1)} %add_convert_fusion.3.a_ref), channel_id=1, source_target_pairs={{0,3},{1,0},{2,1},{3,2},{4,7},{5,4},{6,5},{7,6},{8,11},{9,8},{10,9... | collective-permute-start | bytes 552968 | tf_op jit(solution)/shard_map/ppermute | solution.py:73
  189.0 9.1 %collective-permute-start.21 = (bf16[24,3840]{1,0:T(8,128)(2,1)S(1)}, bf16[24,3840]{1,0:T(8,128)(2,1)S(1)}, u32[]{:S(2)}, u32[]{:S(2)}) collective-permute-start(bf16[24,3840]{1,0:T(8,128)(2,1)S(1)} %add_convert_fusion.3.a_ref), channel_id=1, source_target_pairs={{0,2},{1,3},{2,0},{3,1},{4,6},{5,7},{6,4},{7,5},{8,10},{9,11},{10,... | collective-permute-start | bytes 552968 | tf_op jit(solution)/shard_map/ppermute | solution.py:73
  190.4 7.6 %copy-start = (bf16[768,768]{1,0:T(8,128)(2,1)S(1)}, bf16[768,768]{1,0:T(8,128)(2,1)}, u32[]{:S(2)}) copy-start(bf16[768,768]{1,0:T(8,128)(2,1)} %constant.85.clone.refs_3_.order_ref) | copy-start | bytes 3538948
Sparse Core Ops, SparseCore 0:
  10.9 69.9 all-gather.1
  97.2 68.8 reduce-scatter.1

commit v5 on v4

--- a/solution.py
+++ b/solution.py
@@ -569,10 +569,10 @@
             for step in range(4)
         ]
         total = rows[0].astype(F32)
-        for step in ORDER:
+        for step in (2, 1, 3):
             total = total + to_z(rows[step], step).astype(F32)
         total = total.astype(BF16)
-        return [total] + [to_x(total, step) for step in ORDER]
+        return [total] + [to_x(total, step) for step in (2, 1, 3)]
 
     reduce_parts = spread(0, FF)
     other_parts = spread(FF, FF + D)

time: 207 us -> 209 us (level)
  transfers between devices with their start and end apart: 32 -> 32, of which waited for: 17 -> 16; matrix products, arithmetic and copies ran while one was open for 8% -> 8% of each run, Pallas kernels for 14% -> 14%
where the time goes in v5:
time: 209 us; the launch traced here: 208 us
  waiting for transfers between devices  73.1 us (35%)
  starting transfers between devices  52.7 us (25%)
  Pallas kernels  49.3 us (24%)
  between operations  15.3 us (7%)
  local copies, waits for them, and re-layouts  7.72 us (4%)
  other arithmetic  7.23 us (3%)
  matrix products  2.81 us (1%)
    ppermute x21, waiting for transfers between devices, to_x(): return lax.ppermute(values, 'sp', [(i, (i + step) % SP) for i in range(SP)])  31.7 us
    ppermute x21, starting transfers between devices, to_x(): return lax.ppermute(values, 'sp', [(i, (i + step) % SP) for i in range(SP)])  28.7 us
    all_to_all x1, waiting for transfers between devices, per_device(): lax.all_to_all(early, 'fsdp', split_axis=0, concat_axis=0, tiled=True)  21.4 us
    pallas_call x1, Pallas kernels, attend_back(): pl.pallas_call(attend_back_kernel, out_shape=(jax.ShapeDtypeStruct((LEN,...  18.1 us
    pallas_call x1, Pallas kernels, middle(): pl.pallas_call(middle_kernel, out_shape=(jax.ShapeDtypeStruct(tall, BF16)...  16.1 us
    all_gather x1, waiting for transfers between devices, per_device(): packed = lax.all_gather(packed, 'fsdp', axis=0, tiled=True)  11.8 us
    ppermute x6, starting transfers between devices, to_z(): lax.ppermute(values, 'fsdp', [(i, (i + 8 * step) % 32) for i in range(32)])  10.3 us
    all_to_all x1, starting transfers between devices, per_device(): lax.all_to_all(early, 'fsdp', split_axis=0, concat_axis=0, tiled=True)  8.48 us
  transfers between devices with their start and end apart: 32, of which 16 were waited for; matrix products, arithmetic and copies ran while one was open for 8% of the time, Pallas kernels for 14%

profile of v5, /device:TPU:6, one launch (start us, length us, event | category | flops | bytes accessed | tf_op | source)
XLA Modules:
  0.0 208.1 jit_solution(10301310963085750222)
XLA Ops:
  7.2 2.6 %pack.1.after_ref = bf16[24,6912]{1,0:T(8,128)(2,1)} custom-call(bf16[24,768]{1,0:T(8,128)(2,1)} %refs_0_.2, bf16[24,3072]{1,0:T(8,128)(2,1)} %refs_1_.2, bf16[96,768]{1,0:T(8,128)(2,1)} %refs_2_.2, bf16[768,768]{1,0:T(8,128)(2,1)} %constant.85.clone.refs_3_.order_ref), custom_call_target="tpu_custom_call" | custom-call | tf_op jit(solution)/shard_map/pack/pallas_call | solution.py:381
  10.5 0.6 pad_add_fusion.info_ref
  11.1 3.0 %early_pack.1 = bf16[32,32,576]{2,1,0:T(8,128)(2,1)} custom-call(s32[3]{0:T(128)} %pad_add_fusion.info_ref, bf16[24,6912]{1,0:T(8,128)(2,1)} %pack.1.after_ref, bf16[24,2304]{1,0:T(8,128)(2,1)} %refs_0_.3, bf16[24]{0:T(256)(128)(2,1)} %refs_1_.3, bf16[24]{0:T(256)(128)(2,1)} %refs_2_.3, bf16[24]{0:T(256)(128)(2,1)} %refs_3_.2, bf16[24]{0:T(256)(128)(2,1)} %refs_4_.1, ...), custom_call_target="tpu_custom_call" | custom-call | tf_op jit(solution)/shard_map/early_pack/pallas_call | solution.py:395
  14.2 8.5 %all-to-all-start = ((bf16[32,32,576]{2,1,0:T(8,128)(2,1)}), bf16[32,32,576]{2,1,0:T(8,128)(2,1)S(1)}, u32[]{:S(2)}, u32[]{:S(2)}) async-start(bf16[32,32,576]{2,1,0:T(8,128)(2,1)} %early_pack.1), calls=%async_computation | async-start | bytes 2621440 | tf_op jit(solution)/shard_map/all_to_all | solution.py:531
  22.7 0.9 collective-permute-start
  23.6 1.1 collective-permute-start.1
  24.7 2.1 %collective-permute-start.2 = (bf16[256,768]{1,0:T(8,128)(2,1)S(1)}, bf16[256,768]{1,0:T(8,128)(2,1)S(1)}, u32[]{:S(2)}, u32[]{:S(2)}) collective-permute-start(bf16[256,768]{1,0:T(8,128)(2,1)S(1)} %bitcast.46), channel_id=1, source_target_pairs={{0,1},{1,2},{2,3},{3,0},{4,5},{5,6},{6,7},{7,4},{8,9},{9,10},{10,1... | collective-permute-start | bytes 1179656 | tf_op jit(solution)/shard_map/ppermute | solution.py:73
  26.8 21.4 %all-to-all-done = bf16[32,32,576]{2,1,0:T(8,128)(2,1)S(1)} async-done(((bf16[32,32,576]{2,1,0:T(8,128)(2,1)}), bf16[32,32,576]{2,1,0:T(8,128)(2,1)S(1)}, u32[]{:S(2)}, u32[]{:S(2)}) %all-to-all-start) | async-done | bytes 1179680 | tf_op jit(solution)/shard_map/all_to_all | solution.py:531
  48.8 0.7 copy-done.6
  49.6 1.4 add_convert_fusion.qkv_ref
  51.0 7.3 %attend.1 = bf16[1024,192]{1,0:T(8,128)(2,1)S(1)} custom-call(s32[3]{0:T(128)S(1)} %copy-done.2, bf16[1024,576]{1,0:T(8,128)(2,1)S(1)} %add_convert_fusion.qkv_ref), custom_call_target="tpu_custom_call" | custom-call | flops 3221225472 | bytes 1572864 | tf_op jit(solution)/shard_map/attend/pallas_call | solution.py:339
  58.4 0.6 collective-permute-start.5
  59.0 1.5 collective-permute-start.3
  60.5 1.4 collective-permute-start.4
  62.3 2.4 %collective-permute-done.5 = bf16[256,192]{1,0:T(8,128)(2,1)S(1)} collective-permute-done((bf16[256,192]{1,0:T(8,128)(2,1)S(1)}, bf16[256,192]{1,0:T(8,128)(2,1)S(1)}, u32[]{:S(2)}, u32[]{:S(2)}) %collective-permute-start.5) | collective-permute-done | bytes 98336 | tf_op jit(solution)/shard_map/ppermute | solution.py:73
  64.7 3.4 %collective-permute-done.3 = bf16[256,192]{1,0:T(8,128)(2,1)S(1)} collective-permute-done((bf16[256,192]{1,0:T(8,128)(2,1)S(1)}, bf16[256,192]{1,0:T(8,128)(2,1)S(1)}, u32[]{:S(2)}, u32[]{:S(2)}) %collective-permute-start.3) | collective-permute-done | bytes 98336 | tf_op jit(solution)/shard_map/ppermute | solution.py:73
  68.1 1.0 pad_maximum_fusion.1.context_ref
  69.1 11.8 %all-gather.2.cloned.1.call-done.weights_ref = bf16[768,6912]{1,0:T(8,128)(2,1)} async-done(((bf16[24,6912]{1,0:T(8,128)(2,1)}), bf16[768,6912]{1,0:T(8,128)(2,1)}) %all-gather.2.cloned.1.call-update) | async-done | bytes 10616848 | tf_op jit(solution)/shard_map/all_gather | solution.py:530
  80.9 16.1 %middle.1 = (bf16[256,768]{1,0:T(8,128)(2,1)}, f32[256,768]{1,0:T(8,128)S(1)}, bf16[4,256,192]{2,1,0:T(8,128)(2,1)S(1)}, f32[8,768]{1,0:T(8,128)S(1)}, f32[4,768]{1,0:T(4,128)S(1)}, /*index=5*/bf16[768,6912]{1,0:T(8,128)(2,1)}) custom-call(s32[3]{0:T(128)S(1)} %copy-done.2, bf16[4,256,192]{2,1,0:T(8,128)(2,1)S(1)} %pad_maximum_fusion.1.context_ref, ...), custom_call_target="tpu_custom_call" | custom-call | flops 8153726976 | bytes 25165824 | tf_op jit(solution)/shard_map/middle/pallas_call | solution.py:465
  97.2 1.1 collective-permute-start.6
  98.3 1.2 collective-permute-start.7
  99.4 2.1 collective-permute-start.8
  101.6 5.5 %collective-permute-done.6 = bf16[256,192]{1,0:T(8,128)(2,1)S(1)} collective-permute-done((bf16[256,192]{1,0:T(8,128)(2,1)S(1)}, bf16[256,192]{1,0:T(8,128)(2,1)S(1)}, u32[]{:S(2)}, u32[]{:S(2)}) %collective-permute-start.6) | collective-permute-done | bytes 98336 | tf_op jit(solution)/shard_map/ppermute | solution.py:73
  107.1 0.6 collective-permute-done.8
  107.8 18.1 %attend_back.1 = (bf16[1024,576]{1,0:T(8,128)(2,1)S(1)}, bf16[384,768]{1,0:T(8,128)(2,1)S(1)}, bf16[384,768]{1,0:T(8,128)(2,1)S(1)}) custom-call(s32[3]{0:T(128)S(1)} %copy-done.2, bf16[1024,576]{1,0:T(8,128)(2,1)S(1)} %copy-done.5, bf16[1024,192]{1,0:T(8,128)(2,1)S(1)} %pad_maximum_fusion.2.grad_ref, bf16[1024,768]{1,0:T(8,128)(2,1)S(1)} %pad_maximum_fusion.tokens_ref, ...), custom_call_target="tpu_custom_call" | custom-call | flops 8053063680 | bytes 2752512 | tf_op jit(solution)/shard_map/attend_back/pallas_call | solution.py:353
  126.1 1.4 convolution_convert_fusion
  127.5 1.0 fusion.2
  128.5 0.8 collective-permute-start.10
  129.3 3.4 %collective-permute-start.11 = (bf16[256,768]{1,0:T(8,128)(2,1)}, bf16[256,768]{1,0:T(8,128)(2,1)}, u32[]{:S(2)}, u32[]{:S(2)}) collective-permute-start(bf16[256,768]{1,0:T(8,128)(2,1)} %get-tuple-element.48), channel_id=1, source_target_pairs={{0,2},{1,3},{2,0},{3,1},{4,6},{5,7},{6,4},{7,5},{8,10},{9,11},{10,... | collective-permute-start | bytes 1179656 | tf_op jit(solution)/shard_map/ppermute | solution.py:73
  132.7 1.0 add_convert_fusion.1
  133.7 5.1 %all-to-all-start.1 = ((bf16[16,24,768]{2,1,0:T(8,128)(2,1)}), bf16[16,24,768]{2,1,0:T(8,128)(2,1)S(1)}, u32[]{:S(2)}, u32[]{:S(2)}) async-start(bf16[16,24,768]{2,1,0:T(8,128)(2,1)} %bitcast.19), calls=%async_computation.1 | async-start | bytes 1179648 | tf_op jit(solution)/shard_map/all_to_all | solution.py:593
  138.9 2.6 %collective-permute-done.10 = bf16[256,768]{1,0:T(8,128)(2,1)} collective-permute-done((bf16[256,768]{1,0:T(8,128)(2,1)}, bf16[256,768]{1,0:T(8,128)(2,1)}, u32[]{:S(2)}, u32[]{:S(2)}) %collective-permute-start.10) | collective-permute-done | bytes 393248 | tf_op jit(solution)/shard_map/ppermute | solution.py:73
  141.5 9.3 %collective-permute-done.11 = bf16[256,768]{1,0:T(8,128)(2,1)} collective-permute-done((bf16[256,768]{1,0:T(8,128)(2,1)}, bf16[256,768]{1,0:T(8,128)(2,1)}, u32[]{:S(2)}, u32[]{:S(2)}) %collective-permute-start.11) | collective-permute-done | bytes 393248 | tf_op jit(solution)/shard_map/ppermute | solution.py:73
  150.8 2.2 %fusion = bf16[1,256,768]{2,1,0:T(8,128)(2,1)} fusion(bf16[256,768]{1,0:T(8,128)(2,1)} %collective-permute-done.11, bf16[256,768]{1,0:T(8,128)(2,1)} %collective-permute-done.10, bf16[256,768]{1,0:T(8,128)(2,1)} %collective-permute-done.9, f32[256,768]{1,0:T(8,128)S(1)} %get-tuple-element.27, bf16[1024,768]{1,0:T(8,128)(2,1)S(1)} %convolution_convert_fusion), kind=kLoop, calls=%fused_computation.7 | loop fusion | flops 1769472 | bytes 2752512 | tf_op jit(solution)/shard_map/broadcast_in_dim | solution.py:591
  153.0 1.9 all-to-all-done.1
  155.1 2.0 collective-permute-start.13
  157.0 0.3 collective-permute-start.14
  157.3 2.5 %collective-permute-start.15 = (bf16[24,768]{1,0:T(8,128)(2,1)S(1)}, bf16[24,768]{1,0:T(8,128)(2,1)S(1)}, u32[]{:S(2)}, u32[]{:S(2)}) collective-permute-start(bf16[24,768]{1,0:T(8,128)(2,1)S(1)} %reduce_sum.21), channel_id=1, source_target_pairs={{0,1},{1,2},{2,3},{3,0},{4,5},{5,6},{6,7},{7,4},{8,9},{9,10},{10,1... | collective-permute-start | bytes 110600 | tf_op jit(solution)/shard_map/ppermute | solution.py:73
  159.8 0.5 collective-permute-done.13
  160.3 2.2 %collective-permute-done.14 = bf16[24,768]{1,0:T(8,128)(2,1)S(1)} collective-permute-done((bf16[24,768]{1,0:T(8,128)(2,1)S(1)}, bf16[24,768]{1,0:T(8,128)(2,1)S(1)}, u32[]{:S(2)}, u32[]{:S(2)}) %collective-permute-start.14) | collective-permute-done | bytes 36896 | tf_op jit(solution)/shard_map/ppermute | solution.py:73
  162.6 3.5 %reduce-scatter.2.cloned.1.call-done = bf16[96,6912]{1,0:T(8,128)(2,1)} async-done(((bf16[768,6912]{1,0:T(8,128)(2,1)}), bf16[96,6912]{1,0:T(8,128)(2,1)}) %reduce-scatter.2.cloned.1.call-update) | async-done | bytes 1327120 | tf_op jit(solution)/shard_map/reduce_scatter | solution.py:557
  166.1 1.1 constant_dynamic-slice_fusion.2
  167.2 3.2 %collective-permute-start.22 = (bf16[24,3072]{1,0:T(8,128)(2,1)S(1)}, bf16[24,3072]{1,0:T(8,128)(2,1)S(1)}, u32[]{:S(2)}, u32[]{:S(2)}) collective-permute-start(bf16[24,3072]{1,0:T(8,128)(2,1)S(1)} %get-tuple-element.50), channel_id=1, source_target_pairs={{0,64},{4,68},{8,72},{12,76},{16,80},{20,84},{24,88},{28,92},{32,9... | collective-permute-start | bytes 442376 | tf_op jit(solution)/shard_map/ppermute | solution.py:81
  170.4 0.7 collective-permute-start.23
  171.1 2.6 %collective-permute-start.24 = (bf16[24,3072]{1,0:T(8,128)(2,1)S(1)}, bf16[24,3072]{1,0:T(8,128)(2,1)S(1)}, u32[]{:S(2)}, u32[]{:S(2)}) collective-permute-start(bf16[24,3072]{1,0:T(8,128)(2,1)S(1)} %get-tuple-element.51), channel_id=1, source_target_pairs={{0,96},{4,100},{8,104},{12,108},{16,112},{20,116},{24,120},{28,124... | collective-permute-start | bytes 442376 | tf_op jit(solution)/shard_map/ppermute | solution.py:81
  173.6 1.1 constant_dynamic-slice_fusion.7
  174.9 0.8 collective-permute-start.17
  175.7 2.9 %collective-permute-start.18 = (bf16[24,3840]{1,0:T(8,128)(2,1)S(1)}, bf16[24,3840]{1,0:T(8,128)(2,1)S(1)}, u32[]{:S(2)}, u32[]{:S(2)}) collective-permute-start(bf16[24,3840]{1,0:T(8,128)(2,1)S(1)} %get-tuple-element.54), channel_id=1, source_target_pairs={{0,96},{4,100},{8,104},{12,108},{16,112},{20,116},{24,120},{28,124... | collective-permute-start | bytes 552968 | tf_op jit(solution)/shard_map/ppermute | solution.py:81
  178.6 1.0 collective-permute-done.23
  179.6 1.8 collective-permute-done.24
  181.4 1.0 add_convert_fusion.4.a_ref
  182.3 1.5 collective-permute-start.25
  183.9 2.1 collective-permute-start.26
  186.0 1.0 add_convert_fusion.3.a_ref
  187.0 2.1 %collective-permute-start.19 = (bf16[24,3840]{1,0:T(8,128)(2,1)S(1)}, bf16[24,3840]{1,0:T(8,128)(2,1)S(1)}, u32[]{:S(2)}, u32[]{:S(2)}) collective-permute-start(bf16[24,3840]{1,0:T(8,128)(2,1)S(1)} %add_convert_fusion.3.a_ref), channel_id=1, source_target_pairs={{0,2},{1,3},{2,0},{3,1},{4,6},{5,7},{6,4},{7,5},{8,10},{9,11},{10,... | collective-permute-start | bytes 552968 | tf_op jit(solution)/shard_map/ppermute | solution.py:73
  189.1 1.3 collective-permute-start.20
  190.4 0.8 collective-permute-start.21
  191.6 0.9 reshape.72
  192.6 0.6 reshape.73
  193.2 0.8 slice_reduce_fusion.3
  194.0 2.8 %collective-permute-done.27.d_ref = bf16[24,3072]{1,0:T(8,128)(2,1)S(1)} collective-permute-done((bf16[24,3072]{1,0:T(8,128)(2,1)S(1)}, bf16[24,3072]{1,0:T(8,128)(2,1)S(1)}, u32[]{:S(2)}, u32[]{:S(2)}) %collective-permute-start.27) | collective-permute-done | bytes 147488 | tf_op jit(solution)/shard_map/ppermute | solution.py:73
  196.8 0.8 finish_reduce.1
  197.6 2.4 %collective-permute-done.21.d_ref = bf16[24,3840]{1,0:T(8,128)(2,1)S(1)} collective-permute-done((bf16[24,3840]{1,0:T(8,128)(2,1)S(1)}, bf16[24,3840]{1,0:T(8,128)(2,1)S(1)}, u32[]{:S(2)}, u32[]{:S(2)}) %collective-permute-start.21) | collective-permute-done | bytes 184352 | tf_op jit(solution)/shard_map/ppermute | solution.py:73
  200.0 1.3 finish.1
  (81 shorter events, 2.3 us)
Async XLA Ops:
  7.2 73.7 %all-gather.2.cloned.1.call-start = ((), (), s32[]{:S(2)}) async-start(), calls=%async_computation.3 | async-start | bytes 10948608 | tf_op jit(solution)/shard_map/all_gather | solution.py:530
  14.1 8.5 %copy-start.1 = (bf16[1,256,768]{2,1,0:T(8,128)(2,1)S(1)}, bf16[1,256,768]{2,1,0:T(8,128)(2,1)}, u32[]{:S(2)}) copy-start(bf16[1,256,768]{2,1,0:T(8,128)(2,1)} %param.18) | copy-start | bytes 1179652
  14.2 34.1 %all-to-all-start = ((bf16[32,32,576]{2,1,0:T(8,128)(2,1)}), bf16[32,32,576]{2,1,0:T(8,128)(2,1)S(1)}, u32[]{:S(2)}, u32[]{:S(2)}) async-start(bf16[32,32,576]{2,1,0:T(8,128)(2,1)} %early_pack.1), calls=%async_computation | async-start | bytes 2621440 | tf_op jit(solution)/shard_map/all_to_all | solution.py:531
  22.6 143.5 %reduce-scatter.2.cloned.1.call-start = ((), (), s32[]{:S(2)}) async-start(), calls=%async_computation.4 | async-start | bytes 11943936 | tf_op jit(solution)/shard_map/reduce_scatter | solution.py:557
  22.7 26.1 %collective-permute-start = (bf16[256,768]{1,0:T(8,128)(2,1)S(1)}, bf16[256,768]{1,0:T(8,128)(2,1)S(1)}, u32[]{:S(2)}, u32[]{:S(2)}) collective-permute-start(bf16[256,768]{1,0:T(8,128)(2,1)S(1)} %bitcast.44), channel_id=1, source_target_pairs={{0,3},{1,0},{2,1},{3,2},{4,7},{5,4},{6,5},{7,6},{8,11},{9,8},{10,9... | collective-permute-start | bytes 1179656 | tf_op jit(solution)/shard_map/ppermute | solution.py:73
  23.6 25.2 %collective-permute-start.1 = (bf16[256,768]{1,0:T(8,128)(2,1)S(1)}, bf16[256,768]{1,0:T(8,128)(2,1)S(1)}, u32[]{:S(2)}, u32[]{:S(2)}) collective-permute-start(bf16[256,768]{1,0:T(8,128)(2,1)S(1)} %bitcast.45), channel_id=1, source_target_pairs={{0,2},{1,3},{2,0},{3,1},{4,6},{5,7},{6,4},{7,5},{8,10},{9,11},{10,... | collective-permute-start | bytes 1179656 | tf_op jit(solution)/shard_map/ppermute | solution.py:73
  24.7 24.1 %collective-permute-start.2 = (bf16[256,768]{1,0:T(8,128)(2,1)S(1)}, bf16[256,768]{1,0:T(8,128)(2,1)S(1)}, u32[]{:S(2)}, u32[]{:S(2)}) collective-permute-start(bf16[256,768]{1,0:T(8,128)(2,1)S(1)} %bitcast.46), channel_id=1, source_target_pairs={{0,1},{1,2},{2,3},{3,0},{4,5},{5,6},{6,7},{7,4},{8,9},{9,10},{10,1... | collective-permute-start | bytes 1179656 | tf_op jit(solution)/shard_map/ppermute | solution.py:73
  48.6 1.0 copy-start.6
  48.8 2.2 %copy-start.8 = (bf16[256,768]{1,0:T(8,128)(2,1)}, bf16[256,768]{1,0:T(8,128)(2,1)S(1)}, u32[]{:S(2)}) copy-start(bf16[256,768]{1,0:T(8,128)(2,1)S(1)} %collective-permute-done.1) | copy-start | bytes 1179652
  48.8 2.2 %copy-start.10 = (bf16[256,768]{1,0:T(8,128)(2,1)}, bf16[256,768]{1,0:T(8,128)(2,1)S(1)}, u32[]{:S(2)}) copy-start(bf16[256,768]{1,0:T(8,128)(2,1)S(1)} %collective-permute-done.2) | copy-start | bytes 1179652
  49.6 1.4 copy-start.2
  51.0 7.3 %copy-start.4 = (bf16[1024,576]{1,0:T(8,128)(2,1)}, bf16[1024,576]{1,0:T(8,128)(2,1)S(1)}, u32[]{:S(2)}) copy-start(bf16[1024,576]{1,0:T(8,128)(2,1)S(1)} %add_convert_fusion.qkv_ref) | copy-start | bytes 3538948
  58.3 22.6 %copy-start.3 = (bf16[1,256,768]{2,1,0:T(8,128)(2,1)S(1)}, bf16[1,256,768]{2,1,0:T(8,128)(2,1)}, u32[]{:S(2)}) copy-start(bf16[1,256,768]{2,1,0:T(8,128)(2,1)} %param.33) | copy-start | bytes 1179652
  58.4 6.3 %collective-permute-start.5 = (bf16[256,192]{1,0:T(8,128)(2,1)S(1)}, bf16[256,192]{1,0:T(8,128)(2,1)S(1)}, u32[]{:S(2)}, u32[]{:S(2)}) collective-permute-start(bf16[256,192]{1,0:T(8,128)(2,1)S(1)} %get-tuple-element.61), channel_id=1, source_target_pairs={{0,1},{1,2},{2,3},{3,0},{4,5},{5,6},{6,7},{7,4},{8,9},{9,10},{10,1... | collective-permute-start | bytes 294920 | tf_op jit(solution)/shard_map/ppermute | solution.py:73
  59.0 9.2 %collective-permute-start.3 = (bf16[256,192]{1,0:T(8,128)(2,1)S(1)}, bf16[256,192]{1,0:T(8,128)(2,1)S(1)}, u32[]{:S(2)}, u32[]{:S(2)}) collective-permute-start(bf16[256,192]{1,0:T(8,128)(2,1)S(1)} %get-tuple-element.63), channel_id=1, source_target_pairs={{0,3},{1,0},{2,1},{3,2},{4,7},{5,4},{6,5},{7,6},{8,11},{9,8},{10,9... | collective-permute-start | bytes 294920 | tf_op jit(solution)/shard_map/ppermute | solution.py:73
  60.5 7.6 %collective-permute-start.4 = (bf16[256,192]{1,0:T(8,128)(2,1)S(1)}, bf16[256,192]{1,0:T(8,128)(2,1)}, u32[]{:S(2)}, u32[]{:S(2)}) collective-permute-start(bf16[256,192]{1,0:T(8,128)(2,1)S(1)} %get-tuple-element.62), channel_id=1, source_target_pairs={{0,2},{1,3},{2,0},{3,1},{4,6},{5,7},{6,4},{7,5},{8,10},{9,11},{10,... | collective-permute-start | bytes 294920 | tf_op jit(solution)/shard_map/ppermute | solution.py:73
  97.1 4.5 %copy-start.9 = (bf16[256,768]{1,0:T(8,128)(2,1)S(1)}, bf16[256,768]{1,0:T(8,128)(2,1)}, u32[]{:S(2)}) copy-start(bf16[256,768]{1,0:T(8,128)(2,1)} %copy-done.8) | copy-start | bytes 1179652
  97.1 4.4 %copy-start.11 = (bf16[256,768]{1,0:T(8,128)(2,1)S(1)}, bf16[256,768]{1,0:T(8,128)(2,1)}, u32[]{:S(2)}) copy-start(bf16[256,768]{1,0:T(8,128)(2,1)} %copy-done.10) | copy-start | bytes 1179652
  97.2 10.0 %collective-permute-start.6 = (bf16[256,192]{1,0:T(8,128)(2,1)S(1)}, bf16[256,192]{1,0:T(8,128)(2,1)S(1)}, u32[]{:S(2)}, u32[]{:S(2)}) collective-permute-start(bf16[256,192]{1,0:T(8,128)(2,1)S(1)} %get-tuple-element.59), channel_id=1, source_target_pairs={{0,3},{1,0},{2,1},{3,2},{4,7},{5,4},{6,5},{7,6},{8,11},{9,8},{10,9... | collective-permute-start | bytes 294920 | tf_op jit(solution)/shard_map/ppermute | solution.py:73
  98.3 8.8 %collective-permute-start.7 = (bf16[256,192]{1,0:T(8,128)(2,1)S(1)}, bf16[256,192]{1,0:T(8,128)(2,1)S(1)}, u32[]{:S(2)}, u32[]{:S(2)}) collective-permute-start(bf16[256,192]{1,0:T(8,128)(2,1)S(1)} %get-tuple-element.58), channel_id=1, source_target_pairs={{0,2},{1,3},{2,0},{3,1},{4,6},{5,7},{6,4},{7,5},{8,10},{9,11},{10,... | collective-permute-start | bytes 294920 | tf_op jit(solution)/shard_map/ppermute | solution.py:73
  99.4 8.4 %copy-start.5 = (bf16[1024,576]{1,0:T(8,128)(2,1)S(1)}, bf16[1024,576]{1,0:T(8,128)(2,1)}, u32[]{:S(2)}) copy-start(bf16[1024,576]{1,0:T(8,128)(2,1)} %copy-done.4) | copy-start | bytes 3538948
  99.4 8.3 %collective-permute-start.8 = (bf16[256,192]{1,0:T(8,128)(2,1)S(1)}, bf16[256,192]{1,0:T(8,128)(2,1)S(1)}, u32[]{:S(2)}, u32[]{:S(2)}) collective-permute-start(bf16[256,192]{1,0:T(8,128)(2,1)S(1)} %get-tuple-element.57), channel_id=1, source_target_pairs={{0,1},{1,2},{2,3},{3,0},{4,5},{5,6},{6,7},{7,4},{8,9},{9,10},{10,1... | collective-permute-start | bytes 294920 | tf_op jit(solution)/shard_map/ppermute | solution.py:73
  107.8 18.3 %copy-start.7 = (bf16[32,24,576]{2,1,0:T(8,128)(2,1)S(1)}, bf16[32,24,576]{2,1,0:T(8,128)(2,1)}, u32[]{:S(2)}) copy-start(bf16[32,24,576]{2,1,0:T(8,128)(2,1)} %copy-done.6) | copy-start | bytes 2654212
  126.0 6.8 %collective-permute-start.12 = (bf16[384,768]{1,0:T(8,128)(2,1)S(1)}, bf16[384,768]{1,0:T(8,128)(2,1)S(1)}, u32[]{:S(2)}, u32[]{:S(2)}) collective-permute-start(bf16[384,768]{1,0:T(8,128)(2,1)S(1)} %get-tuple-element.33), channel_id=1, source_target_pairs={{0,4},{4,0},{8,12},{12,8},{16,20},{20,16},{24,28},{28,24},{32,36},... | collective-permute-start | bytes 1769480 | tf_op jit(solution)/shard_map/ppermute | solution.py:77
  128.5 13.0 %collective-permute-start.10 = (bf16[256,768]{1,0:T(8,128)(2,1)}, bf16[256,768]{1,0:T(8,128)(2,1)}, u32[]{:S(2)}, u32[]{:S(2)}) collective-permute-start(bf16[256,768]{1,0:T(8,128)(2,1)} %get-tuple-element.49), channel_id=1, source_target_pairs={{0,3},{1,0},{2,1},{3,2},{4,7},{5,4},{6,5},{7,6},{8,11},{9,8},{10,9... | collective-permute-start | bytes 1179656 | tf_op jit(solution)/shard_map/ppermute | solution.py:73
  129.3 21.5 %collective-permute-start.11 = (bf16[256,768]{1,0:T(8,128)(2,1)}, bf16[256,768]{1,0:T(8,128)(2,1)}, u32[]{:S(2)}, u32[]{:S(2)}) collective-permute-start(bf16[256,768]{1,0:T(8,128)(2,1)} %get-tuple-element.48), channel_id=1, source_target_pairs={{0,2},{1,3},{2,0},{3,1},{4,6},{5,7},{6,4},{7,5},{8,10},{9,11},{10,... | collective-permute-start | bytes 1179656 | tf_op jit(solution)/shard_map/ppermute | solution.py:73
  132.7 18.1 %collective-permute-start.9 = (bf16[256,768]{1,0:T(8,128)(2,1)S(1)}, bf16[256,768]{1,0:T(8,128)(2,1)}, u32[]{:S(2)}, u32[]{:S(2)}) collective-permute-start(bf16[256,768]{1,0:T(8,128)(2,1)S(1)} %get-tuple-element.47), channel_id=1, source_target_pairs={{0,1},{1,2},{2,3},{3,0},{4,5},{5,6},{6,7},{7,4},{8,9},{9,10},{10,1... | collective-permute-start | bytes 1179656 | tf_op jit(solution)/shard_map/ppermute | solution.py:73
  133.7 21.3 %all-to-all-start.1 = ((bf16[16,24,768]{2,1,0:T(8,128)(2,1)}), bf16[16,24,768]{2,1,0:T(8,128)(2,1)S(1)}, u32[]{:S(2)}, u32[]{:S(2)}) async-start(bf16[16,24,768]{2,1,0:T(8,128)(2,1)} %bitcast.19), calls=%async_computation.1 | async-start | bytes 1179648 | tf_op jit(solution)/shard_map/all_to_all | solution.py:593
  155.1 5.2 %collective-permute-start.13 = (bf16[24,768]{1,0:T(8,128)(2,1)S(1)}, bf16[24,768]{1,0:T(8,128)(2,1)S(1)}, u32[]{:S(2)}, u32[]{:S(2)}) collective-permute-start(bf16[24,768]{1,0:T(8,128)(2,1)S(1)} %reduce_sum.21), channel_id=1, source_target_pairs={{0,3},{1,0},{2,1},{3,2},{4,7},{5,4},{6,5},{7,6},{8,11},{9,8},{10,9... | collective-permute-start | bytes 110600 | tf_op jit(solution)/shard_map/ppermute | solution.py:73
  157.0 5.5 %collective-permute-start.14 = (bf16[24,768]{1,0:T(8,128)(2,1)S(1)}, bf16[24,768]{1,0:T(8,128)(2,1)S(1)}, u32[]{:S(2)}, u32[]{:S(2)}) collective-permute-start(bf16[24,768]{1,0:T(8,128)(2,1)S(1)} %reduce_sum.21), channel_id=1, source_target_pairs={{0,2},{1,3},{2,0},{3,1},{4,6},{5,7},{6,4},{7,5},{8,10},{9,11},{10,... | collective-permute-start | bytes 110600 | tf_op jit(solution)/shard_map/ppermute | solution.py:73
  157.3 5.2 %collective-permute-start.15 = (bf16[24,768]{1,0:T(8,128)(2,1)S(1)}, bf16[24,768]{1,0:T(8,128)(2,1)S(1)}, u32[]{:S(2)}, u32[]{:S(2)}) collective-permute-start(bf16[24,768]{1,0:T(8,128)(2,1)S(1)} %reduce_sum.21), channel_id=1, source_target_pairs={{0,1},{1,2},{2,3},{3,0},{4,5},{5,6},{6,7},{7,4},{8,9},{9,10},{10,1... | collective-permute-start | bytes 110600 | tf_op jit(solution)/shard_map/ppermute | solution.py:73
  167.2 8.5 %collective-permute-start.22 = (bf16[24,3072]{1,0:T(8,128)(2,1)S(1)}, bf16[24,3072]{1,0:T(8,128)(2,1)S(1)}, u32[]{:S(2)}, u32[]{:S(2)}) collective-permute-start(bf16[24,3072]{1,0:T(8,128)(2,1)S(1)} %get-tuple-element.50), channel_id=1, source_target_pairs={{0,64},{4,68},{8,72},{12,76},{16,80},{20,84},{24,88},{28,92},{32,9... | collective-permute-start | bytes 442376 | tf_op jit(solution)/shard_map/ppermute | solution.py:81
  170.4 9.2 %collective-permute-start.23 = (bf16[24,3072]{1,0:T(8,128)(2,1)S(1)}, bf16[24,3072]{1,0:T(8,128)(2,1)S(1)}, u32[]{:S(2)}, u32[]{:S(2)}) collective-permute-start(bf16[24,3072]{1,0:T(8,128)(2,1)S(1)} %get-tuple-element.52), channel_id=1, source_target_pairs={{0,32},{4,36},{8,40},{12,44},{16,48},{20,52},{24,56},{28,60},{32,6... | collective-permute-start | bytes 442376 | tf_op jit(solution)/shard_map/ppermute | solution.py:81
  171.1 10.3 %collective-permute-start.24 = (bf16[24,3072]{1,0:T(8,128)(2,1)S(1)}, bf16[24,3072]{1,0:T(8,128)(2,1)S(1)}, u32[]{:S(2)}, u32[]{:S(2)}) collective-permute-start(bf16[24,3072]{1,0:T(8,128)(2,1)S(1)} %get-tuple-element.51), channel_id=1, source_target_pairs={{0,96},{4,100},{8,104},{12,108},{16,112},{20,116},{24,120},{28,124... | collective-permute-start | bytes 442376 | tf_op jit(solution)/shard_map/ppermute | solution.py:81
  174.8 11.2 %collective-permute-start.16 = (bf16[24,3840]{1,0:T(8,128)(2,1)S(1)}, bf16[24,3840]{1,0:T(8,128)(2,1)S(1)}, u32[]{:S(2)}, u32[]{:S(2)}) collective-permute-start(bf16[24,3840]{1,0:T(8,128)(2,1)S(1)} %get-tuple-element.53), channel_id=1, source_target_pairs={{0,64},{4,68},{8,72},{12,76},{16,80},{20,84},{24,88},{28,92},{32,9... | collective-permute-start | bytes 552968 | tf_op jit(solution)/shard_map/ppermute | solution.py:81
  174.9 11.1 %collective-permute-start.17 = (bf16[24,3840]{1,0:T(8,128)(2,1)S(1)}, bf16[24,3840]{1,0:T(8,128)(2,1)S(1)}, u32[]{:S(2)}, u32[]{:S(2)}) collective-permute-start(bf16[24,3840]{1,0:T(8,128)(2,1)S(1)} %get-tuple-element.55), channel_id=1, source_target_pairs={{0,32},{4,36},{8,40},{12,44},{16,48},{20,52},{24,56},{28,60},{32,6... | collective-permute-start | bytes 552968 | tf_op jit(solution)/shard_map/ppermute | solution.py:81
  175.7 10.2 %collective-permute-start.18 = (bf16[24,3840]{1,0:T(8,128)(2,1)S(1)}, bf16[24,3840]{1,0:T(8,128)(2,1)S(1)}, u32[]{:S(2)}, u32[]{:S(2)}) collective-permute-start(bf16[24,3840]{1,0:T(8,128)(2,1)S(1)} %get-tuple-element.54), channel_id=1, source_target_pairs={{0,96},{4,100},{8,104},{12,108},{16,112},{20,116},{24,120},{28,124... | collective-permute-start | bytes 552968 | tf_op jit(solution)/shard_map/ppermute | solution.py:81
  182.3 8.0 %collective-permute-start.25 = (bf16[24,3072]{1,0:T(8,128)(2,1)S(1)}, bf16[24,3072]{1,0:T(8,128)(2,1)S(1)}, u32[]{:S(2)}, u32[]{:S(2)}) collective-permute-start(bf16[24,3072]{1,0:T(8,128)(2,1)S(1)} %add_convert_fusion.4.a_ref), channel_id=1, source_target_pairs={{0,2},{1,3},{2,0},{3,1},{4,6},{5,7},{6,4},{7,5},{8,10},{9,11},{10,... | collective-permute-start | bytes 442376 | tf_op jit(solution)/shard_map/ppermute | solution.py:73
  183.9 10.2 %collective-permute-start.26 = (bf16[24,3072]{1,0:T(8,128)(2,1)S(1)}, bf16[24,3072]{1,0:T(8,128)(2,1)S(1)}, u32[]{:S(2)}, u32[]{:S(2)}) collective-permute-start(bf16[24,3072]{1,0:T(8,128)(2,1)S(1)} %add_convert_fusion.4.a_ref), channel_id=1, source_target_pairs={{0,1},{1,2},{2,3},{3,0},{4,5},{5,6},{6,7},{7,4},{8,9},{9,10},{10,1... | collective-permute-start | bytes 442376 | tf_op jit(solution)/shard_map/ppermute | solution.py:73
  185.9 10.9 %collective-permute-start.27 = (bf16[24,3072]{1,0:T(8,128)(2,1)S(1)}, bf16[24,3072]{1,0:T(8,128)(2,1)S(1)}, u32[]{:S(2)}, u32[]{:S(2)}) collective-permute-start(bf16[24,3072]{1,0:T(8,128)(2,1)S(1)} %add_convert_fusion.4.a_ref), channel_id=1, source_target_pairs={{0,3},{1,0},{2,1},{3,2},{4,7},{5,4},{6,5},{7,6},{8,11},{9,8},{10,9... | collective-permute-start | bytes 442376 | tf_op jit(solution)/shard_map/ppermute | solution.py:73
  187.0 10.6 %collective-permute-start.19 = (bf16[24,3840]{1,0:T(8,128)(2,1)S(1)}, bf16[24,3840]{1,0:T(8,128)(2,1)S(1)}, u32[]{:S(2)}, u32[]{:S(2)}) collective-permute-start(bf16[24,3840]{1,0:T(8,128)(2,1)S(1)} %add_convert_fusion.3.a_ref), channel_id=1, source_target_pairs={{0,2},{1,3},{2,0},{3,1},{4,6},{5,7},{6,4},{7,5},{8,10},{9,11},{10,... | collective-permute-start | bytes 552968 | tf_op jit(solution)/shard_map/ppermute | solution.py:73
  189.1 8.5 %collective-permute-start.20 = (bf16[24,3840]{1,0:T(8,128)(2,1)S(1)}, bf16[24,3840]{1,0:T(8,128)(2,1)S(1)}, u32[]{:S(2)}, u32[]{:S(2)}) collective-permute-start(bf16[24,3840]{1,0:T(8,128)(2,1)S(1)} %add_convert_fusion.3.a_ref), channel_id=1, source_target_pairs={{0,1},{1,2},{2,3},{3,0},{4,5},{5,6},{6,7},{7,4},{8,9},{9,10},{10,1... | collective-permute-start | bytes 552968 | tf_op jit(solution)/shard_map/ppermute | solution.py:73
  190.4 9.6 %collective-permute-start.21 = (bf16[24,3840]{1,0:T(8,128)(2,1)S(1)}, bf16[24,3840]{1,0:T(8,128)(2,1)S(1)}, u32[]{:S(2)}, u32[]{:S(2)}) collective-permute-start(bf16[24,3840]{1,0:T(8,128)(2,1)S(1)} %add_convert_fusion.3.a_ref), channel_id=1, source_target_pairs={{0,3},{1,0},{2,1},{3,2},{4,7},{5,4},{6,5},{7,6},{8,11},{9,8},{10,9... | collective-permute-start | bytes 552968 | tf_op jit(solution)/shard_map/ppermute | solution.py:73
  191.2 8.8 %copy-start = (bf16[768,768]{1,0:T(8,128)(2,1)S(1)}, bf16[768,768]{1,0:T(8,128)(2,1)}, u32[]{:S(2)}) copy-start(bf16[768,768]{1,0:T(8,128)(2,1)} %constant.85.clone.refs_3_.order_ref) | copy-start | bytes 3538948
Sparse Core Ops, SparseCore 0:
  10.9 69.9 all-gather.1
  97.2 68.8 reduce-scatter.1
